TPU v7x, 32 devices: a whole 2x2x4 slice. The times are simulated.
32 devices in a mesh: dp: 4 (over z), heads: 2 (over y), rows: 4 (over x, core).
Axes of the slice: x: 2, y: 2, z: 4, core: 2. Of those that a mesh axis runs over, the one named last changes fastest.
Arguments:
- tokens: bfloat16 [16384, 2048], P(('dp', 'rows')), may hold values from -6 to 6
- segment_lengths: int32 [4, 8], P('dp'), may hold values from 1 to 3072, as said below
- pre_norm_gain: float32 [2048], replicated, may hold values from 0.5 to 1.5
- pre_norm_bias: float32 [2048], replicated, may hold values from -1 to 1
- query_weight: bfloat16 [2048, 2048], P(None, 'heads'), may hold values from -0.1875 to 0.1875
- query_bias: float32 [2048], P('heads'), may hold values from -3 to 3
- key_value_weight: bfloat16 [2048, 256], replicated, may hold values from -0.1875 to 0.1875
- value_bias: float32 [128], replicated, may hold values from -0.3 to 0.3
- output_weight: bfloat16 [2048, 2048], P('heads'), may hold values from -1 to 1
- output_bias: float32 [2048], replicated, may hold values from -2 to 2
- mlp_norm_gain: float32 [2048], replicated, may hold values from 0.5 to 1.5
- mlp_norm_bias: float32 [2048], replicated, may hold values from -1 to 1
- expand_weight: bfloat16 [2048, 8192], P(None, ('heads', 'rows')), may hold values from -0.125 to 0.125
- expand_bias: float32 [8192], P(('heads', 'rows')), may hold values from -3 to 3
- contract_weight: bfloat16 [8192, 2048], P(('heads', 'rows')), may hold values from -0.25 to 0.25
- contract_bias: float32 [2048], replicated, may hold values from -2 to 2
- cotangent: bfloat16 [16384, 2048], P(('dp', 'rows')), may hold values from -6 to 6
Outputs:
- layer_output: bfloat16 [16384, 2048], P(('dp', 'rows'))
- input_grad: bfloat16 [16384, 2048], P(('dp', 'rows'))
- pre_norm_gain_grad: float32 [2048], replicated
- pre_norm_bias_grad: float32 [2048], replicated
- query_weight_grad: float32 [2048, 2048], P(None, 'heads')
- query_bias_grad: float32 [2048], P('heads')
- key_value_weight_grad: float32 [2048, 256], replicated
- value_bias_grad: float32 [128], replicated
- output_weight_grad: float32 [2048, 2048], P('heads')
- output_bias_grad: float32 [2048], replicated
- mlp_norm_gain_grad: float32 [2048], replicated
- mlp_norm_bias_grad: float32 [2048], replicated
- expand_weight_grad: float32 [2048, 8192], P(None, ('heads', 'rows'))
- expand_bias_grad: float32 [8192], P(('heads', 'rows'))
- contract_weight_grad: float32 [8192, 2048], P(('heads', 'rows'))
- contract_bias_grad: float32 [2048], replicated
Inputs may be any that keep to these rules, and one draw needn't show every extreme that they name: `segment_lengths`: each window's 8 segment lengths sum to at most 4096; the rest of the window is padding. Every window has a segment of exactly 3072 positions.
All inputs are finite; a program needn't handle non-finite values.
Results may differ from a plain program's by a relative error of at most 0.015.
Values may be sent and summed in bfloat16 or wider, within the bound.
No kernel may reach another device: no remote copies, remote signals or barrier semaphores. Data moves between devices by JAX's collectives and lax.ppermute only.
A program may use at most 448 MiB of HBM per device.

v0:
```python
import math

import jax
import jax.numpy as jnp
from jax import lax
from jax.sharding import PartitionSpec as P

NORM_EPSILON = 1e-05
MASKED_SCORE = -1000000000.0


def norm_apply(values, gain_vector, bias_vector):
    row_mean = jnp.mean(values, -1, keepdims=True)
    centred = values - row_mean
    row_var = jnp.mean(centred * centred, -1, keepdims=True)
    return centred * lax.rsqrt(row_var + NORM_EPSILON) * gain_vector + bias_vector


def gelu_tanh(values):
    return jax.nn.gelu(values, approximate=True)


def dot_left_t(left, right):
    return lax.dot_general(
        left, right, (((0,), (0,)), ((), ())), preferred_element_type=jnp.float32
    )


def dot_right_t(left, right):
    return lax.dot_general(
        left, right, (((1,), (1,)), ((), ())), preferred_element_type=jnp.float32
    )


def segment_ids(lengths, positions):
    segment_ends = jnp.cumsum(lengths)
    places = jnp.arange(positions, dtype=jnp.int32)
    return jnp.sum((places[:, None] >= segment_ends[None, :]).astype(jnp.int32), 1)


def feed_forward(inputs_whole, weight_cols, bias_cols):
    before_act = jnp.dot(inputs_whole, weight_cols, preferred_element_type=jnp.float32) + bias_cols
    return (before_act, gelu_tanh(before_act).astype(jnp.bfloat16))


def body(
    tokens,
    segment_lengths,
    pre_norm_gain,
    pre_norm_bias,
    query_weight,
    query_bias,
    key_value_weight,
    value_bias,
    output_weight,
    output_bias,
    mlp_norm_gain,
    mlp_norm_bias,
    expand_weight,
    expand_bias,
    contract_weight,
    contract_bias,
    cotangent,
):
    row_count = tokens.shape[0]
    heads_count = lax.axis_size("heads")
    rows_count = lax.axis_size("rows")
    head_index = lax.axis_index("heads")
    row_index = lax.axis_index("rows")
    window = row_count * rows_count
    share_rows = row_count // heads_count
    head_dim = key_value_weight.shape[1] // 2
    local_heads = query_weight.shape[1] // head_dim
    score_scale = 1.0 / math.sqrt(head_dim)
    block_rows = min(512, row_count)
    block_count = row_count // block_rows
    offset = head_index * share_rows
    tokens_f = tokens.astype(jnp.float32)
    normed_first = norm_apply(tokens_f, pre_norm_gain, pre_norm_bias).astype(jnp.bfloat16)
    query = (
        jnp.dot(normed_first, query_weight, preferred_element_type=jnp.float32) + query_bias
    ).astype(jnp.bfloat16)
    kv_bias = jnp.concatenate([jnp.zeros((head_dim,), jnp.float32), value_bias])
    key_value = (
        jnp.dot(normed_first, key_value_weight, preferred_element_type=jnp.float32) + kv_bias
    ).astype(jnp.bfloat16)
    kv_whole = lax.all_gather(key_value, "rows", axis=0, tiled=True)
    key_rows = kv_whole[:, :head_dim]
    value_rows = kv_whole[:, head_dim:]
    segment = segment_ids(segment_lengths[0], window)
    key_places = jnp.arange(window, dtype=jnp.int32)
    first_row = row_index * row_count

    def mask_for(block_index):
        query_start = first_row + block_index * block_rows
        query_pos = query_start + jnp.arange(block_rows, dtype=jnp.int32)
        query_seg = lax.dynamic_slice_in_dim(segment, query_start, block_rows, 0)
        return (query_seg[:, None] == segment[None, :]) & (
            key_places[None, :] <= query_pos[:, None]
        )

    def scores_of(query_block, block_index):
        raw_scores = jnp.einsum(
            "qhd,kd->hqk", query_block, key_rows, preferred_element_type=jnp.float32
        )
        return jnp.where(mask_for(block_index)[None], raw_scores * score_scale, MASKED_SCORE)

    query_blocks = query.reshape(block_count, block_rows, local_heads, head_dim)
    block_numbers = jnp.arange(block_count, dtype=jnp.int32)

    def forward_block(inputs):
        block_index, query_block = inputs
        scores = scores_of(query_block, block_index)
        row_max = jnp.max(scores, -1, keepdims=True)
        exp_total = jnp.sum(jnp.exp(scores - row_max), -1, keepdims=True)
        log_total = row_max + jnp.log(exp_total)
        attn_weights = jnp.exp(scores - log_total).astype(jnp.bfloat16)
        attn_out = jnp.einsum(
            "hqk,kd->qhd", attn_weights, value_rows, preferred_element_type=jnp.float32
        )
        return (
            attn_out.astype(jnp.bfloat16).reshape(block_rows, local_heads * head_dim),
            log_total[..., 0],
        )

    attn_blocks, log_totals = lax.map(forward_block, (block_numbers, query_blocks))
    attended = attn_blocks.reshape(row_count, local_heads * head_dim)
    piece_rows = attended
    attn_share = lax.psum_scatter(
        jnp.dot(piece_rows, output_weight, preferred_element_type=jnp.float32),
        "heads",
        scatter_dimension=0,
        tiled=True,
    )
    tokens_share = lax.dynamic_slice_in_dim(tokens_f, offset, share_rows, 0)
    middle = tokens_share + attn_share + output_bias
    normed_second = norm_apply(middle, mlp_norm_gain, mlp_norm_bias).astype(jnp.bfloat16)
    cot_share = lax.dynamic_slice_in_dim(cotangent, offset, share_rows, 0)
    second_whole = lax.all_gather(normed_second, ("heads", "rows"), axis=0, tiled=True)
    before_act, hidden = feed_forward(second_whole, expand_weight, expand_bias)
    piece_rows = hidden
    mlp_share = lax.psum_scatter(
        jnp.dot(piece_rows, contract_weight, preferred_element_type=jnp.float32),
        ("heads", "rows"),
        scatter_dimension=0,
        tiled=True,
    )
    second_back = lax.all_gather(normed_second, ("heads", "rows"), axis=0, tiled=True)
    before_back, hidden_back = feed_forward(second_back, expand_weight, expand_bias)
    piece_rows = lax.all_gather(cot_share, ("heads", "rows"), axis=0, tiled=True)
    contract_acc = dot_left_t(hidden_back, piece_rows)
    hidden_acc = dot_right_t(piece_rows, contract_weight)
    gelu_value, gelu_back = jax.vjp(gelu_tanh, before_back)
    grad_before = gelu_back(hidden_acc)[0]
    expand_bias_grad = jnp.sum(grad_before, 0)
    grad_before_low = grad_before.astype(jnp.bfloat16)
    expand_weight_grad = dot_left_t(second_back, grad_before_low)
    piece_rows = grad_before_low
    grad_second = lax.psum_scatter(
        dot_right_t(piece_rows, expand_weight), ("heads", "rows"), scatter_dimension=0, tiled=True
    )
    output_share = middle + mlp_share + contract_bias
    cot_f = cot_share.astype(jnp.float32)
    contract_bias_grad = jnp.sum(cot_f, 0)
    norm_two_value, norm_two_back = jax.vjp(norm_apply, middle, mlp_norm_gain, mlp_norm_bias)
    grad_middle_norm, mlp_gain_part, mlp_bias_part = norm_two_back(grad_second)
    grad_middle = cot_f + grad_middle_norm
    output_bias_part = jnp.sum(grad_middle, 0)
    grad_middle_rows = lax.all_gather(grad_middle.astype(jnp.bfloat16), "heads", axis=0, tiled=True)
    grad_attended = dot_right_t(grad_middle_rows, output_weight).astype(jnp.bfloat16)
    output_weight_part = dot_left_t(attended, grad_middle_rows)
    grad_blocks = grad_attended.reshape(block_count, block_rows, local_heads, head_dim)

    def backward_block(state_pair, inputs):
        key_acc, value_acc = state_pair
        block_index, query_block, grad_block, log_total = inputs
        scores = scores_of(query_block, block_index)
        attn_weights = jnp.exp(scores - log_total[..., None])
        grad_weights = jnp.einsum(
            "qhd,kd->hqk", grad_block, value_rows, preferred_element_type=jnp.float32
        )
        inner_sum = jnp.sum(attn_weights * grad_weights, -1, keepdims=True)
        grad_scores = (attn_weights * (grad_weights - inner_sum) * score_scale).astype(jnp.bfloat16)
        grad_query_block = jnp.einsum(
            "hqk,kd->qhd", grad_scores, key_rows, preferred_element_type=jnp.float32
        )
        key_acc = key_acc + jnp.einsum(
            "hqk,qhd->kd", grad_scores, query_block, preferred_element_type=jnp.float32
        )
        value_acc = value_acc + jnp.einsum(
            "hqk,qhd->kd",
            attn_weights.astype(jnp.bfloat16),
            grad_block,
            preferred_element_type=jnp.float32,
        )
        return ((key_acc, value_acc), grad_query_block)

    zero_keys = jnp.zeros((window, head_dim), jnp.float32)
    (grad_keys, grad_values), grad_query_blocks = lax.scan(
        backward_block,
        (zero_keys, zero_keys),
        (block_numbers, query_blocks, grad_blocks, log_totals),
    )
    grad_query = grad_query_blocks.reshape(row_count, local_heads * head_dim).astype(jnp.bfloat16)
    query_bias_part = jnp.sum(grad_query.astype(jnp.float32), 0)
    query_weight_part = dot_left_t(normed_first, grad_query)
    piece_rows = grad_query
    grad_first_query = lax.psum_scatter(
        dot_right_t(piece_rows, query_weight), "heads", scatter_dimension=0, tiled=True
    )
    grad_kv = jnp.concatenate([grad_keys, grad_values], 1)
    ordered = grad_kv.reshape(rows_count, heads_count, share_rows, 2 * head_dim).transpose(
        1, 0, 2, 3
    )
    ordered = ordered.reshape(window, 2 * head_dim)
    grad_kv_share = lax.psum_scatter(
        ordered, ("heads", "rows"), scatter_dimension=0, tiled=True
    ).astype(jnp.bfloat16)
    value_bias_part = jnp.sum(grad_kv_share[:, head_dim:].astype(jnp.float32), 0)
    first_share = lax.dynamic_slice_in_dim(normed_first, offset, share_rows, 0)
    key_value_part = dot_left_t(first_share, grad_kv_share)
    grad_first = grad_first_query + dot_right_t(grad_kv_share, key_value_weight)
    norm_one_value, norm_one_back = jax.vjp(norm_apply, tokens_share, pre_norm_gain, pre_norm_bias)
    grad_tokens_norm, pre_gain_part, pre_bias_part = norm_one_back(grad_first)
    grad_tokens = grad_middle + grad_tokens_norm
    layer_output, input_grad = (
        lax.all_gather(output_share.astype(jnp.bfloat16), "heads", axis=0, tiled=True),
        lax.all_gather(grad_tokens.astype(jnp.bfloat16), "heads", axis=0, tiled=True),
    )
    (
        pre_norm_gain_grad,
        pre_norm_bias_grad,
        key_value_weight_grad,
        value_bias_grad,
        output_bias_grad,
        mlp_norm_gain_grad,
        mlp_norm_bias_grad,
        contract_bias_sum,
    ) = lax.psum(
        (
            pre_gain_part,
            pre_bias_part,
            key_value_part,
            value_bias_part,
            output_bias_part,
            mlp_gain_part,
            mlp_bias_part,
            contract_bias_grad,
        ),
        ("dp", "heads", "rows"),
    )
    query_weight_grad, query_bias_grad, output_weight_grad = lax.psum(
        (query_weight_part, query_bias_part, output_weight_part), ("dp", "rows")
    )
    expand_weight_sum, expand_bias_sum, contract_weight_sum = lax.psum(
        (expand_weight_grad, expand_bias_grad, contract_acc), "dp"
    )
    return (
        layer_output,
        input_grad,
        pre_norm_gain_grad,
        pre_norm_bias_grad,
        query_weight_grad,
        query_bias_grad,
        key_value_weight_grad,
        value_bias_grad,
        output_weight_grad,
        output_bias_grad,
        mlp_norm_gain_grad,
        mlp_norm_bias_grad,
        expand_weight_sum,
        expand_bias_sum,
        contract_weight_sum,
        contract_bias_sum,
    )


def solution(mesh):
    in_specs = (
        P(("dp", "rows"), None),
        P("dp", None),
        P(),
        P(),
        P(None, "heads"),
        P("heads"),
        P(),
        P(),
        P("heads", None),
        P(),
        P(),
        P(),
        P(None, ("heads", "rows")),
        P(("heads", "rows")),
        P(("heads", "rows"), None),
        P(),
        P(("dp", "rows"), None),
    )
    out_specs = (
        P(("dp", "rows"), None),
        P(("dp", "rows"), None),
        P(),
        P(),
        P(None, "heads"),
        P("heads"),
        P(),
        P(),
        P("heads", None),
        P(),
        P(),
        P(),
        P(None, ("heads", "rows")),
        P(("heads", "rows")),
        P(("heads", "rows"), None),
        P(),
    )
    return jax.shard_map(body, mesh=mesh, in_specs=in_specs, out_specs=out_specs, check_vma=False)
```

profile of v0, /device:TPU:0, one launch (start us, length us, event | category | flops | bytes accessed | tf_op | source)
XLA Modules:
  0.0 2901.3 jit_solution(1030131393013338258)
XLA Ops:
  7.3 3.0 convert_reduce_fusion
  18.3 8.0 fusion.66
  28.7 14.8 all-gather.7.cloned.1.call-done
  47.5 177.1 %while.28 = (s32[]{:T(128)}, bf16[2,512,1024]{2,1,0:T(8,128)(2,1)}, f32[2,8,512]{2,1,0:T(8,128)S(1)}, s32[2]{0:T(128)S(1)}, s32[]{:T(128)}, /*index=5*/s32[4096]...) while((s32[]{:T(128)}, bf16[2,512,1024]{2,1,0:T(8,128)(2,1)}, ...), condition=%wide.region_7.8_spmd.clone, body=%wide.region_4.7_spmd.clone.sunk | while | flops 8781295616 | bytes 218261712 | solution.py:126
  49.2 2.7 fusion.137
  51.9 27.5 bitcast_reduce_fusion.2
  79.3 21.7 fusion.138
  101.1 26.3 fusion.139
  131.3 2.7 fusion.137
  134.0 27.5 bitcast_reduce_fusion.2
  161.5 21.7 fusion.138
  183.2 26.3 fusion.139
  224.6 10.7 fusion.89
  235.4 6.7 convert_element_type.72
  244.6 90.1 %reduce-scatter.6.cloned.1.call-done = f32[512,2048]{1,0:T(8,128)} async-done(((f32[1024,2048]{1,0:T(8,128)}), f32[512,2048]{1,0:T(8,128)}) %reduce-scatter.6.cloned.1.call-update) | async-done | bytes 4194320 | tf_op jit(solution)/shard_map/reduce_scatter | solution.py:129
  334.7 5.0 fusion.87
  344.6 3.2 constant_dynamic-slice_fusion.1
  347.8 86.7 %all-gather.9.cloned.1.call-done = bf16[4096,2048]{1,0:T(8,128)(2,1)} async-done(((bf16[512,2048]{1,0:T(8,128)(2,1)}), bf16[4096,2048]{1,0:T(8,128)(2,1)}) %all-gather.9.cloned.1.call-update) | async-done | bytes 16777232 | tf_op jit(solution)/shard_map/all_gather | solution.py:139
  434.5 23.4 fusion.90
  457.9 69.0 %all-gather.13.cloned.1.call-done = bf16[4096,2048]{1,0:T(8,128)(2,1)} async-done(((bf16[512,2048]{1,0:T(8,128)(2,1)}), bf16[4096,2048]{1,0:T(8,128)(2,1)}) %all-gather.13.cloned.1.call-update) | async-done | bytes 16777232 | tf_op jit(solution)/shard_map/all_gather | solution.py:150
  526.9 36.4 %fusion.83 = (f32[1024]{0:T(1024)}, bf16[4096,1024]{1,0:T(8,128)(2,1)}) fusion(f32[4096,1024]{1,0:T(8,128)} %fusion.90, f32[1024]{0:T(1024)S(1)} %copy-done.47, bf16[4096,2048]{1,0:T(8,128)(2,1)} %all-gather.13.cloned.1.call-done, bf16[1024,2048]{1,0:T(8,128)(2,1)} %param.35), kind=kOutput, calls=%fused_computation.134 | convolution fusion | flops 17272143872 | bytes 46145536 | tf_op jit(solution)/shard_map/dot_general | solution.py:30
  563.3 24.5 fusion.64
  587.9 30.7 %fusion.82 = f32[4096,2048]{1,0:T(8,128)} fusion(bf16[1024,2048]{1,0:T(8,128)(2,1)} %param.35, f32[4096,1024]{1,0:T(8,128)} %fusion.90, f32[1024]{0:T(1024)S(1)} %copy-done.47), kind=kOutput, calls=%fused_computation.133 | convolution fusion | flops 17221812224 | bytes 54530048 | tf_op jit(solution)/shard_map/dot_general | solution.py:143
  618.7 174.6 %reduce-scatter.10.cloned.1.call-done = f32[512,2048]{1,0:T(8,128)} async-done(((f32[4096,2048]{1,0:T(8,128)}), f32[512,2048]{1,0:T(8,128)}) %reduce-scatter.10.cloned.1.call-update) | async-done | bytes 4194320 | tf_op jit(solution)/shard_map/reduce_scatter | solution.py:159
  793.3 4.9 multiply_reduce_fusion.1
  798.2 203.8 %reduce-scatter.8.cloned.1.call-done = f32[512,2048]{1,0:T(8,128)} async-done(((f32[4096,2048]{1,0:T(8,128)}), f32[512,2048]{1,0:T(8,128)}) %reduce-scatter.8.cloned.1.call-update) | async-done | bytes 4194320 | tf_op jit(solution)/shard_map/reduce_scatter | solution.py:142
  1002.0 6.6 fusion.86
  1012.5 56.8 %all-gather.15.cloned.1.call-done = bf16[1024,2048]{1,0:T(8,128)(2,1)} async-done(((bf16[512,2048]{1,0:T(8,128)(2,1)}), bf16[1024,2048]{1,0:T(8,128)(2,1)}) %all-gather.15.cloned.1.call-update) | async-done | bytes 4194320 | tf_op jit(solution)/shard_map/all_gather | solution.py:169
  1069.3 8.0 convert_bitcast_fusion
  1079.3 498.6 %while.29 = (s32[]{:T(128)}, f32[4096,128]{1,0:T(8,128)}, f32[4096,128]{1,0:T(8,128)}, bf16[2,512,8,128]{3,1,2,0:T(8,128)(2,1)}, s32[2]{0:T(128)S(1)}, /*index=5...) while((s32[]{:T(128)}, f32[4096,128]{1,0:T(8,128)}, ...), condition=%wide.region_17.18_spmd.clone, body=%wide.region_15.17_spmd.clone.sunk | while | flops 21718122496 | bytes 766585088 | solution.py:199
  1082.2 3.7 fusion.146
  1085.8 28.6 fusion.147
  1114.4 24.3 fusion.150
  1138.8 23.1 fusion.148
  1161.9 83.7 %fusion.149 = f32[4096,128]{1,0:T(8,128)} fusion(f32[8,512,4096]{2,1,0:T(8,128)} %fusion.147, f32[512,8,4096]{2,0,1:T(8,128)} %fusion.148, f32[4096,128]{1,0:T(8,128)} %get-tuple-element.561, pred[]{:T(512)S(6)} %compare.4, bf16[2,512,8,128]{3,1,2,0:T(8,128)(2,1)} %get-tuple-element.583, s32[]{:T(128)S(6)} %copy.106), kind=kOutput, calls=%fused_computation.44.clone.2 | convolution fusion | flops 4379910144 | bytes 273678336 | tf_op jit(solution)/shard_map/while/body/eval_jaxpr/hqk,qhd->kd/dot_general | solution.py:187
  1245.6 82.3 %bitcast_dynamic-update-slice_fusion.5 = bf16[2,512,8,128]{3,1,2,0:T(8,128)(2,1)} fusion(bf16[2,512,8,128]{3,1,2,0:T(8,128)(2,1)} %get-tuple-element.563, s32[]{:T(128)S(6)} %copy.106, f32[8,512,4096]{2,1,0:T(8,128)} %fusion.147, f32[512,8,4096]{2,0,1:T(8,128)} %fusion.148, bf16[4096,128]{1,0:T(8,128)(2,1)S(1)} %copy-done.16), kind=kOutput, calls=%fused_computation.46.clone.1 | convolution fusion | flops 4378861568 | bytes 271581184 | tf_op jit(solution)/shard_map/while/body/eval_jaxpr/hqk,kd->qhd/dot_general | solution.py:184
  1330.6 3.7 fusion.146
  1334.3 28.6 fusion.147
  1362.8 25.0 fusion.150
  1387.8 23.1 fusion.148
  1411.0 84.2 %fusion.149 = f32[4096,128]{1,0:T(8,128)} fusion(f32[8,512,4096]{2,1,0:T(8,128)} %fusion.147, f32[512,8,4096]{2,0,1:T(8,128)} %fusion.148, f32[4096,128]{1,0:T(8,128)} %get-tuple-element.561, pred[]{:T(512)S(6)} %compare.4, bf16[2,512,8,128]{3,1,2,0:T(8,128)(2,1)} %get-tuple-element.583, s32[]{:T(128)S(6)} %copy.106), kind=kOutput, calls=%fused_computation.44.clone.2 | convolution fusion | flops 4379910144 | bytes 273678336 | tf_op jit(solution)/shard_map/while/body/eval_jaxpr/hqk,qhd->kd/dot_general | solution.py:187
  1495.2 82.3 %bitcast_dynamic-update-slice_fusion.5 = bf16[2,512,8,128]{3,1,2,0:T(8,128)(2,1)} fusion(bf16[2,512,8,128]{3,1,2,0:T(8,128)(2,1)} %get-tuple-element.563, s32[]{:T(128)S(6)} %copy.106, f32[8,512,4096]{2,1,0:T(8,128)} %fusion.147, f32[512,8,4096]{2,0,1:T(8,128)} %fusion.148, bf16[4096,128]{1,0:T(8,128)(2,1)S(1)} %copy-done.16), kind=kOutput, calls=%fused_computation.46.clone.1 | convolution fusion | flops 4378861568 | bytes 271581184 | tf_op jit(solution)/shard_map/while/body/eval_jaxpr/hqk,kd->qhd/dot_general | solution.py:184
  1587.2 6.8 fusion.69
  1594.6 39.8 %reduce-scatter.14.cloned.1.call-done = f32[512,256]{1,0:T(8,128)} async-done(((f32[4096,256]{1,0:T(8,128)}), f32[512,256]{1,0:T(8,128)}) %reduce-scatter.14.cloned.1.call-update) | async-done | bytes 524304 | tf_op jit(solution)/shard_map/reduce_scatter | solution.py:216
  1635.5 101.1 %reduce-scatter.12.cloned.1.call-done = f32[512,2048]{1,0:T(8,128)} async-done(((f32[1024,2048]{1,0:T(8,128)}), f32[512,2048]{1,0:T(8,128)}) %reduce-scatter.12.cloned.1.call-update) | async-done | bytes 4194320 | tf_op jit(solution)/shard_map/reduce_scatter | solution.py:208
  1736.6 4.6 multiply_reduce_fusion.2
  1741.2 3.5 fusion.85
  1746.8 2.8 convert_reduce_fusion.1
  1749.7 29.3 %fusion.81 = f32[1024,2048]{1,0:T(8,128)} fusion(bf16[4096,2048]{1,0:T(8,128)(2,1)} %all-gather.13.cloned.1.call-done, f32[4096,1024]{1,0:T(8,128)} %fusion.90, f32[1024]{0:T(1024)S(1)} %copy-done.48), kind=kOutput, calls=%fused_computation.132 | convolution fusion | flops 17221812224 | bytes 41947136 | tf_op jit(solution)/shard_map/dot_general | solution.py:24
  1779.0 24.0 fusion.62
  1803.1 3.9 fusion.71
  1807.3 11.5 fusion.67
  1818.8 6.8 fusion.91
  1826.3 12.2 psum.109
  1838.8 30.2 %psum.101 = f32[1024]{0:T(1024)} all-reduce(f32[1024]{0:T(1024)S(1)} %bitcast.220), channel_id=1, replica_groups=mesh['dp'=4,'heads'=2,'rows'=4] {'dp','rows'}, use_global_device_ids=true, to_apply=%region_30.31 | all-reduce | flops 1024 | bytes 8192 | tf_op jit(solution)/shard_map/psum | solution.py:252
  1869.1 41.8 %all-reduce.1 = (f32[2048]{0:T(1024)}, f32[2048]{0:T(1024)}, f32[128]{0:T(128)}, f32[2048]{0:T(1024)}, f32[2048]{0:T(1024)}, /*index=5*/f32[2048]{0:T(1024)}, f32[2048]{0:T(1024)}) all-reduce(f32[2048]{0:T(1024)S(1)} %get-tuple-element.288, ...), channel_id=1, replica_groups=mesh['dp'=4,'heads'=2,'rows'=4] {'dp','heads','rows'}, use_global_device_ids=true, to_apply=%region_25.26 | all-reduce | flops 12416 | bytes 99328 | tf_op jit(solution)/shard_map/psum | solution.py:239
  1910.9 511.0 %all-reduce.12.cloned.1.call-done = (f32[2048,1024]{1,0:T(8,128)}, f32[1024,2048]{1,0:T(8,128)}) async-done(((f32[2048,1024]{1,0:T(8,128)}, f32[1024,2048]{1,0:T(8,128)}), (f32[2048,1024]{1,0:T(8,128)}, f32[1024,2048]{1,0:T(8,128)})) %all-reduce.12.cloned.1.call-update) | async-done | bytes 16777232 | tf_op jit(solution)/shard_map/psum | solution.py:255
  2421.9 138.9 %all-reduce.8.cloned.1.call-done = f32[2048,256]{1,0:T(8,128)} async-done(((f32[2048,256]{1,0:T(8,128)}), f32[2048,256]{1,0:T(8,128)}) %all-reduce.8.cloned.1.call-update) | async-done | bytes 2097168 | tf_op jit(solution)/shard_map/psum | solution.py:239
  2560.8 302.5 %all-reduce.10.cloned.1.call-done = (f32[2048,1024]{1,0:T(8,128)}, f32[1024,2048]{1,0:T(8,128)}) async-done(((f32[2048,1024]{1,0:T(8,128)}, f32[1024,2048]{1,0:T(8,128)}), (f32[2048,1024]{1,0:T(8,128)}, f32[1024,2048]{1,0:T(8,128)})) %all-reduce.10.cloned.1.call-update) | async-done | bytes 16777232 | tf_op jit(solution)/shard_map/psum | solution.py:252
  2863.4 5.1 copy.121
  2872.5 3.5 copy.123
  2877.4 8.6 copy.125
  2886.0 4.3 copy.126
  2891.2 3.4 copy.127
  (209 shorter events, 59.2 us)
Async XLA Ops:
  7.2 8.8 copy-start
  7.2 4.8 copy-start.41
  7.2 4.8 copy-start.21
  7.2 36.3 %all-gather.7.cloned.1.call-start = ((), (), s32[]{:S(2)}) async-start(), calls=%async_computation.5 | async-start | bytes 2621440 | tf_op jit(solution)/shard_map/all_gather | solution.py:87
  7.3 3.5 copy-start.2
  7.3 4.8 copy-start.37
  13.9 2.0 copy-start.10
  16.0 2.1 copy-start.49
  16.0 2.3 copy-start.46
  18.0 316.7 %reduce-scatter.6.cloned.1.call-start = ((), (), s32[]{:S(2)}) async-start(), calls=%async_computation.6 | async-start | bytes 12582912 | tf_op jit(solution)/shard_map/reduce_scatter | solution.py:129
  224.6 10.7 copy-start.12
  224.6 10.7 copy-start.17
  235.3 199.2 %all-gather.9.cloned.1.call-start = ((), (), s32[]{:S(2)}) async-start(), calls=%async_computation.7 | async-start | bytes 18874368 | tf_op jit(solution)/shard_map/all_gather | solution.py:139
  242.1 92.6 %copy-start.39 = (f32[2048]{0:T(1024)S(1)}, f32[2048]{0:T(1024)}, u32[]{:S(2)}) copy-start(f32[2048]{0:T(1024)} %param.30) | copy-start | bytes 24580
  244.6 95.2 %copy-start.25 = (f32[512]{0:T(512)}, f32[512]{0:T(512)S(1)}, u32[]{:S(2)}) copy-start(f32[512]{0:T(512)S(1)} %broadcast_multiply_fusion.1) | copy-start | bytes 6148
  339.8 2.0 copy-start.1
  339.8 2.6 copy-start.19
  339.8 2.6 copy-start.38
  339.8 2.0 copy-start.23
  344.5 182.4 %all-gather.13.cloned.1.call-start = ((), (), s32[]{:S(2)}) async-start(), calls=%async_computation.10 | async-start | bytes 18874368 | tf_op jit(solution)/shard_map/all_gather | solution.py:150
  347.8 179.1 %copy-start.47 = (f32[1024]{0:T(1024)S(1)}, f32[1024]{0:T(1024)}, u32[]{:S(2)}) copy-start(f32[1024]{0:T(1024)} %param.34) | copy-start | bytes 12292
  347.8 445.5 %reduce-scatter.10.cloned.1.call-start = ((), (), s32[]{:S(2)}) async-start(), calls=%async_computation.11 | async-start | bytes 37748736 | tf_op jit(solution)/shard_map/reduce_scatter | solution.py:159
  526.9 36.4 %copy-start.42 = (bf16[2048,1024]{1,0:T(8,128)(2,1)S(1)}, bf16[2048,1024]{1,0:T(8,128)(2,1)}, u32[]{:S(2)}) copy-start(bf16[2048,1024]{1,0:T(8,128)(2,1)} %param.33) | copy-start | bytes 12582916
  587.8 414.1 %reduce-scatter.8.cloned.1.call-start = ((), (), s32[]{:S(2)}) async-start(), calls=%async_computation.8 | async-start | bytes 37748736 | tf_op jit(solution)/shard_map/reduce_scatter | solution.py:142
  618.6 174.7 %copy-start.20 = (f32[2048]{0:T(1024)S(1)}, f32[2048]{0:T(1024)}, u32[]{:S(2)}) copy-start(f32[2048]{0:T(1024)} %param.31) | copy-start | bytes 24580
  618.6 174.7 %copy-start.24 = (f32[512]{0:T(512)S(1)}, f32[512]{0:T(512)}, u32[]{:S(2)}) copy-start(f32[512]{0:T(512)} %copy-done.23) | copy-start | bytes 6148
  618.6 174.7 %copy-start.28 = (f32[512]{0:T(512)S(1)}, f32[512]{0:T(512)}, u32[]{:S(2)}) copy-start(f32[512]{0:T(512)} %copy-done.27) | copy-start | bytes 6148
  618.6 179.5 %copy-start.32 = (f32[512]{0:T(512)S(1)}, f32[512]{0:T(512)}, u32[]{:S(2)}) copy-start(f32[512]{0:T(512)} %copy-done.31) | copy-start | bytes 6148
  618.6 383.3 %copy-start.36 = (f32[2048]{0:T(1024)S(1)}, f32[2048]{0:T(1024)}, u32[]{:S(2)}) copy-start(f32[2048]{0:T(1024)} %param.36) | copy-start | bytes 24580
  618.6 450.7 %all-gather.15.cloned.1.call-start = ((), (), s32[]{:S(2)}) async-start(), calls=%async_computation.12 | async-start | bytes 6291456 | tf_op jit(solution)/shard_map/all_gather | solution.py:169
  1002.0 8.6 copy-start.7
  1008.5 2.0 copy-start.5
  1008.5 2.0 copy-start.33
  1012.4 622.0 %reduce-scatter.14.cloned.1.call-start = ((), (), s32[]{:S(2)}) async-start(), calls=%async_computation.14 | async-start | bytes 4718592 | tf_op jit(solution)/shard_map/reduce_scatter | solution.py:216
  1077.3 2.0 copy-start.4
  1077.3 2.0 copy-start.13
  1077.4 2.0 copy-start.18
  1161.9 83.7 %copy-start.16 = (bf16[4096,128]{1,0:T(8,128)(2,1)S(1)}, bf16[4096,128]{1,0:T(8,128)(2,1)}, u32[]{:S(2)}) copy-start(bf16[4096,128]{1,0:T(8,128)(2,1)} %get-tuple-element.584) | copy-start | bytes 3145732 | tf_op jit(solution)/shard_map/while
  1411.0 84.2 %copy-start.16 = (bf16[4096,128]{1,0:T(8,128)(2,1)S(1)}, bf16[4096,128]{1,0:T(8,128)(2,1)}, u32[]{:S(2)}) copy-start(bf16[4096,128]{1,0:T(8,128)(2,1)} %get-tuple-element.584) | copy-start | bytes 3145732 | tf_op jit(solution)/shard_map/while
  1582.9 153.6 %reduce-scatter.12.cloned.1.call-start = ((), (), s32[]{:S(2)}) async-start(), calls=%async_computation.13 | async-start | bytes 12582912 | tf_op jit(solution)/shard_map/reduce_scatter | solution.py:208
  1583.0 4.2 copy-start.43
  1593.9 142.6 %copy-start.22 = (f32[2048]{0:T(1024)S(1)}, f32[2048]{0:T(1024)}, u32[]{:S(2)}) copy-start(f32[2048]{0:T(1024)} %param.23) | copy-start | bytes 24580
  1593.9 142.6 %copy-start.26 = (f32[512]{0:T(512)S(1)}, f32[512]{0:T(512)}, u32[]{:S(2)}) copy-start(f32[512]{0:T(512)} %copy-done.25) | copy-start | bytes 6148
  1594.0 244.5 %all-gather.11.cloned.1.call-start = ((), (), s32[]{:S(2)}) async-start(), calls=%async_computation.9 | async-start | bytes 6291456 | tf_op jit(solution)/shard_map/all_gather | solution.py:227
  1594.6 316.4 %all-gather.17.cloned.1.call-start = ((), (), s32[]{:S(2)}) async-start(), calls=%async_computation.15 | async-start | bytes 6291456 | tf_op jit(solution)/shard_map/all_gather | solution.py:228
  1741.2 3.8 copy-start.6
  1741.2 5.6 copy-start.8
  1741.2 5.6 copy-start.34
  1746.8 2.9 copy-start.48
  1749.7 672.3 %all-reduce.12.cloned.1.call-start = ((), (), s32[]{:S(2)}) async-start(), calls=%async_computation.18 | async-start | bytes 33554432 | tf_op jit(solution)/shard_map/psum | solution.py:255
  1803.1 757.8 %all-reduce.8.cloned.1.call-start = ((), (), s32[]{:S(2)}) async-start(), calls=%async_computation.16 | async-start | bytes 4194304 | tf_op jit(solution)/shard_map/psum | solution.py:239
  1807.0 1056.3 %all-reduce.10.cloned.1.call-start = ((), (), s32[]{:S(2)}) async-start(), calls=%async_computation.17 | async-start | bytes 33554432 | tf_op jit(solution)/shard_map/psum | solution.py:252
  1807.3 11.6 copy-start.44
  1807.3 11.5 copy-start.45
  1825.6 43.5 %copy-start.29 = (f32[2048]{0:T(1024)S(1)}, f32[2048]{0:T(1024)}, u32[]{:S(2)}) copy-start(f32[2048]{0:T(1024)} %get-tuple-element.290) | copy-start | bytes 24580
  1825.6 43.5 %copy-start.30 = (f32[2048]{0:T(1024)S(1)}, f32[2048]{0:T(1024)}, u32[]{:S(2)}) copy-start(f32[2048]{0:T(1024)} %get-tuple-element.292) | copy-start | bytes 24580
  2863.4 5.1 copy-start.11
  2863.4 7.2 slice-start.4
  2868.4 4.1 slice-start.5
  2872.5 3.5 copy-start.15
  2876.1 9.9 slice-start.2
  2877.4 8.6 slice-start.3
  2877.4 12.9 slice-start
  2886.0 5.2 slice-start.1
  (7 other events, 6.8 us)
Sparse Core Ops, SparseCore 0:
  18.2 25.2 all-gather.6
  235.5 99.2 reduce-scatter.5
  344.6 89.8 all-gather.8
  437.0 89.8 all-gather.12
  588.0 205.2 reduce-scatter.9
  796.7 205.2 reduce-scatter.7
  1012.6 56.7 all-gather.14
  1583.0 51.3 reduce-scatter.13
  1637.3 99.2 reduce-scatter.11
  1738.0 56.7 all-gather.10
  1797.0 56.7 all-gather.16
  1857.6 564.2 all-reduce.11
  2428.1 132.6 all-reduce.7
  2565.5 297.8 all-reduce.9
where the time goes:
time: 2910 us; the launch traced here: 2900 us
  waiting for transfers between devices  1790 us (62%)
  matrix products  824 us (28%)
  other arithmetic  103 us (4%)
  blocking collectives  84.2 us (3%)
  local copies, waits for them, and re-layouts  69.2 us (2%)
    psum x1, waiting for transfers between devices, body(): lax.psum((expand_weight_grad, expand_bias_grad, contract_acc), 'dp')  511 us
    psum x1, waiting for transfers between devices, body(): lax.psum((query_weight_part, query_bias_part, output_weight_part), ('dp',...  303 us
    reduce_scatter x1, waiting for transfers between devices, body(): lax.psum_scatter(jnp.dot(piece_rows, contract_weight, preferred_element_t...  204 us
    reduce_scatter x1, waiting for transfers between devices, body(): lax.psum_scatter(dot_right_t(piece_rows, expand_weight), ('heads', 'rows'...  175 us
    dot_general x2, matrix products, backward_block(): jnp.einsum('hqk,qhd->kd', grad_scores, query_block, preferred_element_typ...  168 us
    dot_general x2, matrix products, backward_block(): jnp.einsum('hqk,kd->qhd', grad_scores, key_rows, preferred_element_type=j...  165 us
    psum x1, waiting for transfers between devices, body(): lax.psum((pre_gain_part, pre_bias_part, key_value_part, value_bias_part,...  139 us
    dot_general x4, matrix products, scores_of(): jnp.einsum('qhd,kd->hqk', query_block, key_rows, preferred_element_type=j...  112 us
  transfers between devices with their start and end apart: 14, of which 12 were waited for; matrix products, arithmetic and copies ran while one was open for 6% of the time, Pallas kernels for 0%

commit v1 on v0

v1 whole, which is shorter than its diff:
```python
import functools
import math

import jax
import jax.numpy as jnp
from jax import lax
from jax.experimental import pallas as pl
from jax.experimental.pallas import tpu as pltpu
from jax.sharding import PartitionSpec as P

NORM_EPSILON = 1e-05
FAR = -1e30
LOG2E = 1.4426950408889634
GELU_A = math.sqrt(2.0 / math.pi)
GELU_B = 0.044715
F32 = jnp.float32
BF16 = jnp.bfloat16
MIB = 1024 * 1024
FORWARD_BLOCK = (512, 1024)
BACKWARD_BLOCK = (256, 1024)


def dot(left, right):
    return jnp.dot(left, right, preferred_element_type=F32)


def dot_tn(left, right):
    return lax.dot_general(left, right, (((0,), (0,)), ((), ())), preferred_element_type=F32)


def dot_nt(left, right):
    return lax.dot_general(left, right, (((1,), (1,)), ((), ())), preferred_element_type=F32)


def call(kernel, grid, ins, outs, scratch=(), prefetch=0, vmem=48, flops=0, moved=0, alias=None):
    arrays = [a for a, _, _ in ins[prefetch:]]
    specs = [
        pl.BlockSpec(b, m, pipeline_mode=pl.Buffered(1)) if b == a.shape else pl.BlockSpec(b, m) for a, b, m in ins[prefetch:]
    ]
    scalars = [a for a, _, _ in ins[:prefetch]]
    return pl.pallas_call(
        kernel,
        grid_spec=pltpu.PrefetchScalarGridSpec(
            num_scalar_prefetch=prefetch,
            grid=grid,
            in_specs=specs,
            out_specs=[pl.BlockSpec(b, m) for _, _, b, m in outs],
            scratch_shapes=list(scratch),
        ),
        out_shape=[jax.ShapeDtypeStruct(s, d) for s, d, _, _ in outs],
        compiler_params=pltpu.CompilerParams(vmem_limit_bytes=vmem * MIB),
        cost_estimate=pl.CostEstimate(flops=int(flops), bytes_accessed=int(moved), transcendentals=0),
        input_output_aliases=alias or {},
    )(*scalars, *arrays)


def whole(array):
    zeros = (0,) * array.ndim
    return (array, array.shape, lambda *_: zeros)


def rows_of(array, block):
    return (array, (block, array.shape[1]), lambda i, *_: (i, 0))


def normed(values, gain, bias):
    mean = jnp.mean(values, -1, keepdims=True)
    centred = values - mean
    var = jnp.mean(centred * centred, -1, keepdims=True)
    return centred * lax.rsqrt(var + NORM_EPSILON) * gain + bias


def norm_back(values, grad, gain):
    mean = jnp.mean(values, -1, keepdims=True)
    centred = values - mean
    var = jnp.mean(centred * centred, -1, keepdims=True)
    inverse = lax.rsqrt(var + NORM_EPSILON)
    xhat = centred * inverse
    g = grad * gain
    g_mean = jnp.mean(g, -1, keepdims=True)
    gx_mean = jnp.mean(g * xhat, -1, keepdims=True)
    return xhat, (g - g_mean - xhat * gx_mean) * inverse


def norm_kv_kernel(t_ref, g_ref, b_ref, w_ref, wb_ref, n_ref, kv_ref):
    low = normed(t_ref[...].astype(F32), g_ref[...], b_ref[...]).astype(BF16)
    n_ref[...] = low
    kv_ref[...] = (dot(low, w_ref[...]) + wb_ref[...]).astype(BF16)


def project_kernel(core, n_ref, wa_ref, ba_ref, wb_ref, bb_ref, a_ref, b_ref):
    low = n_ref[...]
    b_ref[...] = (dot(low, wb_ref[...]) + bb_ref[...]).astype(BF16)
    a_ref[...] = (dot(low, wa_ref[...]) + ba_ref[...]).astype(BF16)


def attn_forward_kernel(heads, half, bk, scale2, info, qa_ref, qb_ref, kv_ref, vt_ref, st_ref, oa_ref, ob_ref, lse_ref, m_ref, l_ref, acc_ref):
    i = pl.program_id(0)
    first, low, high, clear_from, clear_to = (info[n, i] for n in range(5))
    bq, dim = qa_ref.shape[0], kv_ref.shape[1] // 2
    in_a = i < half
    start = st_ref[...]
    place = first + lax.broadcasted_iota(jnp.int32, (1, bq), 1)
    queries = jnp.where(in_a, qa_ref[...], qb_ref[...])
    m_ref[...] = jnp.full_like(m_ref, FAR)
    l_ref[...] = jnp.zeros_like(l_ref)
    acc_ref[...] = jnp.zeros_like(acc_ref)

    def step(block, masked):
        begin = pl.multiple_of(block * bk, bk)
        keys = kv_ref[pl.ds(begin, bk), :dim]
        values = vt_ref[:, pl.ds(begin, bk)]
        if masked:
            key_place = begin + lax.broadcasted_iota(jnp.int32, (bk, 1), 0)
            allowed = (key_place >= start) & (key_place <= place)
        for h in range(heads):
            s = dot_nt(keys, queries[:, h * dim : (h + 1) * dim])
            if masked:
                s = jnp.where(allowed, s, FAR)
            old = m_ref[h : h + 1, :]
            new = jnp.maximum(old, jnp.max(s, 0, keepdims=True) * scale2)
            p = jnp.exp2(s * scale2 - new)
            fix = jnp.exp2(old - new)
            l_ref[h : h + 1, :] = l_ref[h : h + 1, :] * fix + jnp.sum(p, 0, keepdims=True)
            m_ref[h : h + 1, :] = new
            acc_ref[h] = acc_ref[h] * fix + dot(values, p.astype(BF16))

    def body(block, carry):
        clear = (block >= clear_from) & (block < clear_to)

        @pl.when(clear)
        def _():
            step(block, False)

        @pl.when(jnp.logical_not(clear))
        def _():
            step(block, True)

        return carry

    lax.fori_loop(low, high, body, 0)
    outs = []
    for h in range(heads):
        total = l_ref[h : h + 1, :]
        outs.append((acc_ref[h] / total).T.astype(BF16))
    lse_ref[...] = m_ref[...] + jnp.log2(l_ref[...])

    @pl.when(in_a)
    def _():
        for h in range(heads):
            oa_ref[:, h * dim : (h + 1) * dim] = outs[h]

    @pl.when(jnp.logical_not(in_a))
    def _():
        for h in range(heads):
            ob_ref[:, h * dim : (h + 1) * dim] = outs[h]


def attn_backward_kernel(
    heads, half, bk, scale, scale2, info, qa_ref, qb_ref, ga_ref, gb_ref, oa_ref, ob_ref, kv_ref, kt_ref, st_ref, lse_ref, dqa_ref, dqb_ref, dkv_ref, dq_ref
):
    i = pl.program_id(0)
    first, low, high, clear_from, clear_to = (info[n, i] for n in range(5))
    bq, dim = qa_ref.shape[0], kv_ref.shape[1] // 2
    in_a = i < half

    @pl.when(i == 0)
    def _():
        dkv_ref[...] = jnp.zeros_like(dkv_ref)

    start = st_ref[...]
    place = first + lax.broadcasted_iota(jnp.int32, (1, bq), 1)
    queries = jnp.where(in_a, qa_ref[...], qb_ref[...])
    grads = jnp.where(in_a, ga_ref[...], gb_ref[...])
    outs = jnp.where(in_a, oa_ref[...], ob_ref[...])
    inner, lse = [], []
    for h in range(heads):
        cut = slice(h * dim, (h + 1) * dim)
        product = grads[:, cut].astype(F32) * outs[:, cut].astype(F32)
        inner.append(jnp.sum(product.T, 0, keepdims=True))
        lse.append(lse_ref[h : h + 1, :])
    dq_ref[...] = jnp.zeros_like(dq_ref)

    def step(block, masked):
        begin = pl.multiple_of(block * bk, bk)
        keys = kv_ref[pl.ds(begin, bk), :dim]
        values = kv_ref[pl.ds(begin, bk), dim:]
        keys_t = kt_ref[:, pl.ds(begin, bk)]
        if masked:
            key_place = begin + lax.broadcasted_iota(jnp.int32, (bk, 1), 0)
            allowed = (key_place >= start) & (key_place <= place)
        dk = None
        for h in range(heads):
            cut = slice(h * dim, (h + 1) * dim)
            s = dot_nt(keys, queries[:, cut])
            dp = dot_nt(values, grads[:, cut])
            p = jnp.exp2(s * scale2 - lse[h])
            if masked:
                p = jnp.where(allowed, p, 0.0)
            ds = (p * (dp - inner[h])).astype(BF16)
            dv_part = dot(p.astype(BF16), grads[:, cut])
            dk_part = dot(ds, queries[:, cut])
            dk, dv = (dk_part, dv_part) if dk is None else (dk + dk_part, dv + dv_part)
            dq_ref[h] += dot(keys_t, ds)
        dkv_ref[pl.ds(begin, bk), :dim] += dk * scale
        dkv_ref[pl.ds(begin, bk), dim:] += dv

    def body(block, carry):
        clear = (block >= clear_from) & (block < clear_to)

        @pl.when(clear)
        def _():
            step(block, False)

        @pl.when(jnp.logical_not(clear))
        def _():
            step(block, True)

        return carry

    lax.fori_loop(low, high, body, 0)

    def leave(ref):
        for h in range(heads):
            ref[:, h * dim : (h + 1) * dim] = (dq_ref[h] * scale).T.astype(BF16)

    @pl.when(in_a)
    def _():
        leave(dqa_ref)

    @pl.when(jnp.logical_not(in_a))
    def _():
        leave(dqb_ref)


def balanced(acts, weights, product, by_rows, scratch):
    act_ref, weight_ref, sums = scratch[0], scratch[1], scratch[2:]
    sides = len(sums)
    calls = len(acts) // sides
    cols = acts[0].shape[1] // 2
    for n in range(sides):

        @pl.when(pl.program_id(0) == 0)
        def _():
            keep, send = weights[2 * n], weights[2 * n + 1]
            if by_rows:
                size = keep.shape[0]
                weight_ref[n, :size, :] = keep[...]
                weight_ref[n, size:, :] = send[...]
            else:
                size = keep.shape[1]
                weight_ref[n, :, :size] = keep[...]
                weight_ref[n, :, size:] = send[...]

        for k in range(calls):
            act = acts[k * sides + n]
            act_ref[n, :, k * cols : (k + 1) * cols] = act[:, :cols]
            act_ref[n, :, (calls + k) * cols : (calls + k + 1) * cols] = act[:, cols:]
        sums[n][...] = product(act_ref[n], weight_ref[n])
    return functools.reduce(lambda u, v: u + v, [r[...] for r in sums])


def output_kernel(count, sides, *refs):
    acts, weights = refs[:count], refs[count : count + 2 * sides]
    t_ref, ob_ref, g_ref, b_ref, mid_ref, n_ref, *scratch = refs[count + 2 * sides :]
    near = balanced(acts, weights, dot, True, scratch)
    middle = t_ref[...].astype(F32) + near + ob_ref[...]
    mid_ref[...] = middle
    n_ref[...] = normed(middle, g_ref[...], b_ref[...]).astype(BF16)


def feed_tile(x, c, w, v, bias):
    before = dot(x, w) + bias
    grad = dot_nt(c, v)
    square = before * before
    t = jnp.tanh(before * (GELU_A + (GELU_A * GELU_B) * square))
    half = 0.5 + 0.5 * t
    slope = half + before * (half * (1.0 - t)) * (GELU_A + (3.0 * GELU_A * GELU_B) * square)
    return (before * half).astype(BF16), grad * slope


def stack(scratch, first, second):
    rows = first.shape[0]
    scratch[:rows, :] = first[...]
    scratch[rows:, :] = second[...]


def add_to(ref, value, fresh):
    @pl.when(fresh)
    def _():
        ref[...] = jnp.zeros_like(ref)

    ref[...] += jnp.broadcast_to(value, ref.shape)


def feed_near_kernel(blk, xa_ref, xb_ref, ca_ref, cb_ref, w_ref, v_ref, b_ref, ha_ref, hb_ref, da_ref, db_ref, sum_ref, x_ref, c_ref):
    rows = xa_ref.shape[0]
    stack(x_ref, xa_ref, xb_ref)
    stack(c_ref, ca_ref, cb_ref)
    sums = []
    for at in range(0, w_ref.shape[1], blk):
        cut = slice(at, at + blk)
        hidden, grad = feed_tile(x_ref[...], c_ref[...], w_ref[:, cut], v_ref[cut, :], b_ref[:, cut])
        low = grad.astype(BF16)
        ha_ref[:, cut] = hidden[:rows]
        hb_ref[:, cut] = hidden[rows:]
        da_ref[:, cut] = low[:rows]
        db_ref[:, cut] = low[rows:]
        sums.append(jnp.sum(grad, 0, keepdims=True))
    add_to(sum_ref, jnp.concatenate(sums, 1), pl.program_id(0) == 0)


def feed_far_kernel(steps, xa_ref, xb_ref, ca_ref, cb_ref, b_ref, ea_ref, eb_ref, u_ref, *rest):
    w_refs, z_refs, v_ref = rest[:steps], rest[steps : 2 * steps], rest[2 * steps]
    ga_ref, gb_ref, ha_ref, hb_ref, da_ref, db_ref, sum_ref, x_ref, c_ref, e_ref, low_ref = rest[-11:]
    i = pl.program_id(0)
    rows = xa_ref.shape[0]

    @pl.when(i == 0)
    def _():
        stack(x_ref, xa_ref, xb_ref)
        stack(c_ref, ca_ref, cb_ref)
        stack(e_ref, ea_ref, eb_ref)

    for k in range(steps):

        @pl.when(i == k)
        def _():
            hidden, grad = feed_tile(x_ref[...], c_ref[...], w_refs[k][...], v_ref[...], b_ref[...])
            low = grad.astype(BF16)
            ha_ref[...] = hidden[:rows]
            hb_ref[...] = hidden[rows:]
            da_ref[...] = low[:rows]
            db_ref[...] = low[rows:]
            low_ref[k] = low
            sum_ref[...] = jnp.broadcast_to(jnp.sum(grad, 0, keepdims=True), sum_ref.shape)

    @pl.when(i >= steps)
    def _():
        total = dot_nt(e_ref[...], u_ref[...])
        for k in range(steps):
            total = total + dot_nt(low_ref[k], z_refs[k][...])
        ga_ref[...] = total[:rows].astype(BF16)
        gb_ref[...] = total[rows:].astype(BF16)


def feed_near(chunk, first_row, x_own, x_other, c_own, c_other, w, v, bias):
    rows, width = x_own.shape
    hid = w.shape[1]
    base = first_row // chunk
    at = lambda i: (i, 0)
    at_all = lambda i: (base + i, 0)
    return call(
        functools.partial(feed_near_kernel, min(512, hid)),
        (rows // chunk,),
        [
            (x_own, (chunk, width), at),
            (x_other, (chunk, width), at),
            (c_own, (chunk, width), at_all),
            (c_other, (chunk, width), at_all),
            whole(w),
            whole(v),
            whole(bias),
        ],
        [((rows, hid), BF16, (chunk, hid), at)] * 4 + [((8, hid), F32, (8, hid), lambda i: (0, 0))],
        scratch=[pltpu.VMEM((2 * chunk, width), BF16)] * 2,
        vmem=56,
        flops=8 * rows * width * hid,
        moved=8 * width * hid + 8 * rows * width,
    )


def feed_far(chunk, index, first_row, x_own, x_other, c_own, c_other, w, v, bias, near_own, near_other, w_near, kept):
    rows, width = x_own.shape
    hid = w_near.shape[1]
    steps = len(w)
    blk = hid // steps
    out_blk = min(512, width)
    back = width // out_blk
    base = first_row // chunk
    at = lambda i: (index, 0)
    at_all = lambda i: (base + index, 0)
    tile = lambda i: jnp.minimum(i, steps - 1)
    after = lambda i: jnp.maximum(i - steps, 0)
    ins = [
        (x_own, (chunk, width), at),
        (x_other, (chunk, width), at),
        (c_own, (chunk, width), at_all),
        (c_other, (chunk, width), at_all),
        (bias, (1, blk), lambda i: (0, tile(i))),
        (near_own, (chunk, hid), at),
        (near_other, (chunk, hid), at),
        (w_near, (out_blk, hid), lambda i: (after(i), 0)),
    ]
    ins += [whole(p) for p in w]
    ins += [(p, (out_blk, blk), lambda i: (after(i), 0)) for p in w]
    ins += [(v, (blk, width), lambda i: (tile(i), 0))]
    outs = [((chunk, width), BF16, (chunk, out_blk), lambda i: (0, after(i)))] * 2
    outs += [((rows, hid), BF16, (chunk, blk), lambda i: (index, tile(i)))] * 4
    outs += [((8, hid), F32, (8, blk), lambda i: (0, tile(i)))]
    alias = {}
    arrays = [a for a, _, _ in ins]
    specs = [
        pl.BlockSpec(b, m, pipeline_mode=pl.Buffered(1)) if b == a.shape else pl.BlockSpec(b, m) for a, b, m in ins
    ]
    if kept is not None:
        for place, array in enumerate(kept):
            alias[len(arrays)] = 2 + place
            arrays.append(array)
            specs.append(pl.BlockSpec(memory_space=pl.ANY))
    result = pl.pallas_call(
        functools.partial(feed_far_kernel, steps),
        grid=(steps + back,),
        in_specs=specs,
        out_specs=[pl.BlockSpec(b, m) for _, _, b, m in outs],
        out_shape=[jax.ShapeDtypeStruct(s, d) for s, d, _, _ in outs],
        scratch_shapes=[
            pltpu.VMEM((2 * chunk, width), BF16),
            pltpu.VMEM((2 * chunk, width), BF16),
            pltpu.VMEM((2 * chunk, hid), BF16),
            pltpu.VMEM((steps, 2 * chunk, blk), BF16),
        ],
        input_output_aliases=alias,
        compiler_params=pltpu.CompilerParams(vmem_limit_bytes=56 * MIB),
        cost_estimate=pl.CostEstimate(
            flops=8 * 2 * chunk * width * hid, bytes_accessed=8 * width * hid + 24 * chunk * width, transcendentals=0
        ),
    )(*arrays)
    return result[:2], result[2:6], result[6]


def contract_kernel(count, *refs):
    near, far = refs[:count], refs[count : 2 * count]
    va_ref, vb_ref, own_ref, other_ref = refs[2 * count :]
    size = near[0].shape[0]
    for k in range(count):
        y_ref = own_ref if k < count // 2 else other_ref
        at = k % (count // 2) * size
        y_ref[at : at + size, :] = (dot(near[k][...], va_ref[...]) + dot(far[k][...], vb_ref[...])).astype(BF16)


def pair_grad_kernel(*refs):
    out_ref = refs[-1]
    count = (len(refs) - 1) // 2
    total = None
    for left, right in zip(refs[:count], refs[count:-1]):
        piece = dot_tn(left[...], right[...])
        total = piece if total is None else total + piece
    out_ref[...] = total.astype(BF16)


def second_back_kernel(count, *refs):
    firsts, seconds = refs[:count], refs[count : 2 * count]
    mid_ref, cot_ref, gain_ref, wk_ref, ws_ref, gm_ref, low_ref, keep_ref, send_ref, sums_ref = refs[2 * count :]
    size = firsts[0].shape[0]
    totals = [0.0, 0.0, 0.0, 0.0]
    for k in range(count):
        at = slice(k * size, (k + 1) * size)
        grad = firsts[k][...].astype(F32) + seconds[k][...].astype(F32)
        xhat, back = norm_back(mid_ref[at, :], grad, gain_ref[...])
        cot = cot_ref[at, :].astype(F32)
        total = cot + back
        gm_ref[at, :] = total
        low_ref[at, :] = total.astype(BF16)
        for n, value in enumerate((grad * xhat, grad, total, cot)):
            totals[n] = totals[n] + jnp.sum(value, 0, keepdims=True)
    send_ref[...] = dot_nt(low_ref[...], ws_ref[...]).astype(BF16)
    keep_ref[...] = dot_nt(low_ref[...], wk_ref[...]).astype(BF16)
    for n in range(4):
        sums_ref[n : n + 1, :] = totals[n]


def first_back_kernel(count, sides, *refs):
    acts, weights = refs[:count], refs[count : count + 2 * sides]
    kv_ref, kvw_ref, t_ref, gm_ref, gain_ref, out_ref, sums_ref, *scratch = refs[count + 2 * sides :]
    grad = balanced(acts, weights, dot_nt, False, scratch) + dot_nt(kv_ref[...], kvw_ref[...])
    xhat, back = norm_back(t_ref[...].astype(F32), grad, gain_ref[...])
    out_ref[...] = (gm_ref[...] + back).astype(BF16)

    @pl.when(pl.program_id(0) == 0)
    def _():
        sums_ref[...] = jnp.zeros_like(sums_ref)

    sums_ref[0:1, :] += jnp.sum(grad * xhat, 0, keepdims=True)
    sums_ref[1:2, :] += jnp.sum(grad, 0, keepdims=True)


def body(
    tokens,
    segment_lengths,
    pre_norm_gain,
    pre_norm_bias,
    query_weight,
    query_bias,
    key_value_weight,
    value_bias,
    output_weight,
    output_bias,
    mlp_norm_gain,
    mlp_norm_bias,
    expand_weight,
    expand_bias,
    contract_weight,
    contract_bias,
    cotangent,
):
    rows, width = tokens.shape
    n_heads, n_rows, n_dp = (lax.axis_size(a) for a in ("heads", "rows", "dp"))
    row_index = lax.axis_index("rows")
    core = lax.rem(row_index, 2)
    dim = key_value_weight.shape[1] // 2
    local_heads = query_weight.shape[1] // dim
    group = local_heads // 2
    cols = group * dim
    window = rows * n_rows
    scale = 1.0 / math.sqrt(dim)
    hid = expand_weight.shape[1]

    chips = n_rows // 2
    chip = row_index // 2
    dp_index = lax.axis_index("dp")

    def near(value):
        return lax.ppermute(value, "rows", [(i, i ^ 1) for i in range(n_rows)])

    def far(value):
        return lax.ppermute(value, "rows", [(i, i ^ 2) for i in range(n_rows)])

    def across(value):
        return lax.ppermute(value, "heads", [(0, 1), (1, 0)])

    def beside(value):
        return lax.ppermute(value, "dp", [(i, i ^ 1) for i in range(n_dp)])

    def line(vector):
        return vector.reshape(1, -1)

    def tie(*values):
        return lax.optimization_barrier(values)

    def add(*terms):
        return functools.reduce(lambda u, v: u + v, (t.astype(F32) for t in terms)).astype(BF16)

    def ordered(bit, mine, other, axis):
        return jnp.where(bit == 0, jnp.concatenate([mine, other], axis), jnp.concatenate([other, mine], axis))

    def heads_sum(value):
        if n_heads == 2:
            return value, across(value)
        total = lax.psum(value.astype(F32), "heads")
        high = total.astype(BF16)
        return high, (total - high.astype(F32)).astype(BF16)

    last = n_dp - 1

    class Chain:
        def __init__(self, value):
            self.value, self.size = value, value.shape[0] // n_dp
            self.up = self.down = self.out = None
            self.t = 0

        def piece(self, index):
            return lax.dynamic_slice_in_dim(self.value, jnp.clip(index, 0, last) * self.size, self.size, 0)

        def put(self, part, place):
            self.out = lax.dynamic_update_slice_in_dim(self.out, part, (place + last) * self.size, 0)

        def step(self):
            t, self.t = self.t, self.t + 1
            if t < last:
                up, down = self.piece(last + dp_index - t), self.piece(dp_index - last + t)
                if t > 0:
                    up, down = add(up, self.up), add(down, self.down)
                ends = range(t + 1)
            else:
                if t == last:
                    own = add(self.piece(dp_index), self.up, self.down)
                    self.out = jnp.zeros(((3 * n_dp - 2) * self.size,) + own.shape[1:], BF16)
                    self.put(own, dp_index)
                    up = down = own
                else:
                    up, down = self.up, self.down
                ends = range(t - last, last)
            self.up = lax.ppermute(up, "dp", [(i, i + 1) for i in ends])
            self.down = lax.ppermute(down, "dp", [(last - i, last - i - 1) for i in ends])
            if t >= last:
                self.put(self.up, dp_index - 1 - (t - last))
                self.put(self.down, dp_index + 1 + (t - last))

        def result(self):
            while self.t < 2 * last:
                self.step()
            return self.out[last * self.size : (last + n_dp) * self.size]

    def together(chains, behind):
        for chain, values in zip(chains + behind, held(chains + behind)):
            if chain.t == 0:
                (chain.value,) = values
            else:
                chain.up, chain.down = values
        for chain in chains:
            chain.step()

    def held(chains):
        flat = [v for c in chains for v in ([c.value] if c.t == 0 else [c.up, c.down])]
        flat = list(tie(*flat))
        return [[flat.pop(0) for _ in range(1 if c.t == 0 else 2)] for c in chains]

    def landed(chains, *values):
        for chain in chains:
            chain.up, chain.down, *values = tie(chain.up, chain.down, *values)
        return values

    def small_sum(value):
        for axis, size in (("rows", n_rows), ("dp", n_dp)):
            hop = 1
            while hop < size:
                value = value + lax.ppermute(value, axis, [(i, i ^ hop) for i in range(size)])
                hop *= 2
        return value

    keep_at, send_at = core * cols, (1 - core) * cols
    out_keep = lax.dynamic_slice_in_dim(output_weight, keep_at, cols, 0)
    out_send = lax.dynamic_slice_in_dim(output_weight, send_at, cols, 0)
    query_keep = lax.dynamic_slice_in_dim(query_weight, keep_at, cols, 1)
    query_send = lax.dynamic_slice_in_dim(query_weight, send_at, cols, 1)

    sides = 2 if n_heads == 2 else 1
    other_head = 1 - lax.axis_index("heads")

    def heads_acts(value):
        if n_heads == 2:
            return [value, across(value)]
        size = value.shape[1] // 2
        return [
            jnp.concatenate([lax.all_gather(v, "heads", axis=1, tiled=True) for v in (value[:, :size], value[:, size:])], 1)
        ]

    def heads_weights(keep, send, axis):
        whole_keep = lax.all_gather(keep, "heads", axis=axis, tiled=True)
        if n_heads > 2:
            return [whole_keep, near(whole_keep)]
        other = lax.dynamic_slice_in_dim(whole_keep, other_head * keep.shape[axis], keep.shape[axis], axis)
        return [keep, send, other, near(other)]

    expand_bias_far = far(expand_bias)
    cot_near = near(cotangent)

    blk = min(256, rows)
    grid = (rows // blk,)
    kv_bias = jnp.concatenate([jnp.zeros((dim,), F32), value_bias])
    normed_first, key_value = call(
        norm_kv_kernel,
        grid,
        [rows_of(tokens, blk), whole(line(pre_norm_gain)), whole(line(pre_norm_bias)), whole(key_value_weight), whole(line(kv_bias))],
        [
            ((rows, width), BF16, (blk, width), lambda i: (i, 0)),
            ((rows, 2 * dim), BF16, (blk, 2 * dim), lambda i: (i, 0)),
        ],
        flops=4 * rows * width * dim,
        moved=4 * rows * width,
    )
    far_kv = far(key_value)
    near_kv = near(key_value)
    far_kv, expand_start, contract_start = tie(far_kv, expand_weight, contract_weight)
    pieces = hid // min(512, hid)
    size = hid // pieces
    expand_far = [far(expand_start[:, :size])]
    columns = [[g + 2 * b for b in range(chips)] for g in range(2)]
    contract_both = lax.all_gather(contract_start, "rows", axis=0, tiled=True, axis_index_groups=columns)
    contract_far = lax.dynamic_slice_in_dim(contract_both, (1 - chip) * hid, hid, 0)
    pair_kv = ordered(core, key_value, near_kv, 0)
    far_pair = ordered(core, far_kv, near(far_kv), 0)
    kv_whole = ordered(chip, pair_kv, far_pair, 0)
    kv_turned = kv_whole.T

    query_a, query_for_near = call(
        project_kernel,
        grid,
        [
            (core.reshape(1), None, None),
            rows_of(normed_first, blk),
            (query_weight, (width, cols), lambda i, core: (0, core[0])),
            (line(query_bias), (1, cols), lambda i, core: (0, core[0])),
            (query_weight, (width, cols), lambda i, core: (0, 1 - core[0])),
            (line(query_bias), (1, cols), lambda i, core: (0, 1 - core[0])),
        ],
        [((rows, cols), BF16, (blk, cols), lambda i, *_: (i, 0))] * 2,
        prefetch=1,
        flops=4 * rows * width * cols,
        moved=2 * rows * width,
    )
    query_b = near(query_for_near)

    ends = jnp.cumsum(segment_lengths[0])
    own_place = row_index * rows
    near_place = (row_index + 1 - 2 * core) * rows
    steps = jnp.arange(rows, dtype=jnp.int32)
    places = jnp.concatenate([own_place + steps, near_place + steps])
    starts = jnp.max(jnp.where(ends[None, :] <= places[:, None], ends[None, :], 0), 1).astype(jnp.int32)

    def blocks_of(block):
        bq, bk = min(block[0], rows), min(block[1], window)
        first = places.reshape(-1, bq)[:, 0]
        start = starts.reshape(-1, bq)
        info = [first, start[:, 0] // bk, (first + bq - 1) // bk + 1, (start[:, -1] + bk - 1) // bk, (first + 1) // bk]
        return bq, bk, rows // bq, (jnp.stack(info).astype(jnp.int32), None, None)

    start_row = starts.reshape(1, -1)
    calls = 2 if group % 2 == 0 else 1
    part_heads = group // calls
    part_cols = part_heads * dim
    pairs_guess = 2 * rows * window // 4
    bq, bk, half, scalars = blocks_of(FORWARD_BLOCK)

    def at_a(n, half):
        return lambda i, *_: (jnp.minimum(i, half - 1), n)

    def at_b(n, half):
        return lambda i, *_: (jnp.maximum(i - half, 0), n)

    def attn_forward(n, info):
        return call(
            functools.partial(attn_forward_kernel, part_heads, half, bk, scale * LOG2E),
            (2 * half,),
            [
                (info, None, None),
                (query_a, (bq, part_cols), at_a(n, half)),
                (query_b, (bq, part_cols), at_b(n, half)),
                whole(kv_whole),
                (kv_turned, (dim, window), lambda i, *_: (1, 0)),
                (start_row, (1, bq), lambda i, *_: (0, i)),
            ],
            [
                ((rows, part_cols), BF16, (bq, part_cols), at_a(0, half)),
                ((rows, part_cols), BF16, (bq, part_cols), at_b(0, half)),
                ((part_heads, 2 * rows), F32, (part_heads, bq), lambda i, *_: (0, i)),
            ],
            scratch=[pltpu.VMEM((part_heads, bq), F32), pltpu.VMEM((part_heads, bq), F32), pltpu.VMEM((part_heads, dim, bq), F32)],
            prefetch=1,
            vmem=40,
            flops=16 * pairs_guess * part_cols,
            moved=8 * rows * part_cols,
        )

    attn, acts = [], []
    out_all = heads_weights(out_keep, out_send, 0)
    info = scalars[0]
    for n in range(calls):
        if n == 1:
            info, acts[0], expand_far[0] = tie(info, acts[0], expand_far[0])
        own, for_near, lse = attn_forward(n, info)
        if n == 0:
            expand_start, lse = tie(expand_start, lse)
            expand_far += [far(expand_start[:, k * size : (k + 1) * size]) for k in range(1, pieces)]
        other = near(for_near)
        attn.append((own, other, for_near, lse))
        acts.append(jnp.concatenate([own, other], 1))
    acts = [a for act in acts for a in heads_acts(act)]
    acts[-1], expand_far[-1] = tie(acts[-1], expand_far[-1])

    halves = 2
    part_rows = rows // halves
    wide = min(512, part_rows)
    chunk = min(256, part_rows)
    sub = part_rows // chunk
    down = lambda i: (i, 0)

    def output_part(j):
        base = j * part_rows // wide
        at = lambda i: (base + i, 0)
        return call(
            functools.partial(output_kernel, len(acts), sides),
            (part_rows // wide,),
            [(a, (wide, a.shape[1]), at) for a in acts]
            + [whole(w) for w in out_all]
            + [(tokens, (wide, width), at), whole(line(output_bias)), whole(line(mlp_norm_gain)), whole(line(mlp_norm_bias))],
            [((part_rows, width), F32, (wide, width), down), ((part_rows, width), BF16, (wide, width), down)],
            flops=2 * part_rows * width * width,
            moved=20 * part_rows * width,
            vmem=60,
            scratch=[
                pltpu.VMEM((sides, wide, width // sides), BF16),
                pltpu.VMEM((sides, width // sides, width), BF16),
            ]
            + [pltpu.VMEM((wide, width), F32)] * sides,
        )

    middles, seconds, others = [], [], []
    for j in range(halves):
        middle, normed_second = output_part(j)
        middles.append(middle)
        seconds.append(normed_second)
        others.append(near(normed_second))

    near_parts = [
        list(feed_near(
            chunk, j * part_rows, seconds[j], others[j], cotangent, cot_near, expand_weight, contract_weight, line(expand_bias)
        ))
        for j in range(halves)
    ]
    far_parts, far_sums, grads, sums_own = [], [], [], []
    for j in range(halves):
        kept = None
        for k in range(sub):
            far_bias = line(expand_bias_far)
            if sums_own:
                far_bias, sums_own[-1] = tie(far_bias, sums_own[-1])
            if len(grads) >= 3:
                far_bias, *grads[-3] = tie(far_bias, *grads[-3])
            (g_own, g_near), kept, bias_sum = feed_far(
                chunk,
                k,
                j * part_rows,
                seconds[j],
                others[j],
                cotangent,
                cot_near,
                expand_far,
                contract_far,
                far_bias,
                near_parts[j][2],
                near_parts[j][3],
                expand_weight,
                kept,
            )
            far_sums.append(bias_sum[0])
            sums_own.append(add(g_own, near(g_near)))
            grads.append(None)
            for m in range(len(grads)):
                if grads[m] is None and m < len(sums_own) - 1:
                    grads[m] = list(heads_sum(sums_own[m]))
        far_parts.append(list(kept))

    grads[-1] = list(heads_sum(sums_own[-1]))

    hblk = min(512, hid)
    n_blk = hid // hblk

    def contract_grad(parts, at, count):
        lefts = [(p[n], (part_rows, hblk), lambda i: (0, at + i)) for n in range(2) for p in parts]
        rights = [(c, (part_rows, width), lambda i, j=j: (j, 0)) for c in (cotangent, cot_near) for j in range(halves)]
        return call(
            pair_grad_kernel,
            (count,),
            lefts + rights,
            [((count * hblk, width), BF16, (hblk, width), down)],
            flops=4 * 2 * rows * width * hblk * count,
            moved=8 * width * rows,
            vmem=56,
        )[0]

    def expand_grad(parts, at, count):
        lefts = [(x, (part_rows, hblk), lambda i: (0, at + i)) for x in seconds + others]
        rights = [whole(p[n]) for n in (2, 3) for p in parts]
        return call(
            pair_grad_kernel,
            (count,),
            lefts + rights,
            [((count * hblk, hid), BF16, (hblk, hid), down)],
            flops=4 * 2 * rows * hblk * hid * count,
            moved=8 * width * rows,
            vmem=56,
        )[0]

    far_parts[1][3], *grads[1] = tie(far_parts[1][3], *grads[1])
    contract_send = contract_grad(far_parts, 0, n_blk)
    contract_moved = far(contract_send)
    expand_send = expand_grad(far_parts, 0, width // hblk)
    near_parts[1][3], expand_send, *grads[2] = tie(near_parts[1][3], expand_send, *grads[2])
    contract_own = contract_grad(near_parts, 0, n_blk)
    expand_own = expand_grad(near_parts, 0, width // hblk)
    bias_near = near_parts[0][4][0] + near_parts[1][4][0]
    bias_far = functools.reduce(lambda u, v: u + v, far_sums)
    expand_send, contract_moved = tie(expand_send, contract_moved)
    expand_moved = far(expand_send)
    grads[0][0], contract_own, expand_own = tie(grads[0][0], contract_own, expand_own)

    gms, lows, keeps, sends, sums = [], [], [], [], []
    for j in range(halves):
        terms = grads[j * sub : (j + 1) * sub]
        at = lambda i, j=j: (j, 0)
        gm, low, keep, send, part = call(
            functools.partial(second_back_kernel, sub),
            (1,),
            [whole(t[0]) for t in terms]
            + [whole(t[1]) for t in terms]
            + [
                whole(middles[j]),
                (cotangent, (part_rows, width), at),
                whole(line(mlp_norm_gain)),
                whole(out_keep),
                whole(out_send),
            ],
            [
                ((part_rows, width), F32, (part_rows, width), lambda i: (0, 0)),
                ((part_rows, width), BF16, (part_rows, width), lambda i: (0, 0)),
                ((part_rows, cols), BF16, (part_rows, cols), lambda i: (0, 0)),
                ((part_rows, cols), BF16, (part_rows, cols), lambda i: (0, 0)),
                ((8, width), F32, (8, width), lambda i: (0, 0)),
            ],
            flops=4 * part_rows * width * cols,
            moved=16 * part_rows * width + 4 * width * cols,
            vmem=58,
        )
        gms.append(gm)
        lows.append(low)
        keeps.append(keep)
        sends.append(near(send))
        sums.append(part[:4])
    grad_low = jnp.concatenate(lows)
    grad_middle = jnp.concatenate(gms)
    grad_a, grad_b = jnp.concatenate(keeps), jnp.concatenate(sends)
    mid_sums = functools.reduce(lambda u, v: u + v, sums)

    query_all = heads_weights(query_keep, query_send, 1)

    def dot_left(left, right):
        return dot_tn(left, right).astype(BF16)

    def chips_half(block):
        size = block.shape[0] // chips
        mine = lax.dynamic_slice_in_dim(block, chip * size, size, 0)
        other = lax.dynamic_slice_in_dim(block, (1 - chip) * size, size, 0)
        return mine, far(other)

    def all_blocks(total):
        pair = ordered(chip, total, far(total), 0)
        return pair, near(pair)

    contract_sum = add(contract_own, contract_moved)

    bq, bk, half, scalars = blocks_of(BACKWARD_BLOCK)

    def attn_backward(n, info):
        own, other, for_near, lse = attn[n]
        return call(
            functools.partial(attn_backward_kernel, part_heads, half, bk, scale, scale * LOG2E),
            (2 * half,),
            [
                (info, None, None),
                (query_a, (bq, part_cols), at_a(n, half)),
                (query_b, (bq, part_cols), at_b(n, half)),
                (grad_a, (bq, part_cols), at_a(n, half)),
                (grad_b, (bq, part_cols), at_b(n, half)),
                (own, (bq, part_cols), at_a(0, half)),
                (for_near, (bq, part_cols), at_b(0, half)),
                whole(kv_whole),
                (kv_turned, (dim, window), lambda i, *_: (0, 0)),
                (start_row, (1, bq), lambda i, *_: (0, i)),
                (lse, (part_heads, bq), lambda i, *_: (0, i)),
            ],
            [
                ((rows, part_cols), BF16, (bq, part_cols), at_a(0, half)),
                ((rows, part_cols), BF16, (bq, part_cols), at_b(0, half)),
                ((window, 2 * dim), F32, (window, 2 * dim), lambda i, *_: (0, 0)),
            ],
            scratch=[pltpu.VMEM((part_heads, dim, bq), F32)],
            prefetch=1,
            vmem=48,
            flops=40 * pairs_guess * part_cols,
            moved=16 * rows * part_cols,
        )

    back_acts, dq_own, dq_other, dkv = [], [], [], None
    info = scalars[0]
    for n in range(calls):
        if n == 0:
            info, contract_sum = tie(info, contract_sum)
            contract_total = lax.psum(contract_sum, "dp")
        if n == 1:
            info, back_acts[0], expand_moved = tie(info, back_acts[0], expand_moved)
        own, for_near, dkv_part = attn_backward(n, info)
        other = near(for_near)
        dq_own.append(own)
        dq_other.append(other)
        back_acts.append(jnp.concatenate([own, other], 1))
        dkv = dkv_part if dkv is None else dkv + dkv_part
    back_acts = [a for act in back_acts for a in heads_acts(act)]

    count = 2 * halves
    out_cols = min(512, width)
    near_parts[0][0], dkv = tie(near_parts[0][0], dkv)
    mlp_own, mlp_near = call(
        functools.partial(contract_kernel, count),
        (width // out_cols,),
        [whole(p[n]) for n in range(2) for p in near_parts]
        + [whole(p[n]) for n in range(2) for p in far_parts]
        + [(v, (hid, out_cols), lambda i: (0, i)) for v in (contract_weight, contract_far)],
        [((rows, width), BF16, (rows, out_cols), lambda i: (0, i))] * 2,
        flops=8 * rows * width * hid,
        moved=16 * rows * width,
        vmem=56,
    )

    dkv = dkv.reshape(chips, 2, rows, 2 * dim)

    def half_of(value, axis, bit):
        return lax.dynamic_index_in_dim(value, bit, axis, keepdims=False)

    core_sum = half_of(dkv, 1, core) + near(half_of(dkv, 1, 1 - core).astype(BF16)).astype(F32)
    chip_sum = add(half_of(core_sum, 0, chip), far(half_of(core_sum, 0, 1 - chip).astype(BF16)))
    first, second = heads_sum(chip_sum)
    grad_kv = add(first, second)

    input_grad, first_sums = call(
        functools.partial(first_back_kernel, len(back_acts), sides),
        (rows // wide,),
        [rows_of(a, wide) for a in back_acts]
        + [whole(w) for w in query_all]
        + [rows_of(grad_kv, wide), whole(key_value_weight)]
        + [rows_of(tokens, wide), rows_of(grad_middle, wide), whole(line(pre_norm_gain))],
        [((rows, width), BF16, (wide, width), down), ((8, width), F32, (8, width), lambda i: (0, 0))],
        flops=2 * rows * width * (width + 2 * dim),
        moved=20 * rows * width,
        vmem=60,
        scratch=[
            pltpu.VMEM((sides, wide, width // sides), BF16),
            pltpu.VMEM((sides, width, width // sides), BF16),
        ]
        + [pltpu.VMEM((wide, width), F32)] * sides,
    )

    mlp_first, mlp_second = heads_sum(add(mlp_own, near(mlp_near)))
    mlp_total = mlp_first.astype(F32) + mlp_second.astype(F32)
    layer_output = (jnp.concatenate(middles) + mlp_total + contract_bias).astype(BF16)

    own_all = jnp.concatenate([a[0] for a in attn], 1)
    other_all = jnp.concatenate([a[1] for a in attn], 1)
    out_half = add(*chips_half(add(dot_left(own_all, grad_low), near(dot_left(other_all, grad_low)))))
    expand_size = width // n_dp
    out_size = out_half.shape[0] * width // hid // n_dp
    joined = jnp.concatenate(
        [add(expand_own, expand_moved).reshape(n_dp, expand_size, hid), out_half.reshape(n_dp, out_size, hid)], 1
    )
    expand_chain = Chain(joined.reshape(-1, hid))
    kv_keep = lax.dynamic_slice_in_dim(grad_kv, core * dim, dim, 1)
    kv_send = lax.dynamic_slice_in_dim(grad_kv, (1 - core) * dim, dim, 1)
    query_sent = near(dot_left(normed_first, jnp.concatenate(dq_other + [kv_send], 1)))
    query_block = add(dot_left(normed_first, jnp.concatenate(dq_own + [kv_keep], 1)), query_sent)
    query_chain = Chain(add(*chips_half(query_block)))
    expand_chain.step()
    expand_chain.step()
    expand_chain.step()
    expand_chain.up, contract_total = tie(expand_chain.up, contract_total)
    for _ in range(3):
        together([expand_chain, query_chain], [])
    contract_weight_grad = contract_total.astype(F32)
    joined = expand_chain.result().reshape(n_dp, -1, hid)
    expand_weight_grad = joined[:, :expand_size].reshape(width, hid).astype(F32)
    out_block, out_block_near = all_blocks(joined[:, expand_size:].reshape(out_half.shape))
    output_weight_grad = ordered(core, out_block, out_block_near, 0).astype(F32)
    query_block, query_block_near = all_blocks(query_chain.result())
    query_weight_grad = ordered(core, query_block[:, :cols], query_block_near[:, :cols], 1).astype(F32)
    key_value_weight_grad = ordered(core, query_block[:, cols:], query_block_near[:, cols:], 1).astype(F32)

    dq_bias_keep = jnp.concatenate([jnp.sum(v.astype(F32), 0) for v in dq_own])
    dq_bias_send = jnp.concatenate([jnp.sum(v.astype(F32), 0) for v in dq_other])
    query_bias_part = ordered(core, dq_bias_keep, dq_bias_send, 0)
    value_bias_part = jnp.sum(grad_kv[:, dim:].astype(F32), 0)

    mid_total = lax.psum(mid_sums, ("dp", "rows"))
    late = small_sum(jnp.concatenate([first_sums[0], first_sums[1], query_bias_part, value_bias_part]))
    local = query_bias_part.shape[0]
    expand_bias_grad = bias_near + far(bias_far)
    hop = 1
    while hop < n_dp:
        expand_bias_grad = expand_bias_grad + lax.ppermute(expand_bias_grad, "dp", [(i, i ^ hop) for i in range(n_dp)])
        hop *= 2
    return (
        layer_output,
        input_grad,
        late[:width],
        late[width : 2 * width],
        query_weight_grad,
        late[2 * width : 2 * width + local],
        key_value_weight_grad,
        late[2 * width + local :],
        output_weight_grad,
        mid_total[2],
        mid_total[0],
        mid_total[1],
        expand_weight_grad,
        expand_bias_grad,
        contract_weight_grad,
        mid_total[3],
    )


def solution(mesh):
    both = P(("heads", "rows"))
    in_specs = (
        P(("dp", "rows"), None),
        P("dp", None),
        P(),
        P(),
        P(None, "heads"),
        P("heads"),
        P(),
        P(),
        P("heads", None),
        P(),
        P(),
        P(),
        P(None, ("heads", "rows")),
        both,
        P(("heads", "rows"), None),
        P(),
        P(("dp", "rows"), None),
    )
    out_specs = (
        P(("dp", "rows"), None),
        P(("dp", "rows"), None),
        P(),
        P(),
        P(None, "heads"),
        P("heads"),
        P(),
        P(),
        P("heads", None),
        P(),
        P(),
        P(),
        P(None, ("heads", "rows")),
        both,
        P(("heads", "rows"), None),
        P(),
    )
    return jax.shard_map(body, mesh=mesh, in_specs=in_specs, out_specs=out_specs, check_vma=False)
```

time: 2910 us -> 1200 us (0.41)
  waiting for transfers between devices: 1790 us -> 379 us
  matrix products: 824 us -> 22 us
  Pallas kernels: 0 us -> 358 us
  starting transfers between devices: 0.75 us -> 152 us
  local copies, waits for them, and re-layouts: 69.2 us -> 111 us
    psum x3 -> x1, waiting for transfers between devices: 952 us -> 0.02 us  [body(): contract_total = lax.psum(contract_sum, 'dp')]
    dot_general x29 -> x4, matrix products: 824 us -> 22 us  [dot_tn(): lax.dot_general(left, right, (((0,), (0,)), ((), ())), preferred_element_...]
    reduce_scatter x5 -> x0, waiting for transfers between devices: 609 us -> none  [the longest x1 204 us: body(): lax.psum_scatter(jnp.dot(piece_rows, contract_weight, preferred_element_t...]
    ppermute x0 -> x76, waiting for transfers between devices: none -> 371 us  [the longest x12 219 us: far(): return lax.ppermute(value, 'rows', [(i, i ^ 2) for i in range(n_rows)])]
    pallas_call x0 -> x22, Pallas kernels: none -> 358 us  [the longest x18 286 us: call(): pl.pallas_call(kernel, grid_spec=pltpu.PrefetchScalarGridSpec(num_scalar_...]
    all_gather x6 -> x3, waiting for transfers between devices: 227 us -> 8.28 us  [the longest x1 8.26 us: body(): lax.all_gather(contract_start, 'rows', axis=0, tiled=True, axis_index_gro...]
    ppermute x0 -> x76, starting transfers between devices: none -> 151 us  [the longest x12 69.3 us: step(): self.up = lax.ppermute(up, 'dp', [(i, i + 1) for i in ends])]
    reduce_sum x14 -> x5, other arithmetic: 73.8 us -> 0.76 us  [the longest x2 0.3 us: body(): jnp.sum(v.astype(F32), 0)]
  transfers between devices with their start and end apart: 14 -> 80, of which waited for: 12 -> 27; matrix products, arithmetic and copies ran while one was open for 6% -> 15% of each run, Pallas kernels for 0% -> 28%
where the time goes in v1:
time: 1200 us
  waiting for transfers between devices  379 us (32%)
  Pallas kernels  358 us (30%)
  starting transfers between devices  152 us (13%)
  local copies, waits for them, and re-layouts  111 us (9%)
  other arithmetic  102 us (8%)
  blocking collectives  57.6 us (5%)
  matrix products  22 us (2%)
  between operations  15.4 us (1%)
    pallas_call x18, Pallas kernels, call(): pl.pallas_call(kernel, grid_spec=pltpu.PrefetchScalarGridSpec(num_scalar_...  286 us
    ppermute x12, waiting for transfers between devices, far(): return lax.ppermute(value, 'rows', [(i, i ^ 2) for i in range(n_rows)])  219 us
    pallas_call x4, Pallas kernels, feed_far(): pl.pallas_call(functools.partial(feed_far_kernel, steps), grid=(steps + b...  71.8 us
    ppermute x12, starting transfers between devices, step(): self.up = lax.ppermute(up, 'dp', [(i, i + 1) for i in ends])  69.3 us
    ppermute x12, waiting for transfers between devices, step(): lax.ppermute(down, 'dp', [(last - i, last - i - 1) for i in ends])  59.8 us
    ppermute x12, waiting for transfers between devices, step(): self.up = lax.ppermute(up, 'dp', [(i, i + 1) for i in ends])  59.2 us
    psum x1, blocking collectives, body(): mid_total = lax.psum(mid_sums, ('dp', 'rows'))  57.6 us
    convert_element_type x18, other arithmetic, add(): functools.reduce(lambda u, v: u + v, (t.astype(F32) for t in terms))  46.3 us
  transfers between devices with their start and end apart: 80, of which 27 were waited for; matrix products, arithmetic and copies ran while one was open for 15% of the time, Pallas kernels for 28%

profile of v1, /device:TPU:0, one launch (start us, length us, event | category | flops | bytes accessed | tf_op | source)
XLA Modules:
  0.0 1196.6 jit_solution(18328823059577021656)
XLA Ops:
  7.3 4.9 constant_dynamic-slice_fusion.13
  13.4 5.6 shard_map.288
  24.2 8.2 shard_map.289
  48.3 16.6 %shard_map.290 = (bf16[1024,256]{1,0:T(8,128)(2,1)S(1)}, bf16[1024,256]{1,0:T(8,128)(2,1)}, f32[2,2048]{1,0:T(2,128)S(1)}) custom-call(s32[5,4]{1,0:T(8,128)S(1)} %stack.4.info, bf16[1024,512]{1,0:T(8,128)(2,1)S(1)} %copy-done.18, bf16[1024,512]{1,0:T(8,128)(2,1)} %collective-permute-done.qb_ref, bf16[4096,256]{1,0:T(8,128)(2,1)S(1)} %copy-done.1, ...), custom_call_target="tpu_custom_call" | custom-call | flops 8589934592 | bytes 2097152 | tf_op jit(solution)/shard_map/pallas_call | solution.py:41
  68.2 11.0 collective-permute-start.9
  81.4 7.8 collective-permute-done.5.rest_0_.rest_2_
  93.5 16.1 %shard_map.291 = (bf16[1024,256]{1,0:T(8,128)(2,1)S(1)}, bf16[1024,256]{1,0:T(8,128)(2,1)S(1)}, f32[2,2048]{1,0:T(2,128)S(1)}) custom-call(s32[5,4]{1,0:T(8,128)S(1)} %stack.4.info, bf16[1024,512]{1,0:T(8,128)(2,1)S(1)} %copy-done.19, bf16[1024,512]{1,0:T(8,128)(2,1)} %collective-permute-done.qb_ref, bf16[4096,256]{1,0:T(8,128)(2,1)S(1)} %copy-done.2, ...), custom_call_target="tpu_custom_call" | custom-call | flops 8589934592 | bytes 2097152 | tf_op jit(solution)/shard_map/pallas_call | solution.py:41
  114.6 64.1 %collective-permute-done.9.rest_1_.rest_3_ = bf16[2048,512]{1,0:T(8,128)(2,1)} collective-permute-done((bf16[2048,512]{1,0:T(8,128)(2,1)}, bf16[2048,512]{1,0:T(8,128)(2,1)}, u32[]{:S(2)}, u32[]{:S(2)}) %collective-permute-start.9) | collective-permute-done | bytes 2097184 | tf_op jit(solution)/shard_map/ppermute | solution.py:527
  180.7 12.1 %shard_map.292 = (f32[512,2048]{1,0:T(8,128)}, bf16[512,2048]{1,0:T(8,128)(2,1)}) custom-call(bf16[1024,512]{1,0:T(8,128)(2,1)} %pad_maximum_fusion.3.refs_0_, bf16[1024,512]{1,0:T(8,128)(2,1)} %copy-done.41, bf16[1024,512]{1,0:T(8,128)(2,1)} %copy-done.34, bf16[1024,512]{1,0:T(8,128)(2,1)} %copy-done.40, ...), custom_call_target="tpu_custom_call" | custom-call | flops 4294967296 | bytes 20971520 | tf_op jit(solution)/shard_map/pallas_call | solution.py:41
  198.5 15.9 %shard_map.294 = (bf16[512,1024]{1,0:T(8,128)(2,1)}, bf16[512,1024]{1,0:T(8,128)(2,1)}, bf16[512,1024]{1,0:T(8,128)(2,1)}, bf16[512,1024]{1,0:T(8,128)(2,1)}, f32[8,1024]{1,0:T(8,128)}) custom-call(bf16[512,2048]{1,0:T(8,128)(2,1)} %get-tuple-element.156.xa_ref.refs_0_, bf16[512,2048]{1,0:T(8,128)(2,1)} %copy-done.49, bf16[1024,2048]{1,0:T(8,128)(2,1)} %refs_5_.7, ...), custom_call_target="tpu_custom_call" | custom-call | flops 8589934592 | bytes 25165824 | tf_op jit(solution)/shard_map/pallas_call | solution.py:41
  214.4 8.3 all-gather.6.cloned.1.call-done
  222.6 4.8 constant_dynamic-slice_fusion.11.rest_4_.refs_9_
  228.0 18.0 %shard_map.295 = (bf16[256,2048]{1,0:T(8,128)(2,1)}, bf16[256,2048]{1,0:T(8,128)(2,1)}, bf16[512,1024]{1,0:T(8,128)(2,1)}, bf16[512,1024]{1,0:T(8,128)(2,1)}, bf...) custom-call(bf16[512,2048]{1,0:T(8,128)(2,1)} %get-tuple-element.156.xa_ref.refs_0_, ...), custom_call_target="tpu_custom_call" | custom-call | flops 8589934592 | bytes 29360128 | tf_op jit(solution)/shard_map/pallas_call | solution.py:411
  246.2 12.2 %shard_map.293 = (f32[512,2048]{1,0:T(8,128)}, bf16[512,2048]{1,0:T(8,128)(2,1)}) custom-call(bf16[1024,512]{1,0:T(8,128)(2,1)} %pad_maximum_fusion.3.refs_0_, bf16[1024,512]{1,0:T(8,128)(2,1)} %copy-done.41, bf16[1024,512]{1,0:T(8,128)(2,1)} %copy-done.34, bf16[1024,512]{1,0:T(8,128)(2,1)} %copy-done.40, ...), custom_call_target="tpu_custom_call" | custom-call | flops 4294967296 | bytes 20971520 | tf_op jit(solution)/shard_map/pallas_call | solution.py:41
  259.3 17.8 %shard_map.296 = (bf16[256,2048]{1,0:T(8,128)(2,1)}, bf16[256,2048]{1,0:T(8,128)(2,1)}, bf16[512,1024]{1,0:T(8,128)(2,1)}, bf16[512,1024]{1,0:T(8,128)(2,1)}, bf...) custom-call(bf16[512,2048]{1,0:T(8,128)(2,1)} %get-tuple-element.156, ...), custom_call_target="tpu_custom_call", output_to_operand_aliasing={{2}: (13, {}), {3}: (14, {}), {4}: (15, {}), {5}: (16, {})} | custom-call | flops 8589934592 | bytes 29360128 | tf_op jit(solution)/shard_map/pallas_call | solution.py:411
  277.4 15.9 %shard_map.297 = (bf16[512,1024]{1,0:T(8,128)(2,1)}, bf16[512,1024]{1,0:T(8,128)(2,1)}, bf16[512,1024]{1,0:T(8,128)(2,1)}, bf16[512,1024]{1,0:T(8,128)(2,1)}, f32[8,1024]{1,0:T(8,128)}) custom-call(bf16[512,2048]{1,0:T(8,128)(2,1)} %get-tuple-element.158.xa_ref.refs_1_, bf16[512,2048]{1,0:T(8,128)(2,1)} %collective-permute-done.14.xb_ref.refs_3_, ...), custom_call_target="tpu_custom_call" | custom-call | flops 8589934592 | bytes 25165824 | tf_op jit(solution)/shard_map/pallas_call | solution.py:41
  297.9 17.8 %shard_map.298 = (bf16[256,2048]{1,0:T(8,128)(2,1)}, bf16[256,2048]{1,0:T(8,128)(2,1)}, bf16[512,1024]{1,0:T(8,128)(2,1)}, bf16[512,1024]{1,0:T(8,128)(2,1)}, bf...) custom-call(bf16[512,2048]{1,0:T(8,128)(2,1)} %get-tuple-element.158.xa_ref.refs_1_, ...), custom_call_target="tpu_custom_call" | custom-call | flops 8589934592 | bytes 29360128 | tf_op jit(solution)/shard_map/pallas_call | solution.py:411
  315.9 14.8 %shard_map.299 = bf16[1024,2048]{1,0:T(8,128)(2,1)} custom-call(bf16[512,1024]{1,0:T(8,128)(2,1)} %get-tuple-element.225.refs_0_, bf16[512,1024]{1,0:T(8,128)(2,1)} %get-tuple-element.181.refs_1_, bf16[512,1024]{1,0:T(8,128)(2,1)} %get-tuple-element.182.refs_2_, bf16[512,1024]{1,0:T(8,128)(2,1)} %get-tuple-element.183.refs_3_, bf16[1024,2048]{1,0:T(8,128)(2,1)} %refs_5_.7, ...), custom_call_target="tpu_custom_call" | custom-call | flops 17179869184 | bytes 16777216 | tf_op jit(solution)/shard_map/pallas_call | solution.py:41
  331.5 18.1 %shard_map.300 = (bf16[256,2048]{1,0:T(8,128)(2,1)}, bf16[256,2048]{1,0:T(8,128)(2,1)}, bf16[512,1024]{1,0:T(8,128)(2,1)}, bf16[512,1024]{1,0:T(8,128)(2,1)}, bf...) custom-call(bf16[512,2048]{1,0:T(8,128)(2,1)} %get-tuple-element.158, ...), custom_call_target="tpu_custom_call", output_to_operand_aliasing={{2}: (13, {}), {3}: (14, {}), {4}: (15, {}), {5}: (16, {})} | custom-call | flops 8589934592 | bytes 29360128 | tf_op jit(solution)/shard_map/pallas_call | solution.py:411
  349.6 6.6 collective-permute-done.19.refs_3_
  356.5 14.8 %shard_map.303 = bf16[1024,2048]{1,0:T(8,128)(2,1)} custom-call(bf16[512,1024]{1,0:T(8,128)(2,1)} %get-tuple-element.199.refs_0_.refs_4_, bf16[512,1024]{1,0:T(8,128)(2,1)} %get-tuple-element.200.refs_1_.refs_5_, bf16[512,1024]{1,0:T(8,128)(2,1)} %get-tuple-element.201.refs_2_.refs_6_, bf16[512,1024]{1,0:T(8,128)(2,1)} %get-tuple-element.202.refs_3_.refs_7_, ...), custom_call_target="tpu_custom_call" | custom-call | flops 17179869184 | bytes 16777216 | tf_op jit(solution)/shard_map/pallas_call | solution.py:41
  373.1 13.6 %shard_map.301 = bf16[2048,1024]{1,0:T(8,128)(2,1)} custom-call(bf16[512,2048]{1,0:T(8,128)(2,1)} %get-tuple-element.156.xa_ref.refs_0_, bf16[512,2048]{1,0:T(8,128)(2,1)} %get-tuple-element.158.xa_ref.refs_1_, bf16[512,2048]{1,0:T(8,128)(2,1)} %copy-done.49, bf16[512,2048]{1,0:T(8,128)(2,1)} %collective-permute-done.14.xb_ref.refs_3_, ...), custom_call_target="tpu_custom_call" | custom-call | flops 17179869184 | bytes 16777216 | tf_op jit(solution)/shard_map/pallas_call | solution.py:41
  388.7 13.7 %shard_map.302 = bf16[2048,1024]{1,0:T(8,128)(2,1)} custom-call(bf16[512,2048]{1,0:T(8,128)(2,1)} %get-tuple-element.156.xa_ref.refs_0_, bf16[512,2048]{1,0:T(8,128)(2,1)} %get-tuple-element.158.xa_ref.refs_1_, bf16[512,2048]{1,0:T(8,128)(2,1)} %copy-done.49, bf16[512,2048]{1,0:T(8,128)(2,1)} %collective-permute-done.14.xb_ref.refs_3_, ...), custom_call_target="tpu_custom_call" | custom-call | flops 17179869184 | bytes 16777216 | tf_op jit(solution)/shard_map/pallas_call | solution.py:41
  402.5 12.9 %shard_map.304 = (f32[512,2048]{1,0:T(8,128)}, bf16[512,2048]{1,0:T(8,128)(2,1)}, bf16[512,512]{1,0:T(8,128)(2,1)}, bf16[512,512]{1,0:T(8,128)(2,1)}, f32[8,2048]{1,0:T(8,128)}) custom-call(bf16[256,2048]{1,0:T(8,128)(2,1)} %copy-done.44, bf16[256,2048]{1,0:T(8,128)(2,1)} %copy-done.45, bf16[256,2048]{1,0:T(8,128)(2,1)} %copy-done.58, ...), custom_call_target="tpu_custom_call" | custom-call | flops 2147483648 | bytes 20971520 | tf_op jit(solution)/shard_map/pallas_call | solution.py:41
  419.7 12.7 %shard_map.305 = (f32[512,2048]{1,0:T(8,128)}, bf16[512,2048]{1,0:T(8,128)(2,1)}, bf16[512,512]{1,0:T(8,128)(2,1)}, bf16[512,512]{1,0:T(8,128)(2,1)}, f32[8,2048]{1,0:T(8,128)}) custom-call(bf16[256,2048]{1,0:T(8,128)(2,1)} %copy-done.46, bf16[256,2048]{1,0:T(8,128)(2,1)} %copy-done.47, bf16[256,2048]{1,0:T(8,128)(2,1)} %copy-done.60, ...), custom_call_target="tpu_custom_call" | custom-call | flops 2147483648 | bytes 20971520 | tf_op jit(solution)/shard_map/pallas_call | solution.py:41
  435.6 6.3 convolution_convert_fusion.2
  444.0 6.0 convolution_convert_fusion.3
  451.1 12.8 %collective-permute-done.21 = bf16[1024,2048]{1,0:T(8,128)(2,1)} collective-permute-done((bf16[1024,2048]{1,0:T(8,128)(2,1)}, bf16[1024,2048]{1,0:T(8,128)(2,1)}, u32[]{:S(2)}, u32[]{:S(2)}) %collective-permute-start.21) | collective-permute-done | bytes 4194336 | tf_op jit(solution)/shard_map/ppermute | solution.py:527
  465.3 6.1 add_convert_fusion.2
  476.9 26.2 %shard_map.306 = (bf16[1024,256]{1,0:T(8,128)(2,1)S(1)}, bf16[1024,256]{1,0:T(8,128)(2,1)S(1)}, f32[4096,256]{1,0:T(8,128)}) custom-call(s32[5,8]{1,0:T(8,128)S(1)} %stack.5.info, bf16[1024,512]{1,0:T(8,128)(2,1)S(1)} %copy-done.20, bf16[1024,512]{1,0:T(8,128)(2,1)} %collective-permute-done.qb_ref, ...), custom_call_target="tpu_custom_call" | custom-call | flops 21474836480 | bytes 4194304 | tf_op jit(solution)/shard_map/pallas_call | solution.py:41
  506.1 71.8 %collective-permute-done.42 = bf16[256,2048]{1,0:T(8,128)(2,1)} collective-permute-done((bf16[256,2048]{1,0:T(8,128)(2,1)}, bf16[256,2048]{1,0:T(8,128)(2,1)}, u32[]{:S(2)}, u32[]{:S(2)}) %collective-permute-start.42) | collective-permute-done | bytes 1048608 | tf_op jit(solution)/shard_map/ppermute | solution.py:527
  584.3 26.5 %shard_map.307 = (bf16[1024,256]{1,0:T(8,128)(2,1)S(1)}, bf16[1024,256]{1,0:T(8,128)(2,1)S(1)}, f32[4096,256]{1,0:T(8,128)}) custom-call(s32[5,8]{1,0:T(8,128)S(1)} %stack.5.info, bf16[1024,512]{1,0:T(8,128)(2,1)S(1)} %copy-done.21, bf16[1024,512]{1,0:T(8,128)(2,1)} %collective-permute-done.qb_ref, ...), custom_call_target="tpu_custom_call" | custom-call | flops 21474836480 | bytes 4194304 | tf_op jit(solution)/shard_map/pallas_call | solution.py:41
  627.8 11.7 collective-permute-start.35
  639.5 12.5 %collective-permute-done.35 = bf16[1024,256]{1,0:T(8,128)(2,1)S(1)} collective-permute-done((bf16[1024,256]{1,0:T(8,128)(2,1)S(1)}, bf16[1024,256]{1,0:T(8,128)(2,1)S(1)}, u32[]{:S(2)}, u32[]{:S(2)}) %collective-permute-start.35) | collective-permute-done | bytes 524320 | tf_op jit(solution)/shard_map/ppermute | solution.py:527
  654.8 4.6 collective-permute-start.43
  673.9 19.6 %collective-permute-done.43 = bf16[640,1024]{1,0:T(8,128)(2,1)} collective-permute-done((bf16[640,1024]{1,0:T(8,128)(2,1)}, bf16[640,1024]{1,0:T(8,128)(2,1)}, u32[]{:S(2)}, u32[]{:S(2)}) %collective-permute-start.43) | collective-permute-done | bytes 1310752 | tf_op jit(solution)/shard_map/ppermute | solution.py:584
  693.5 4.8 add_convert_fusion.7
  698.3 32.6 %collective-permute-start.44 = (bf16[640,1024]{1,0:T(8,128)(2,1)S(1)}, bf16[640,1024]{1,0:T(8,128)(2,1)}, u32[]{:S(2)}, u32[]{:S(2)}) collective-permute-start(bf16[640,1024]{1,0:T(8,128)(2,1)S(1)} %get-tuple-element.367), channel_id=1, source_target_pairs={{0,8},{8,16},{1,9},{9,17},{2,10},{10,18},{3,11},{11,19},{4,12},{12... | collective-permute-start | bytes 3932168 | tf_op jit(solution)/shard_map/ppermute | solution.py:584
  733.5 5.2 convolution_convert_fusion.1
  738.6 19.4 %collective-permute-done.44 = bf16[640,1024]{1,0:T(8,128)(2,1)} collective-permute-done((bf16[640,1024]{1,0:T(8,128)(2,1)S(1)}, bf16[640,1024]{1,0:T(8,128)(2,1)}, u32[]{:S(2)}, u32[]{:S(2)}) %collective-permute-start.44) | collective-permute-done | bytes 1310752 | tf_op jit(solution)/shard_map/ppermute | solution.py:584
  760.2 6.1 collective-permute-start.45
  771.8 8.7 collective-permute-start.50
  781.8 10.4 collective-permute-done.45
  792.2 15.3 %collective-permute-done.50 = bf16[1024,640]{0,1:T(8,128)(2,1)} collective-permute-done((bf16[1024,640]{0,1:T(8,128)(2,1)}, bf16[1024,640]{0,1:T(8,128)(2,1)}, u32[]{:S(2)}, u32[]{:S(2)}) %collective-permute-start.50) | collective-permute-done | bytes 1310752 | tf_op jit(solution)/shard_map/ppermute | solution.py:527
  810.8 6.4 broadcast_in_dim.23
  817.2 4.5 constant_dynamic-update-slice_fusion.16
  824.9 23.1 %shard_map.308 = (bf16[1024,2048]{1,0:T(8,128)(2,1)}, bf16[1024,2048]{1,0:T(8,128)(2,1)}) custom-call(bf16[512,1024]{1,0:T(8,128)(2,1)} %get-tuple-element.225.refs_0_, bf16[512,1024]{1,0:T(8,128)(2,1)} %get-tuple-element.181.refs_1_, bf16[512,1024]{1,0:T(8,128)(2,1)} %get-tuple-element.182.refs_2_, bf16[512,1024]{1,0:T(8,128)(2,1)} %get-tuple-element.183.refs_3_, ...), custom_call_target="tpu_custom_call" | custom-call | flops 17179869184 | bytes 33554432 | tf_op jit(solution)/shard_map/pallas_call | solution.py:41
  856.0 5.6 collective-permute-done.53
  865.0 8.0 pad_maximum_fusion.refs_11_
  873.8 20.9 %collective-permute-done.52 = bf16[640,1024]{1,0:T(8,128)(2,1)} collective-permute-done((bf16[640,1024]{1,0:T(8,128)(2,1)}, bf16[640,1024]{1,0:T(8,128)(2,1)}, u32[]{:S(2)}, u32[]{:S(2)}) %collective-permute-start.52) | collective-permute-done | bytes 1310752 | tf_op jit(solution)/shard_map/ppermute | solution.py:585
  897.8 12.5 %collective-permute-done.32.refs_3_ = bf16[1024,512]{1,0:T(8,128)(2,1)S(1)} collective-permute-done((bf16[1024,512]{1,0:T(8,128)(2,1)S(1)}, bf16[1024,512]{1,0:T(8,128)(2,1)S(1)}, u32[]{:S(2)}, u32[]{:S(2)}) %collective-permute-start.32) | collective-permute-done | bytes 1048608 | tf_op jit(solution)/shard_map/ppermute | solution.py:530
  911.3 25.4 %shard_map.309 = (bf16[1024,2048]{1,0:T(8,128)(2,1)}, f32[8,2048]{1,0:T(8,128)}) custom-call(bf16[1024,512]{1,0:T(8,128)(2,1)} %pad_maximum_fusion.5.refs_0_, bf16[1024,512]{1,0:T(8,128)(2,1)} %copy-done.70, bf16[1024,512]{1,0:T(8,128)(2,1)} %copy-done.66, bf16[1024,512]{1,0:T(8,128)(2,1)} %copy-done.71, bf16[2048,512]{1,0:T(8,128)(2,1)} %get-tuple-element.371.refs_4_, ...), custom_call_target="tpu_custom_call" | custom-call | flops 9663676416 | bytes 41943040 | tf_op jit(solution)/shard_map/pallas_call | solution.py:41
  938.0 5.0 collective-permute-start.57
  950.4 8.1 collective-permute-start.59
  958.5 7.8 add_convert_fusion.1
  983.8 25.0 %collective-permute-done.62 = bf16[256,640]{0,1:T(8,128)(2,1)S(1)} collective-permute-done((bf16[256,640]{0,1:T(8,128)(2,1)S(1)}, bf16[256,640]{0,1:T(8,128)(2,1)S(1)}, u32[]{:S(2)}, u32[]{:S(2)}) %collective-permute-start.62) | collective-permute-done | bytes 327712 | tf_op jit(solution)/shard_map/ppermute | solution.py:585
  1013.4 5.3 collective-permute-done.64
  1020.1 7.5 collective-permute-done.66
  1042.0 33.3 %collective-permute-done.73 = f32[1024]{0:T(1024)S(1)} collective-permute-done((f32[1024]{0:T(1024)S(1)}, f32[1024]{0:T(1024)S(1)}, u32[]{:S(2)}, u32[]{:S(2)}) %collective-permute-start.73) | collective-permute-done | bytes 4128 | tf_op jit(solution)/shard_map/ppermute | solution.py:527
  1086.8 57.6 %psum.15 = f32[4,2048]{1,0:T(4,128)S(1)} all-reduce(f32[4,2048]{1,0:T(4,128)S(1)} %slice_add_fusion), channel_id=1, replica_groups=mesh['dp'=4,'heads'=2,'rows'=4] {'dp','rows'}, use_global_device_ids=true, to_apply=%region_8.9 | all-reduce | flops 8192 | bytes 65536 | tf_op jit(solution)/shard_map/psum | solution.py:1062
  1151.2 5.3 convert_element_type.371
  1157.7 6.5 fusion.1
  1164.6 4.7 bitcast_convert_fusion
  1178.6 9.2 copy.116
  (414 shorter events, 228.7 us)
Async XLA Ops:
  7.2 82.0 %all-gather.4.cloned.1.call-start = ((), (), s32[]{:S(2)}) async-start(), calls=%async_computation | async-start | bytes 6291456 | tf_op jit(solution)/shard_map/all_gather | solution.py:640
  12.2 210.5 %all-gather.6.cloned.1.call-start = ((), (), s32[]{:S(2)}) async-start(), calls=%async_computation.1 | async-start | bytes 12582912 | tf_op jit(solution)/shard_map/all_gather | solution.py:670
  21.2 14.9 %collective-permute-start.2 = (bf16[1024,256]{0,1:T(8,128)(2,1)S(1)}, bf16[1024,256]{0,1:T(8,128)(2,1)S(1)}, u32[]{:S(2)}, u32[]{:S(2)}) collective-permute-start(bf16[1024,256]{0,1:T(8,128)(2,1)S(1)} %copy.106), channel_id=1, source_target_pairs={{0,2},{1,3},{2,0},{3,1},{4,6},{5,7},{6,4},{7,5},{8,10},{9,11},{10,... | collective-permute-start | bytes 1572872 | tf_op jit(solution)/shard_map/ppermute | solution.py:527
  24.2 17.0 %collective-permute-start.1 = (bf16[1024,256]{0,1:T(8,128)(2,1)S(1)}, bf16[1024,256]{0,1:T(8,128)(2,1)S(1)}, u32[]{:S(2)}, u32[]{:S(2)}) collective-permute-start(bf16[1024,256]{0,1:T(8,128)(2,1)S(1)} %copy.106), channel_id=1, source_target_pairs={{0,1},{1,0},{2,3},{3,2},{4,5},{5,4},{6,7},{7,6},{8,9},{9,8},{10,11... | collective-permute-start | bytes 1572872 | tf_op jit(solution)/shard_map/ppermute | solution.py:524
  33.4 12.1 %collective-permute-start = (bf16[1024,512]{1,0:T(8,128)(2,1)}, bf16[1024,512]{1,0:T(8,128)(2,1)}, u32[]{:S(2)}, u32[]{:S(2)}) collective-permute-start(bf16[1024,512]{1,0:T(8,128)(2,1)} %get-tuple-element.141), channel_id=1, source_target_pairs={{0,1},{1,0},{2,3},{3,2},{4,5},{5,4},{6,7},{7,6},{8,9},{9,8},{10,11... | collective-permute-start | bytes 3145736 | tf_op jit(solution)/shard_map/ppermute | solution.py:524
  39.2 50.0 %collective-permute-start.5 = (bf16[2048,512]{1,0:T(8,128)(2,1)}, bf16[2048,512]{1,0:T(8,128)(2,1)}, u32[]{:S(2)}, u32[]{:S(2)}) collective-permute-start(bf16[2048,512]{1,0:T(8,128)(2,1)} %slice.108), channel_id=1, source_target_pairs={{0,2},{1,3},{2,0},{3,1},{4,6},{5,7},{6,4},{7,5},{8,10},{9,11},{10,... | collective-permute-start | bytes 6291464 | tf_op jit(solution)/shard_map/ppermute | solution.py:527
  41.0 740.8 %all-reduce.3.cloned.1.call-start = ((), (), s32[]{:S(2)}) async-start(), calls=%async_computation.3 | async-start | bytes 8388608 | tf_op jit(solution)/shard_map/psum | solution.py:970
  64.9 14.3 %collective-permute-start.4 = (bf16[1024,256]{1,0:T(8,128)(2,1)}, bf16[1024,256]{1,0:T(8,128)(2,1)}, u32[]{:S(2)}, u32[]{:S(2)}) collective-permute-start(bf16[1024,256]{1,0:T(8,128)(2,1)} %get-tuple-element.145.ob_ref), channel_id=1, source_target_pairs={{0,1},{1,0},{2,3},{3,2},{4,5},{5,4},{6,7},{7,6},{8,9},{9,8},{10,11... | collective-permute-start | bytes 1572872 | tf_op jit(solution)/shard_map/ppermute | solution.py:524
  68.2 110.5 %collective-permute-start.9 = (bf16[2048,512]{1,0:T(8,128)(2,1)}, bf16[2048,512]{1,0:T(8,128)(2,1)}, u32[]{:S(2)}, u32[]{:S(2)}) collective-permute-start(bf16[2048,512]{1,0:T(8,128)(2,1)} %slice.109), channel_id=1, source_target_pairs={{0,2},{1,3},{2,0},{3,1},{4,6},{5,7},{6,4},{7,5},{8,10},{9,11},{10,... | collective-permute-start | bytes 6291464 | tf_op jit(solution)/shard_map/ppermute | solution.py:527
  91.4 87.3 %collective-permute-start.10 = (bf16[512,2048]{1,0:T(8,128)(2,1)S(1)}, bf16[512,2048]{1,0:T(8,128)(2,1)S(1)}, u32[]{:S(2)}, u32[]{:S(2)}) collective-permute-start(bf16[512,2048]{1,0:T(8,128)(2,1)S(1)} %constant_dynamic-slice_fusion.12.refs_6_), channel_id=1, source_target_pairs={{0,1},{1,0},{2,3},{3,2},{4,5},{5,4},{6,7},{7,6},{8,9},{9,8},{10,11... | collective-permute-start | bytes 6291464 | tf_op jit(solution)/shard_map/ppermute | solution.py:524
  109.7 85.6 %collective-permute-start.12 = (bf16[1024,2048]{1,0:T(8,128)(2,1)}, bf16[1024,2048]{1,0:T(8,128)(2,1)}, u32[]{:S(2)}, u32[]{:S(2)}) collective-permute-start(bf16[1024,2048]{1,0:T(8,128)(2,1)} %refs_5_.7), channel_id=1, source_target_pairs={{0,1},{1,0},{2,3},{3,2},{4,5},{5,4},{6,7},{7,6},{8,9},{9,8},{10,11... | collective-permute-start | bytes 12582920 | tf_op jit(solution)/shard_map/ppermute | solution.py:524
  112.5 66.2 %collective-permute-start.8 = (bf16[1024,512]{1,0:T(8,128)(2,1)S(1)}, bf16[1024,512]{1,0:T(8,128)(2,1)S(1)}, u32[]{:S(2)}, u32[]{:S(2)}) collective-permute-start(bf16[1024,512]{1,0:T(8,128)(2,1)S(1)} %constant_dynamic-update-slice_fusion.refs_2_), channel_id=1, source_target_pairs={{0,4},{4,0},{1,5},{5,1},{2,6},{6,2},{3,7},{7,3},{8,12},{12,8},{9,1... | collective-permute-start | bytes 3145736 | tf_op jit(solution)/shard_map/ppermute | solution.py:530
  114.0 64.7 %collective-permute-start.6 = (bf16[1024,512]{1,0:T(8,128)(2,1)S(1)}, bf16[1024,512]{1,0:T(8,128)(2,1)S(1)}, u32[]{:S(2)}, u32[]{:S(2)}) collective-permute-start(bf16[1024,512]{1,0:T(8,128)(2,1)S(1)} %copy-done.30), channel_id=1, source_target_pairs={{0,4},{4,0},{1,5},{5,1},{2,6},{6,2},{3,7},{7,3},{8,12},{12,8},{9,1... | collective-permute-start | bytes 3145736 | tf_op jit(solution)/shard_map/ppermute | solution.py:530
  192.8 34.7 %collective-permute-start.13 = (f32[1024]{0:T(1024)S(1)}, f32[1024]{0:T(1024)S(1)}, u32[]{:S(2)}, u32[]{:S(2)}) collective-permute-start(f32[1024]{0:T(1024)S(1)} %copy-done.73), channel_id=1, source_target_pairs={{0,2},{1,3},{2,0},{3,1},{4,6},{5,7},{6,4},{7,5},{8,10},{9,11},{10,... | collective-permute-start | bytes 12296 | tf_op jit(solution)/shard_map/ppermute | solution.py:527
  246.1 12.8 %collective-permute-start.15 = (bf16[256,2048]{1,0:T(8,128)(2,1)}, bf16[256,2048]{1,0:T(8,128)(2,1)S(1)}, u32[]{:S(2)}, u32[]{:S(2)}) collective-permute-start(bf16[256,2048]{1,0:T(8,128)(2,1)} %get-tuple-element.165), channel_id=1, source_target_pairs={{0,1},{1,0},{2,3},{3,2},{4,5},{5,4},{6,7},{7,6},{8,9},{9,8},{10,11... | collective-permute-start | bytes 3145736 | tf_op jit(solution)/shard_map/ppermute | solution.py:524
  258.4 19.0 %collective-permute-start.14 = (bf16[512,2048]{1,0:T(8,128)(2,1)}, bf16[512,2048]{1,0:T(8,128)(2,1)}, u32[]{:S(2)}, u32[]{:S(2)}) collective-permute-start(bf16[512,2048]{1,0:T(8,128)(2,1)} %get-tuple-element.158.xa_ref.refs_1_), channel_id=1, source_target_pairs={{0,1},{1,0},{2,3},{3,2},{4,5},{5,4},{6,7},{7,6},{8,9},{9,8},{10,11... | collective-permute-start | bytes 6291464 | tf_op jit(solution)/shard_map/ppermute | solution.py:524
  277.1 18.2 %collective-permute-start.16 = (bf16[256,2048]{1,0:T(8,128)(2,1)}, bf16[256,2048]{1,0:T(8,128)(2,1)S(1)}, u32[]{:S(2)}, u32[]{:S(2)}) collective-permute-start(bf16[256,2048]{1,0:T(8,128)(2,1)} %get-tuple-element.172), channel_id=1, source_target_pairs={{0,1},{1,0},{2,3},{3,2},{4,5},{5,4},{6,7},{7,6},{8,9},{9,8},{10,11... | collective-permute-start | bytes 3145736 | tf_op jit(solution)/shard_map/ppermute | solution.py:524
  293.4 38.1 %collective-permute-start.18 = (bf16[256,2048]{1,0:T(8,128)(2,1)S(1)}, bf16[256,2048]{1,0:T(8,128)(2,1)S(1)}, u32[]{:S(2)}, u32[]{:S(2)}) collective-permute-start(bf16[256,2048]{1,0:T(8,128)(2,1)S(1)} %add_convert_fusion.15.refs_0_), channel_id=1, source_target_pairs={{0,4},{4,0},{1,5},{5,1},{2,6},{6,2},{3,7},{7,3},{8,12},{12,8},{9,1... | collective-permute-start | bytes 3145736 | tf_op jit(solution)/shard_map/ppermute | solution.py:530
  315.7 15.4 %collective-permute-start.17 = (bf16[256,2048]{1,0:T(8,128)(2,1)}, bf16[256,2048]{1,0:T(8,128)(2,1)S(1)}, u32[]{:S(2)}, u32[]{:S(2)}) collective-permute-start(bf16[256,2048]{1,0:T(8,128)(2,1)} %get-tuple-element.177), channel_id=1, source_target_pairs={{0,1},{1,0},{2,3},{3,2},{4,5},{5,4},{6,7},{7,6},{8,9},{9,8},{10,11... | collective-permute-start | bytes 3145736 | tf_op jit(solution)/shard_map/ppermute | solution.py:524
  330.7 25.6 %collective-permute-start.19 = (bf16[256,2048]{1,0:T(8,128)(2,1)S(1)}, bf16[256,2048]{1,0:T(8,128)(2,1)S(1)}, u32[]{:S(2)}, u32[]{:S(2)}) collective-permute-start(bf16[256,2048]{1,0:T(8,128)(2,1)S(1)} %add_convert_fusion.14.refs_1_), channel_id=1, source_target_pairs={{0,4},{4,0},{1,5},{5,1},{2,6},{6,2},{3,7},{7,3},{8,12},{12,8},{9,1... | collective-permute-start | bytes 3145736 | tf_op jit(solution)/shard_map/ppermute | solution.py:530
  356.3 30.4 %collective-permute-start.20 = (bf16[256,2048]{1,0:T(8,128)(2,1)S(1)}, bf16[256,2048]{1,0:T(8,128)(2,1)S(1)}, u32[]{:S(2)}, u32[]{:S(2)}) collective-permute-start(bf16[256,2048]{1,0:T(8,128)(2,1)S(1)} %add_convert_fusion.13.refs_0_), channel_id=1, source_target_pairs={{0,4},{4,0},{1,5},{5,1},{2,6},{6,2},{3,7},{7,3},{8,12},{12,8},{9,1... | collective-permute-start | bytes 3145736 | tf_op jit(solution)/shard_map/ppermute | solution.py:530
  371.3 92.5 %collective-permute-start.21 = (bf16[1024,2048]{1,0:T(8,128)(2,1)}, bf16[1024,2048]{1,0:T(8,128)(2,1)}, u32[]{:S(2)}, u32[]{:S(2)}) collective-permute-start(bf16[1024,2048]{1,0:T(8,128)(2,1)} %shard_map.303), channel_id=1, source_target_pairs={{0,2},{1,3},{2,0},{3,1},{4,6},{5,7},{6,4},{7,5},{8,10},{9,11},{10,... | collective-permute-start | bytes 12582920 | tf_op jit(solution)/shard_map/ppermute | solution.py:527
  373.1 13.6 %collective-permute-start.22 = (bf16[256,2048]{1,0:T(8,128)(2,1)S(1)}, bf16[256,2048]{1,0:T(8,128)(2,1)S(1)}, u32[]{:S(2)}, u32[]{:S(2)}) collective-permute-start(bf16[256,2048]{1,0:T(8,128)(2,1)S(1)} %copy-done.72), channel_id=1, source_target_pairs={{0,1},{1,0},{2,3},{3,2},{4,5},{5,4},{6,7},{7,6},{8,9},{9,8},{10,11... | collective-permute-start | bytes 3145736 | tf_op jit(solution)/shard_map/ppermute | solution.py:524
  387.1 31.6 %collective-permute-start.23 = (bf16[256,2048]{1,0:T(8,128)(2,1)S(1)}, bf16[256,2048]{1,0:T(8,128)(2,1)S(1)}, u32[]{:S(2)}, u32[]{:S(2)}) collective-permute-start(bf16[256,2048]{1,0:T(8,128)(2,1)S(1)} %add_convert_fusion.12.refs_1_), channel_id=1, source_target_pairs={{0,4},{4,0},{1,5},{5,1},{2,6},{6,2},{3,7},{7,3},{8,12},{12,8},{9,1... | collective-permute-start | bytes 3145736 | tf_op jit(solution)/shard_map/ppermute | solution.py:530
  415.3 27.2 %collective-permute-start.24 = (bf16[512,512]{1,0:T(8,128)(2,1)}, bf16[512,512]{1,0:T(8,128)(2,1)S(1)}, u32[]{:S(2)}, u32[]{:S(2)}) collective-permute-start(bf16[512,512]{1,0:T(8,128)(2,1)} %get-tuple-element.215), channel_id=1, source_target_pairs={{0,1},{1,0},{2,3},{3,2},{4,5},{5,4},{6,7},{7,6},{8,9},{9,8},{10,11... | collective-permute-start | bytes 1572872 | tf_op jit(solution)/shard_map/ppermute | solution.py:524
  442.0 29.5 %collective-permute-start.41 = (bf16[512,2048]{1,0:T(8,128)(2,1)}, bf16[512,2048]{1,0:T(8,128)(2,1)}, u32[]{:S(2)}, u32[]{:S(2)}) collective-permute-start(bf16[512,2048]{1,0:T(8,128)(2,1)} %convolution_convert_fusion.2), channel_id=1, source_target_pairs={{0,1},{1,0},{2,3},{3,2},{4,5},{5,4},{6,7},{7,6},{8,9},{9,8},{10,11... | collective-permute-start | bytes 6291464 | tf_op jit(solution)/shard_map/ppermute | solution.py:524
  463.9 119.2 %collective-permute-start.27 = (bf16[2048,1024]{1,0:T(8,128)(2,1)}, bf16[2048,1024]{1,0:T(8,128)(2,1)}, u32[]{:S(2)}, u32[]{:S(2)}) collective-permute-start(bf16[2048,1024]{1,0:T(8,128)(2,1)} %shard_map.301), channel_id=1, source_target_pairs={{0,2},{1,3},{2,0},{3,1},{4,6},{5,7},{6,4},{7,5},{8,10},{9,11},{10,... | collective-permute-start | bytes 12582920 | tf_op jit(solution)/shard_map/ppermute | solution.py:527
  476.4 101.6 %collective-permute-start.42 = (bf16[256,2048]{1,0:T(8,128)(2,1)}, bf16[256,2048]{1,0:T(8,128)(2,1)}, u32[]{:S(2)}, u32[]{:S(2)}) collective-permute-start(bf16[256,2048]{1,0:T(8,128)(2,1)} %constant_dynamic-slice_fusion.7), channel_id=1, source_target_pairs={{0,2},{1,3},{2,0},{3,1},{4,6},{5,7},{6,4},{7,5},{8,10},{9,11},{10,... | collective-permute-start | bytes 3145736 | tf_op jit(solution)/shard_map/ppermute | solution.py:527
  503.1 345.0 %all-gather.8.cloned.1.call-start = ((), (), s32[]{:S(2)}) async-start(), calls=%async_computation.2 | async-start | bytes 6291456 | tf_op jit(solution)/shard_map/all_gather | solution.py:640
  622.6 36.9 %collective-permute-start.46 = (bf16[640,1024]{1,0:T(8,128)(2,1)}, bf16[640,1024]{1,0:T(8,128)(2,1)}, u32[]{:S(2)}, u32[]{:S(2)}) collective-permute-start(bf16[640,1024]{1,0:T(8,128)(2,1)} %get-tuple-element.368), channel_id=1, source_target_pairs={{24,16},{25,17},{26,18},{27,19},{28,20},{29,21},{30,22},{31,23}} | collective-permute-start | bytes 3932168 | tf_op jit(solution)/shard_map/ppermute | solution.py:585
  627.8 24.2 %collective-permute-start.35 = (bf16[1024,256]{1,0:T(8,128)(2,1)S(1)}, bf16[1024,256]{1,0:T(8,128)(2,1)S(1)}, u32[]{:S(2)}, u32[]{:S(2)}) collective-permute-start(bf16[1024,256]{1,0:T(8,128)(2,1)S(1)} %fusion.21), channel_id=1, source_target_pairs={{0,2},{1,3},{2,0},{3,1},{4,6},{5,7},{6,4},{7,5},{8,10},{9,11},{10,... | collective-permute-start | bytes 1572872 | tf_op jit(solution)/shard_map/ppermute | solution.py:527
  653.4 13.9 %collective-permute-start.36 = (bf16[1024,256]{1,0:T(8,128)(2,1)S(1)}, bf16[1024,256]{1,0:T(8,128)(2,1)}, u32[]{:S(2)}, u32[]{:S(2)}) collective-permute-start(bf16[1024,256]{1,0:T(8,128)(2,1)S(1)} %fusion.20), channel_id=1, source_target_pairs={{0,4},{4,0},{1,5},{5,1},{2,6},{6,2},{3,7},{7,3},{8,12},{12,8},{9,1... | collective-permute-start | bytes 1572872 | tf_op jit(solution)/shard_map/ppermute | solution.py:530
  654.8 14.6 %collective-permute-start.31 = (bf16[1024,256]{1,0:T(8,128)(2,1)S(1)}, bf16[1024,256]{1,0:T(8,128)(2,1)S(1)}, u32[]{:S(2)}, u32[]{:S(2)}) collective-permute-start(bf16[1024,256]{1,0:T(8,128)(2,1)S(1)} %copy-done.15), channel_id=1, source_target_pairs={{0,1},{1,0},{2,3},{3,2},{4,5},{5,4},{6,7},{7,6},{8,9},{9,8},{10,11... | collective-permute-start | bytes 1572872 | tf_op jit(solution)/shard_map/ppermute | solution.py:524
  654.8 38.7 %collective-permute-start.43 = (bf16[640,1024]{1,0:T(8,128)(2,1)}, bf16[640,1024]{1,0:T(8,128)(2,1)}, u32[]{:S(2)}, u32[]{:S(2)}) collective-permute-start(bf16[640,1024]{1,0:T(8,128)(2,1)} %get-tuple-element.369), channel_id=1, source_target_pairs={{0,8},{1,9},{2,10},{3,11},{4,12},{5,13},{6,14},{7,15}} | collective-permute-start | bytes 3932168 | tf_op jit(solution)/shard_map/ppermute | solution.py:584
  662.8 30.7 %collective-permute-start.47 = (bf16[640,1024]{1,0:T(8,128)(2,1)}, bf16[640,1024]{1,0:T(8,128)(2,1)}, u32[]{:S(2)}, u32[]{:S(2)}) collective-permute-start(bf16[640,1024]{1,0:T(8,128)(2,1)} %add_convert_fusion.8), channel_id=1, source_target_pairs={{24,16},{16,8},{25,17},{17,9},{26,18},{18,10},{27,19},{19,11},{28,... | collective-permute-start | bytes 3932168 | tf_op jit(solution)/shard_map/ppermute | solution.py:585
  673.8 92.4 %collective-permute-start.49 = (bf16[2048,640]{0,1:T(8,128)(2,1)}, bf16[2048,640]{0,1:T(8,128)(2,1)}, u32[]{:S(2)}, u32[]{:S(2)}) collective-permute-start(bf16[2048,640]{0,1:T(8,128)(2,1)} %convolution_convert_fusion), channel_id=1, source_target_pairs={{0,1},{1,0},{2,3},{3,2},{4,5},{5,4},{6,7},{7,6},{8,9},{9,8},{10,11... | collective-permute-start | bytes 7864328 | tf_op jit(solution)/shard_map/ppermute | solution.py:524
  698.3 59.7 %collective-permute-start.44 = (bf16[640,1024]{1,0:T(8,128)(2,1)S(1)}, bf16[640,1024]{1,0:T(8,128)(2,1)}, u32[]{:S(2)}, u32[]{:S(2)}) collective-permute-start(bf16[640,1024]{1,0:T(8,128)(2,1)S(1)} %get-tuple-element.367), channel_id=1, source_target_pairs={{0,8},{8,16},{1,9},{9,17},{2,10},{10,18},{3,11},{11,19},{4,12},{12... | collective-permute-start | bytes 3932168 | tf_op jit(solution)/shard_map/ppermute | solution.py:584
  760.2 32.0 %collective-permute-start.45 = (bf16[640,1024]{1,0:T(8,128)(2,1)S(1)}, bf16[640,1024]{1,0:T(8,128)(2,1)}, u32[]{:S(2)}, u32[]{:S(2)}) collective-permute-start(bf16[640,1024]{1,0:T(8,128)(2,1)S(1)} %add_convert_fusion.9), channel_id=1, source_target_pairs={{0,8},{8,16},{16,24},{1,9},{9,17},{17,25},{2,10},{10,18},{18,26},{... | collective-permute-start | bytes 3932168 | tf_op jit(solution)/shard_map/ppermute | solution.py:584
  771.8 35.7 %collective-permute-start.50 = (bf16[1024,640]{0,1:T(8,128)(2,1)}, bf16[1024,640]{0,1:T(8,128)(2,1)}, u32[]{:S(2)}, u32[]{:S(2)}) collective-permute-start(bf16[1024,640]{0,1:T(8,128)(2,1)} %constant_dynamic-slice_fusion.2), channel_id=1, source_target_pairs={{0,2},{1,3},{2,0},{3,1},{4,6},{5,7},{6,4},{7,5},{8,10},{9,11},{10,... | collective-permute-start | bytes 3932168 | tf_op jit(solution)/shard_map/ppermute | solution.py:527
  780.4 30.4 %collective-permute-start.48 = (bf16[640,1024]{1,0:T(8,128)(2,1)}, bf16[640,1024]{1,0:T(8,128)(2,1)}, u32[]{:S(2)}, u32[]{:S(2)}) collective-permute-start(bf16[640,1024]{1,0:T(8,128)(2,1)} %get-tuple-element.366), channel_id=1, source_target_pairs={{24,16},{16,8},{8,0},{25,17},{17,9},{9,1},{26,18},{18,10},{10,2},{... | collective-permute-start | bytes 3932168 | tf_op jit(solution)/shard_map/ppermute | solution.py:585
  821.8 42.6 %collective-permute-start.51 = (bf16[640,1024]{1,0:T(8,128)(2,1)}, bf16[640,1024]{1,0:T(8,128)(2,1)}, u32[]{:S(2)}, u32[]{:S(2)}) collective-permute-start(bf16[640,1024]{1,0:T(8,128)(2,1)} %get-tuple-element.363), channel_id=1, source_target_pairs={{0,8},{8,16},{16,24},{1,9},{9,17},{17,25},{2,10},{10,18},{18,26},{... | collective-permute-start | bytes 3932168 | tf_op jit(solution)/shard_map/ppermute | solution.py:584
  848.0 110.4 %collective-permute-start.28 = (bf16[1024,2048]{1,0:T(8,128)(2,1)}, bf16[1024,2048]{1,0:T(8,128)(2,1)}, u32[]{:S(2)}, u32[]{:S(2)}) collective-permute-start(bf16[1024,2048]{1,0:T(8,128)(2,1)} %get-tuple-element.227), channel_id=1, source_target_pairs={{0,1},{1,0},{2,3},{3,2},{4,5},{5,4},{6,7},{7,6},{8,9},{9,8},{10,11... | collective-permute-start | bytes 12582920 | tf_op jit(solution)/shard_map/ppermute | solution.py:524
  851.1 45.3 %collective-permute-start.33 = (bf16[2048,512]{1,0:T(8,128)(2,1)}, bf16[2048,512]{1,0:T(8,128)(2,1)}, u32[]{:S(2)}, u32[]{:S(2)}) collective-permute-start(bf16[2048,512]{1,0:T(8,128)(2,1)} %constant_dynamic-slice_fusion.8.refs_6_), channel_id=1, source_target_pairs={{0,1},{1,0},{2,3},{3,2},{4,5},{5,4},{6,7},{7,6},{8,9},{9,8},{10,11... | collective-permute-start | bytes 6291464 | tf_op jit(solution)/shard_map/ppermute | solution.py:524
  861.5 33.1 %collective-permute-start.52 = (bf16[640,1024]{1,0:T(8,128)(2,1)}, bf16[640,1024]{1,0:T(8,128)(2,1)}, u32[]{:S(2)}, u32[]{:S(2)}) collective-permute-start(bf16[640,1024]{1,0:T(8,128)(2,1)} %get-tuple-element.363), channel_id=1, source_target_pairs={{24,16},{16,8},{8,0},{25,17},{17,9},{9,1},{26,18},{18,10},{10,2},{... | collective-permute-start | bytes 3932168 | tf_op jit(solution)/shard_map/ppermute | solution.py:585
  862.9 34.9 %collective-permute-start.30 = (bf16[1024,512]{1,0:T(8,128)(2,1)}, bf16[1024,512]{1,0:T(8,128)(2,1)S(1)}, u32[]{:S(2)}, u32[]{:S(2)}) collective-permute-start(bf16[1024,512]{1,0:T(8,128)(2,1)} %pad_maximum_fusion.5.refs_0_), channel_id=1, source_target_pairs={{0,4},{4,0},{1,5},{5,1},{2,6},{6,2},{3,7},{7,3},{8,12},{12,8},{9,1... | collective-permute-start | bytes 3145736 | tf_op jit(solution)/shard_map/ppermute | solution.py:530
  864.4 45.8 %collective-permute-start.32 = (bf16[1024,512]{1,0:T(8,128)(2,1)S(1)}, bf16[1024,512]{1,0:T(8,128)(2,1)S(1)}, u32[]{:S(2)}, u32[]{:S(2)}) collective-permute-start(bf16[1024,512]{1,0:T(8,128)(2,1)S(1)} %constant_dynamic-update-slice_fusion.6.refs_2_), channel_id=1, source_target_pairs={{0,4},{4,0},{1,5},{5,1},{2,6},{6,2},{3,7},{7,3},{8,12},{12,8},{9,1... | collective-permute-start | bytes 3145736 | tf_op jit(solution)/shard_map/ppermute | solution.py:530
  894.7 54.1 %collective-permute-start.55 = (bf16[640,1024]{1,0:T(8,128)(2,1)}, bf16[640,1024]{1,0:T(8,128)(2,1)}, u32[]{:S(2)}, u32[]{:S(2)}) collective-permute-start(bf16[640,1024]{1,0:T(8,128)(2,1)} %collective-permute-done.51), channel_id=1, source_target_pairs={{8,16},{16,24},{9,17},{17,25},{10,18},{18,26},{11,19},{19,27},{12,... | collective-permute-start | bytes 3932168 | tf_op jit(solution)/shard_map/ppermute | solution.py:584
  896.5 52.4 %collective-permute-start.56 = (bf16[640,1024]{1,0:T(8,128)(2,1)}, bf16[640,1024]{1,0:T(8,128)(2,1)}, u32[]{:S(2)}, u32[]{:S(2)}) collective-permute-start(bf16[640,1024]{1,0:T(8,128)(2,1)} %collective-permute-done.52), channel_id=1, source_target_pairs={{16,8},{8,0},{17,9},{9,1},{18,10},{10,2},{19,11},{11,3},{20,12},{1... | collective-permute-start | bytes 3932168 | tf_op jit(solution)/shard_map/ppermute | solution.py:585
  949.1 19.4 %collective-permute-start.60 = (bf16[256,640]{0,1:T(8,128)(2,1)S(1)}, bf16[256,640]{0,1:T(8,128)(2,1)S(1)}, u32[]{:S(2)}, u32[]{:S(2)}) collective-permute-start(bf16[256,640]{0,1:T(8,128)(2,1)S(1)} %get-tuple-element.375), channel_id=1, source_target_pairs={{24,16},{16,8},{8,0},{25,17},{17,9},{9,1},{26,18},{18,10},{10,2},{... | collective-permute-start | bytes 983048 | tf_op jit(solution)/shard_map/ppermute | solution.py:585
  950.4 18.1 %collective-permute-start.59 = (bf16[256,640]{0,1:T(8,128)(2,1)S(1)}, bf16[256,640]{0,1:T(8,128)(2,1)S(1)}, u32[]{:S(2)}, u32[]{:S(2)}) collective-permute-start(bf16[256,640]{0,1:T(8,128)(2,1)S(1)} %get-tuple-element.374), channel_id=1, source_target_pairs={{0,8},{8,16},{16,24},{1,9},{9,17},{17,25},{2,10},{10,18},{18,26},{... | collective-permute-start | bytes 983048 | tf_op jit(solution)/shard_map/ppermute | solution.py:584
  966.3 190.2 %collective-permute-start.29 = (bf16[1024,2048]{1,0:T(8,128)(2,1)}, bf16[1024,2048]{1,0:T(8,128)(2,1)}, u32[]{:S(2)}, u32[]{:S(2)}) collective-permute-start(bf16[1024,2048]{1,0:T(8,128)(2,1)} %add_convert_fusion.1), channel_id=1, source_target_pairs={{0,4},{4,0},{1,5},{5,1},{2,6},{6,2},{3,7},{7,3},{8,12},{12,8},{9,1... | collective-permute-start | bytes 12582920 | tf_op jit(solution)/shard_map/ppermute | solution.py:530
  967.7 60.8 %collective-permute-start.69 = (bf16[640,1024]{1,0:T(8,128)(2,1)}, bf16[640,1024]{1,0:T(8,128)(2,1)S(1)}, u32[]{:S(2)}, u32[]{:S(2)}) collective-permute-start(bf16[640,1024]{1,0:T(8,128)(2,1)} %collective-permute-done.55), channel_id=1, source_target_pairs={{16,24},{17,25},{18,26},{19,27},{20,28},{21,29},{22,30},{23,31}} | collective-permute-start | bytes 3932168 | tf_op jit(solution)/shard_map/ppermute | solution.py:584
  968.8 11.8 collective-permute-start.61
  972.8 57.0 %collective-permute-start.70 = (bf16[640,1024]{1,0:T(8,128)(2,1)}, bf16[640,1024]{1,0:T(8,128)(2,1)S(1)}, u32[]{:S(2)}, u32[]{:S(2)}) collective-permute-start(bf16[640,1024]{1,0:T(8,128)(2,1)} %collective-permute-done.56), channel_id=1, source_target_pairs={{8,0},{9,1},{10,2},{11,3},{12,4},{13,5},{14,6},{15,7}} | collective-permute-start | bytes 3932168 | tf_op jit(solution)/shard_map/ppermute | solution.py:585
  974.1 34.8 %collective-permute-start.62 = (bf16[256,640]{0,1:T(8,128)(2,1)S(1)}, bf16[256,640]{0,1:T(8,128)(2,1)S(1)}, u32[]{:S(2)}, u32[]{:S(2)}) collective-permute-start(bf16[256,640]{0,1:T(8,128)(2,1)S(1)} %get-tuple-element.365), channel_id=1, source_target_pairs={{24,16},{16,8},{8,0},{25,17},{17,9},{9,1},{26,18},{18,10},{10,2},{... | collective-permute-start | bytes 983048 | tf_op jit(solution)/shard_map/ppermute | solution.py:585
  980.6 32.0 %collective-permute-start.63 = (bf16[256,640]{0,1:T(8,128)(2,1)S(1)}, bf16[256,640]{0,1:T(8,128)(2,1)S(1)}, u32[]{:S(2)}, u32[]{:S(2)}) collective-permute-start(bf16[256,640]{0,1:T(8,128)(2,1)S(1)} %collective-permute-done.61), channel_id=1, source_target_pairs={{8,16},{16,24},{9,17},{17,25},{10,18},{18,26},{11,19},{19,27},{12,... | collective-permute-start | bytes 983048 | tf_op jit(solution)/shard_map/ppermute | solution.py:584
  1020.0 19.8 %collective-permute-start.37 = (f32[5248]{0:T(1024)S(1)}, f32[5248]{0:T(1024)S(1)}, u32[]{:S(2)}, u32[]{:S(2)}) collective-permute-start(f32[5248]{0:T(1024)S(1)} %pad_maximum_fusion.6), channel_id=1, source_target_pairs={{0,1},{1,0},{2,3},{3,2},{4,5},{5,4},{6,7},{7,6},{8,9},{9,8},{10,11... | collective-permute-start | bytes 62984 | tf_op jit(solution)/shard_map/ppermute | solution.py:618
  1027.8 117.7 %collective-permute-start.67 = (bf16[1024,640]{0,1:T(8,128)(2,1)S(1)}, bf16[1024,640]{0,1:T(8,128)(2,1)}, u32[]{:S(2)}, u32[]{:S(2)}) collective-permute-start(bf16[1024,640]{0,1:T(8,128)(2,1)S(1)} %slice.147), channel_id=1, source_target_pairs={{0,2},{1,3},{2,0},{3,1},{4,6},{5,7},{6,4},{7,5},{8,10},{9,11},{10,... | collective-permute-start | bytes 3932168 | tf_op jit(solution)/shard_map/ppermute | solution.py:527
  1036.8 107.7 %collective-permute-start.71 = (bf16[256,2048]{1,0:T(8,128)(2,1)S(1)}, bf16[256,2048]{1,0:T(8,128)(2,1)S(1)}, u32[]{:S(2)}, u32[]{:S(2)}) collective-permute-start(bf16[256,2048]{1,0:T(8,128)(2,1)S(1)} %reshape.645), channel_id=1, source_target_pairs={{0,2},{1,3},{2,0},{3,1},{4,6},{5,7},{6,4},{7,5},{8,10},{9,11},{10,... | collective-permute-start | bytes 3145736 | tf_op jit(solution)/shard_map/ppermute | solution.py:527
  1039.1 36.2 %collective-permute-start.73 = (f32[1024]{0:T(1024)S(1)}, f32[1024]{0:T(1024)S(1)}, u32[]{:S(2)}, u32[]{:S(2)}) collective-permute-start(f32[1024]{0:T(1024)S(1)} %bitcast.132), channel_id=1, source_target_pairs={{0,2},{1,3},{2,0},{3,1},{4,6},{5,7},{6,4},{7,5},{8,10},{9,11},{10,... | collective-permute-start | bytes 12296 | tf_op jit(solution)/shard_map/ppermute | solution.py:527
  1039.8 44.2 %collective-permute-start.38 = (f32[5248]{0:T(1024)S(1)}, f32[5248]{0:T(1024)S(1)}, u32[]{:S(2)}, u32[]{:S(2)}) collective-permute-start(f32[5248]{0:T(1024)S(1)} %fusion.36), channel_id=1, source_target_pairs={{0,2},{1,3},{2,0},{3,1},{4,6},{5,7},{6,4},{7,5},{8,10},{9,11},{10,... | collective-permute-start | bytes 62984 | tf_op jit(solution)/shard_map/ppermute | solution.py:618
  1084.0 60.4 %collective-permute-start.39 = (f32[5248]{0:T(1024)S(1)}, f32[5248]{0:T(1024)S(1)}, u32[]{:S(2)}, u32[]{:S(2)}) collective-permute-start(f32[5248]{0:T(1024)S(1)} %add.590), channel_id=1, source_target_pairs={{0,8},{8,0},{16,24},{24,16},{1,9},{9,1},{17,25},{25,17},{2,10},{10... | collective-permute-start | bytes 62984 | tf_op jit(solution)/shard_map/ppermute | solution.py:618
  1145.5 24.1 %collective-permute-start.72 = (bf16[512,2048]{1,0:T(8,128)(2,1)S(1)}, bf16[512,2048]{1,0:T(8,128)(2,1)S(1)}, u32[]{:S(2)}, u32[]{:S(2)}) collective-permute-start(bf16[512,2048]{1,0:T(8,128)(2,1)S(1)} %maximum_select_fusion.4), channel_id=1, source_target_pairs={{0,1},{1,0},{2,3},{3,2},{4,5},{5,4},{6,7},{7,6},{8,9},{9,8},{10,11... | collective-permute-start | bytes 6291464 | tf_op jit(solution)/shard_map/ppermute | solution.py:524
  1148.3 25.8 %collective-permute-start.68 = (bf16[2048,640]{0,1:T(8,128)(2,1)S(1)}, bf16[2048,640]{0,1:T(8,128)(2,1)S(1)}, u32[]{:S(2)}, u32[]{:S(2)}) collective-permute-start(bf16[2048,640]{0,1:T(8,128)(2,1)S(1)} %maximum_select_fusion.2), channel_id=1, source_target_pairs={{0,1},{1,0},{2,3},{3,2},{4,5},{5,4},{6,7},{7,6},{8,9},{9,8},{10,11... | collective-permute-start | bytes 7864328 | tf_op jit(solution)/shard_map/ppermute | solution.py:524
  (93 other events, 1305.5 us)
Sparse Core Ops, SparseCore 0:
  12.3 59.4 all-gather.3
  73.3 149.2 all-gather.5
  503.2 168.2 all-reduce.2
  733.6 63.6 all-gather.7

commit v2 on v1

--- a/solution.py
+++ b/solution.py
@@ -310,8 +310,8 @@
     add_to(sum_ref, jnp.concatenate(sums, 1), pl.program_id(0) == 0)
 
 
-def feed_far_kernel(steps, xa_ref, xb_ref, ca_ref, cb_ref, b_ref, ea_ref, eb_ref, u_ref, *rest):
-    w_refs, z_refs, v_ref = rest[:steps], rest[steps : 2 * steps], rest[2 * steps]
+def feed_far_kernel(steps, order, xa_ref, xb_ref, ca_ref, cb_ref, b_ref, ea_ref, eb_ref, u_ref, *rest):
+    w_refs, z_refs, v_refs = rest[:steps], rest[steps : 2 * steps], rest[2 * steps : 3 * steps]
     ga_ref, gb_ref, ha_ref, hb_ref, da_ref, db_ref, sum_ref, x_ref, c_ref, e_ref, low_ref = rest[-11:]
     i = pl.program_id(0)
     rows = xa_ref.shape[0]
@@ -326,7 +326,7 @@
 
         @pl.when(i == k)
         def _():
-            hidden, grad = feed_tile(x_ref[...], c_ref[...], w_refs[k][...], v_ref[...], b_ref[...])
+            hidden, grad = feed_tile(x_ref[...], c_ref[...], w_refs[k][...], v_refs[k][...], b_ref[...])
             low = grad.astype(BF16)
             ha_ref[...] = hidden[:rows]
             hb_ref[...] = hidden[rows:]
@@ -370,7 +370,7 @@
     )
 
 
-def feed_far(chunk, index, first_row, x_own, x_other, c_own, c_other, w, v, bias, near_own, near_other, w_near, kept):
+def feed_far(chunk, index, first_row, x_own, x_other, c_own, c_other, w, v, bias, near_own, near_other, w_near, kept, parity):
     rows, width = x_own.shape
     hid = w_near.shape[1]
     steps = len(w)
@@ -378,26 +378,26 @@
     out_blk = min(512, width)
     back = width // out_blk
     base = first_row // chunk
-    at = lambda i: (index, 0)
-    at_all = lambda i: (base + index, 0)
-    tile = lambda i: jnp.minimum(i, steps - 1)
+    at = lambda i, p: (index, 0)
+    at_all = lambda i, p: (base + index, 0)
+    tile = lambda i, p: lax.rem(jnp.minimum(i, steps - 1) + p[0], steps)
     after = lambda i: jnp.maximum(i - steps, 0)
     ins = [
         (x_own, (chunk, width), at),
         (x_other, (chunk, width), at),
         (c_own, (chunk, width), at_all),
         (c_other, (chunk, width), at_all),
-        (bias, (1, blk), lambda i: (0, tile(i))),
+        (bias, (1, blk), lambda i, p: (0, tile(i, p))),
         (near_own, (chunk, hid), at),
         (near_other, (chunk, hid), at),
-        (w_near, (out_blk, hid), lambda i: (after(i), 0)),
+        (w_near, (out_blk, hid), lambda i, p: (after(i), 0)),
     ]
     ins += [whole(p) for p in w]
-    ins += [(p, (out_blk, blk), lambda i: (after(i), 0)) for p in w]
-    ins += [(v, (blk, width), lambda i: (tile(i), 0))]
-    outs = [((chunk, width), BF16, (chunk, out_blk), lambda i: (0, after(i)))] * 2
-    outs += [((rows, hid), BF16, (chunk, blk), lambda i: (index, tile(i)))] * 4
-    outs += [((8, hid), F32, (8, blk), lambda i: (0, tile(i)))]
+    ins += [(u, (out_blk, blk), lambda i, p: (after(i), 0)) for u in w]
+    ins += [whole(p) for p in v]
+    outs = [((chunk, width), BF16, (chunk, out_blk), lambda i, p: (0, after(i)))] * 2
+    outs += [((rows, hid), BF16, (chunk, blk), lambda i, p: (index, tile(i, p)))] * 4
+    outs += [((8, hid), F32, (8, blk), lambda i, p: (0, tile(i, p)))]
     alias = {}
     arrays = [a for a, _, _ in ins]
     specs = [
@@ -405,38 +405,45 @@
     ]
     if kept is not None:
         for place, array in enumerate(kept):
-            alias[len(arrays)] = 2 + place
+            alias[len(arrays) + 1] = 2 + place
             arrays.append(array)
             specs.append(pl.BlockSpec(memory_space=pl.ANY))
     result = pl.pallas_call(
         functools.partial(feed_far_kernel, steps),
-        grid=(steps + back,),
-        in_specs=specs,
-        out_specs=[pl.BlockSpec(b, m) for _, _, b, m in outs],
+        grid_spec=pltpu.PrefetchScalarGridSpec(
+            num_scalar_prefetch=1,
+            grid=(steps + back,),
+            in_specs=specs,
+            out_specs=[pl.BlockSpec(b, m) for _, _, b, m in outs],
+            scratch_shapes=[
+                pltpu.VMEM((2 * chunk, width), BF16),
+                pltpu.VMEM((2 * chunk, width), BF16),
+                pltpu.VMEM((2 * chunk, hid), BF16),
+                pltpu.VMEM((steps, 2 * chunk, blk), BF16),
+            ],
+        ),
         out_shape=[jax.ShapeDtypeStruct(s, d) for s, d, _, _ in outs],
-        scratch_shapes=[
-            pltpu.VMEM((2 * chunk, width), BF16),
-            pltpu.VMEM((2 * chunk, width), BF16),
-            pltpu.VMEM((2 * chunk, hid), BF16),
-            pltpu.VMEM((steps, 2 * chunk, blk), BF16),
-        ],
         input_output_aliases=alias,
         compiler_params=pltpu.CompilerParams(vmem_limit_bytes=56 * MIB),
         cost_estimate=pl.CostEstimate(
             flops=8 * 2 * chunk * width * hid, bytes_accessed=8 * width * hid + 24 * chunk * width, transcendentals=0
         ),
-    )(*arrays)
+    )(parity.reshape(1), *arrays)
     return result[:2], result[2:6], result[6]
 
 
-def contract_kernel(count, *refs):
-    near, far = refs[:count], refs[count : 2 * count]
-    va_ref, vb_ref, own_ref, other_ref = refs[2 * count :]
+def contract_kernel(count, pieces, parity, *refs):
+    near, far = refs[:count], refs[count : count + count * pieces]
+    va_ref, *vb_refs = refs[count + count * pieces : count + count * pieces + pieces + 1]
+    own_ref, other_ref = refs[-2:]
     size = near[0].shape[0]
     for k in range(count):
         y_ref = own_ref if k < count // 2 else other_ref
         at = k % (count // 2) * size
-        y_ref[at : at + size, :] = (dot(near[k][...], va_ref[...]) + dot(far[k][...], vb_ref[...])).astype(BF16)
+        total = dot(near[k][...], va_ref[...])
+        for n in range(pieces):
+            total = total + dot(far[k * pieces + n][...], vb_refs[n][...])
+        y_ref[at : at + size, :] = total.astype(BF16)
 
 
 def pair_grad_kernel(*refs):
@@ -483,6 +490,17 @@
 
     sums_ref[0:1, :] += jnp.sum(grad * xhat, 0, keepdims=True)
     sums_ref[1:2, :] += jnp.sum(grad, 0, keepdims=True)
+
+
+def side_by_side_kernel(core, mine_ref, near_ref, query_ref, kv_ref):
+    first = core[0] == 0
+    mine, near = mine_ref[...].astype(F32), near_ref[...].astype(F32)
+    cols = query_ref.shape[1] // 2
+    left, right = jnp.where(first, mine, near), jnp.where(first, near, mine)
+    query_ref[:, :cols] = left[:, :cols]
+    query_ref[:, cols:] = right[:, :cols]
+    kv_ref[:, : kv_ref.shape[1] // 2] = left[:, cols:]
+    kv_ref[:, kv_ref.shape[1] // 2 :] = right[:, cols:]
 
 
 def body(
@@ -620,8 +638,6 @@
         return value
 
     keep_at, send_at = core * cols, (1 - core) * cols
-    out_keep = lax.dynamic_slice_in_dim(output_weight, keep_at, cols, 0)
-    out_send = lax.dynamic_slice_in_dim(output_weight, send_at, cols, 0)
     query_keep = lax.dynamic_slice_in_dim(query_weight, keep_at, cols, 1)
     query_send = lax.dynamic_slice_in_dim(query_weight, send_at, cols, 1)
 
@@ -660,15 +676,25 @@
         flops=4 * rows * width * dim,
         moved=4 * rows * width,
     )
+    output_weight, key_value = tie(output_weight, key_value)
+    out_keep = lax.dynamic_slice_in_dim(output_weight, keep_at, cols, 0)
+    out_send = lax.dynamic_slice_in_dim(output_weight, send_at, cols, 0)
     far_kv = far(key_value)
     near_kv = near(key_value)
     far_kv, expand_start, contract_start = tie(far_kv, expand_weight, contract_weight)
     pieces = hid // min(512, hid)
     size = hid // pieces
-    expand_far = [far(expand_start[:, :size])]
-    columns = [[g + 2 * b for b in range(chips)] for g in range(2)]
-    contract_both = lax.all_gather(contract_start, "rows", axis=0, tiled=True, axis_index_groups=columns)
-    contract_far = lax.dynamic_slice_in_dim(contract_both, (1 - chip) * hid, hid, 0)
+    helped = pieces == 2 and n_dp % 2 == 0
+    parity = lax.rem(dp_index, 2) if helped else jnp.int32(0)
+    if helped:
+        expand_far = [far(lax.dynamic_slice_in_dim(expand_start, parity * size, size, 1))]
+    else:
+        expand_far = [far(expand_start[:, k * size : (k + 1) * size]) for k in range(pieces)]
+    contract_start, expand_far[0] = tie(contract_start, expand_far[0])
+    if helped:
+        contract_far = [far(lax.dynamic_slice_in_dim(contract_start, parity * size, size, 0))]
+    else:
+        contract_far = [far(contract_start[k * size : (k + 1) * size]) for k in range(pieces)]
     pair_kv = ordered(core, key_value, near_kv, 0)
     far_pair = ordered(core, far_kv, near(far_kv), 0)
     kv_whole = ordered(chip, pair_kv, far_pair, 0)
@@ -744,20 +770,33 @@
         )
 
     attn, acts = [], []
-    out_all = heads_weights(out_keep, out_send, 0)
+    if n_heads == 2:
+        out_other = across(out_keep)
+    else:
+        out_all = heads_weights(out_keep, out_send, 0)
     info = scalars[0]
     for n in range(calls):
         if n == 1:
-            info, acts[0], expand_far[0] = tie(info, acts[0], expand_far[0])
+            if n_heads == 2:
+                info, out_other = tie(info, out_other)
+            info, expand_far[0] = tie(info, expand_far[0])
         own, for_near, lse = attn_forward(n, info)
-        if n == 0:
-            expand_start, lse = tie(expand_start, lse)
-            expand_far += [far(expand_start[:, k * size : (k + 1) * size]) for k in range(1, pieces)]
+        if n == 1:
+            own, for_near, acts[0][-1] = tie(own, for_near, acts[0][-1])
         other = near(for_near)
         attn.append((own, other, for_near, lse))
-        acts.append(jnp.concatenate([own, other], 1))
-    acts = [a for act in acts for a in heads_acts(act)]
-    acts[-1], expand_far[-1] = tie(acts[-1], expand_far[-1])
+        act = jnp.concatenate([own, other], 1)
+        if n == 0 and calls > 1:
+            info, act, cot_near = tie(info, act, cot_near)
+        acts.append(heads_acts(act))
+    acts = [a for act in acts for a in act]
+    if n_heads == 2:
+        out_all = [out_keep, out_send, out_other, near(out_other)]
+    if helped:
+        expand_far.append(beside(expand_far[0]))
+    acts[-1], contract_far[0], expand_far[-1] = tie(acts[-1], contract_far[0], expand_far[-1])
+    if helped:
+        contract_far.append(beside(contract_far[0]))
 
     halves = 2
     part_rows = rows // halves
@@ -823,6 +862,7 @@
                 near_parts[j][3],
                 expand_weight,
                 kept,
+                parity,
             )
             far_sums.append(bias_sum[0])
             sums_own.append(add(g_own, near(g_near)))
@@ -908,12 +948,18 @@
         keeps.append(keep)
         sends.append(near(send))
         sums.append(part[:4])
-    grad_low = jnp.concatenate(lows)
     grad_middle = jnp.concatenate(gms)
     grad_a, grad_b = jnp.concatenate(keeps), jnp.concatenate(sends)
     mid_sums = functools.reduce(lambda u, v: u + v, sums)
 
-    query_all = heads_weights(query_keep, query_send, 1)
+    if n_heads == 2:
+        query_late, lows[-1] = tie(query_keep, lows[-1])
+        query_other = across(query_late)
+        query_all = [query_keep, query_send, query_other, near(query_other)]
+    else:
+        query_all = heads_weights(query_keep, query_send, 1)
+
+    grad_low = jnp.concatenate(lows)
 
     def dot_left(left, right):
         return dot_tn(left, right).astype(BF16)
@@ -958,8 +1004,41 @@
             scratch=[pltpu.VMEM((part_heads, dim, bq), F32)],
             prefetch=1,
             vmem=48,
-            flops=40 * pairs_guess * part_cols,
-            moved=16 * rows * part_cols,
+            flops=pairs_guess,
+            moved=rows,
+        )
+
+    own_all = jnp.concatenate([a[0] for a in attn], 1)
+    other_all = jnp.concatenate([a[1] for a in attn], 1)
+    out_half = add(*chips_half(add(dot_left(own_all, grad_low), near(dot_left(other_all, grad_low)))))
+    expand_size = width // n_dp
+    out_size = out_half.shape[0] * width // hid // n_dp
+    joined = jnp.concatenate(
+        [add(expand_own, expand_moved).reshape(n_dp, expand_size, hid), out_half.reshape(n_dp, out_size, hid)], 1
+    )
+    joined = joined.reshape(-1, hid)
+
+    def feed_output(first_input):
+        count = 2 * halves
+        out_cols = min(512, width)
+        blocks = [
+            (p[n], (part_rows, size), lambda i, shift, k=k: (0, lax.rem(k + shift[0], pieces)))
+            for n in range(2)
+            for p in far_parts
+            for k in range(pieces)
+        ]
+        return call(
+            functools.partial(contract_kernel, count, pieces),
+            (width // out_cols,),
+            [(parity.reshape(1), None, None)]
+            + [whole(p) for p in [first_input, near_parts[1][0], near_parts[0][1], near_parts[1][1]]]
+            + blocks
+            + [(v, (v.shape[0], out_cols), lambda i, *_: (0, i)) for v in [contract_weight] + contract_far],
+            [((rows, width), BF16, (rows, out_cols), lambda i, *_: (0, i))] * 2,
+            flops=rows,
+            moved=rows,
+            vmem=56,
+            prefetch=1,
         )
 
     back_acts, dq_own, dq_other, dkv = [], [], [], None
@@ -967,31 +1046,28 @@
     for n in range(calls):
         if n == 0:
             info, contract_sum = tie(info, contract_sum)
-            contract_total = lax.psum(contract_sum, "dp")
-        if n == 1:
-            info, back_acts[0], expand_moved = tie(info, back_acts[0], expand_moved)
+            contract_half = contract_sum.shape[0] // 2
+            contract_first = lax.psum(contract_sum[:contract_half], "dp")
         own, for_near, dkv_part = attn_backward(n, info)
+        if n == 0:
+            mlp_start, dkv_part = tie(near_parts[0][0], dkv_part)
+            mlp_own, mlp_near = feed_output(mlp_start)
+            info, mlp_own, query_all[-2] = tie(info, mlp_own, query_all[-2])
+        if n == calls - 1:
+            for_near, contract_first = tie(for_near, contract_first)
+            contract_rest, contract_first = tie(contract_sum[contract_half:], contract_first)
+            contract_second = lax.psum(contract_rest, "dp")
+            for_near, joined = tie(for_near, joined)
+            expand_chain = Chain(joined)
+            expand_chain.step()
         other = near(for_near)
         dq_own.append(own)
         dq_other.append(other)
         back_acts.append(jnp.concatenate([own, other], 1))
+        if n == 0 and calls > 1:
+            info, back_acts[0] = tie(info, back_acts[0])
         dkv = dkv_part if dkv is None else dkv + dkv_part
     back_acts = [a for act in back_acts for a in heads_acts(act)]
-
-    count = 2 * halves
-    out_cols = min(512, width)
-    near_parts[0][0], dkv = tie(near_parts[0][0], dkv)
-    mlp_own, mlp_near = call(
-        functools.partial(contract_kernel, count),
-        (width // out_cols,),
-        [whole(p[n]) for n in range(2) for p in near_parts]
-        + [whole(p[n]) for n in range(2) for p in far_parts]
-        + [(v, (hid, out_cols), lambda i: (0, i)) for v in (contract_weight, contract_far)],
-        [((rows, width), BF16, (rows, out_cols), lambda i: (0, i))] * 2,
-        flops=8 * rows * width * hid,
-        moved=16 * rows * width,
-        vmem=56,
-    )
 
     dkv = dkv.reshape(chips, 2, rows, 2 * dim)
 
@@ -1003,6 +1079,13 @@
     first, second = heads_sum(chip_sum)
     grad_kv = add(first, second)
 
+    kv_keep = lax.dynamic_slice_in_dim(grad_kv, core * dim, dim, 1)
+    kv_send = lax.dynamic_slice_in_dim(grad_kv, (1 - core) * dim, dim, 1)
+    query_sent = near(dot_left(normed_first, jnp.concatenate(dq_other + [kv_send], 1)))
+    query_block = add(dot_left(normed_first, jnp.concatenate(dq_own + [kv_keep], 1)), query_sent)
+    query_chain = Chain(add(*chips_half(query_block)))
+    expand_chain.step()
+    grad_kv, expand_chain.up, expand_chain.down = tie(grad_kv, expand_chain.up, expand_chain.down)
     input_grad, first_sums = call(
         functools.partial(first_back_kernel, len(back_acts), sides),
         (rows // wide,),
@@ -1021,61 +1104,68 @@
         + [pltpu.VMEM((wide, width), F32)] * sides,
     )
 
-    mlp_first, mlp_second = heads_sum(add(mlp_own, near(mlp_near)))
+    mlp_sum, first_sums = tie(add(mlp_own, near(mlp_near)), first_sums)
+    mlp_first, mlp_second = heads_sum(mlp_sum)
     mlp_total = mlp_first.astype(F32) + mlp_second.astype(F32)
     layer_output = (jnp.concatenate(middles) + mlp_total + contract_bias).astype(BF16)
 
-    own_all = jnp.concatenate([a[0] for a in attn], 1)
-    other_all = jnp.concatenate([a[1] for a in attn], 1)
-    out_half = add(*chips_half(add(dot_left(own_all, grad_low), near(dot_left(other_all, grad_low)))))
-    expand_size = width // n_dp
-    out_size = out_half.shape[0] * width // hid // n_dp
-    joined = jnp.concatenate(
-        [add(expand_own, expand_moved).reshape(n_dp, expand_size, hid), out_half.reshape(n_dp, out_size, hid)], 1
-    )
-    expand_chain = Chain(joined.reshape(-1, hid))
-    kv_keep = lax.dynamic_slice_in_dim(grad_kv, core * dim, dim, 1)
-    kv_send = lax.dynamic_slice_in_dim(grad_kv, (1 - core) * dim, dim, 1)
-    query_sent = near(dot_left(normed_first, jnp.concatenate(dq_other + [kv_send], 1)))
-    query_block = add(dot_left(normed_first, jnp.concatenate(dq_own + [kv_keep], 1)), query_sent)
-    query_chain = Chain(add(*chips_half(query_block)))
     expand_chain.step()
-    expand_chain.step()
-    expand_chain.step()
-    expand_chain.up, contract_total = tie(expand_chain.up, contract_total)
-    for _ in range(3):
+    expand_chain.up, input_grad, contract_second = tie(expand_chain.up, input_grad, contract_second)
+    contract_weight_grad = jnp.concatenate([contract_first, contract_second]).astype(F32)
+    for k in range(3):
+        if k == 2:
+            expand_chain.up, contract_weight_grad = tie(expand_chain.up, contract_weight_grad)
         together([expand_chain, query_chain], [])
-    contract_weight_grad = contract_total.astype(F32)
     joined = expand_chain.result().reshape(n_dp, -1, hid)
     expand_weight_grad = joined[:, :expand_size].reshape(width, hid).astype(F32)
-    out_block, out_block_near = all_blocks(joined[:, expand_size:].reshape(out_half.shape))
-    output_weight_grad = ordered(core, out_block, out_block_near, 0).astype(F32)
-    query_block, query_block_near = all_blocks(query_chain.result())
-    query_weight_grad = ordered(core, query_block[:, :cols], query_block_near[:, :cols], 1).astype(F32)
-    key_value_weight_grad = ordered(core, query_block[:, cols:], query_block_near[:, cols:], 1).astype(F32)
-
     dq_bias_keep = jnp.concatenate([jnp.sum(v.astype(F32), 0) for v in dq_own])
     dq_bias_send = jnp.concatenate([jnp.sum(v.astype(F32), 0) for v in dq_other])
     query_bias_part = ordered(core, dq_bias_keep, dq_bias_send, 0)
     value_bias_part = jnp.sum(grad_kv[:, dim:].astype(F32), 0)
 
-    mid_total = lax.psum(mid_sums, ("dp", "rows"))
-    late = small_sum(jnp.concatenate([first_sums[0], first_sums[1], query_bias_part, value_bias_part]))
-    local = query_bias_part.shape[0]
-    expand_bias_grad = bias_near + far(bias_far)
-    hop = 1
-    while hop < n_dp:
-        expand_bias_grad = expand_bias_grad + lax.ppermute(expand_bias_grad, "dp", [(i, i ^ hop) for i in range(n_dp)])
-        hop *= 2
+    places_of_units = jnp.arange(n_rows)[:, None]
+    units = jnp.where(places_of_units == row_index, bias_near, 0.0) + jnp.where(
+        places_of_units == jnp.bitwise_xor(row_index, 2), bias_far, 0.0
+    )
+    shorts = [mid_sums, first_sums[:2], query_bias_part, value_bias_part, units]
+    short_sums = small_sum(jnp.concatenate([v.reshape(-1) for v in shorts]))
+    query_chain.up, expand_weight_grad, layer_output, short_sums = tie(
+        query_chain.up, expand_weight_grad, layer_output, short_sums
+    )
+    out_block, out_block_near = all_blocks(joined[:, expand_size:].reshape(out_half.shape))
+    output_weight_grad = ordered(core, out_block, out_block_near, 0).astype(F32)
+    query_block, query_block_near = all_blocks(query_chain.result())
+    query_weight_grad, key_value_weight_grad = call(
+        side_by_side_kernel,
+        (width // min(512, width),),
+        [
+            (core.reshape(1), None, None),
+            (query_block, (min(512, width), cols + dim), lambda i, *_: (i, 0)),
+            (query_block_near, (min(512, width), cols + dim), lambda i, *_: (i, 0)),
+        ],
+        [
+            ((width, 2 * cols), F32, (min(512, width), 2 * cols), lambda i, *_: (i, 0)),
+            ((width, 2 * dim), F32, (min(512, width), 2 * dim), lambda i, *_: (i, 0)),
+        ],
+        prefetch=1,
+        moved=12 * width * (cols + dim),
+    )
+
+    short_totals, at = [], 0
+    for v in shorts:
+        short_totals.append(short_sums[at : at + v.size].reshape(v.shape))
+        at += v.size
+    mid_total, first_total, query_bias_grad, value_bias_grad, units = short_totals
+    expand_bias_grad = lax.dynamic_index_in_dim(units, row_index, 0, keepdims=False)
     return (
         layer_output,
         input_grad,
-        late[:width],
-        late[width : 2 * width],
+        first_total[0],
+        first_total[1],
         query_weight_grad,
-        late[2 * width : 2 * width + local],
+        query_bias_grad,
         key_value_weight_grad,
-        late[2 * width + local :],
+        value_bias_grad,
         output_weight_grad,
         mid_total[2],
         mid_total[0],

time: 1200 us -> 1050 us (0.88)
  blocking collectives: 57.6 us -> 0 us
  starting transfers between devices: 152 us -> 118 us
  local copies, waits for them, and re-layouts: 111 us -> 78.9 us
  waiting for transfers between devices: 379 us -> 352 us
    ppermute x12 -> x11, waiting for transfers between devices: 219 us -> 113 us  [far(): return lax.ppermute(value, 'rows', [(i, i ^ 2) for i in range(n_rows)])]
    psum x1 -> x0, blocking collectives: 57.6 us -> none  [body(): mid_total = lax.psum(mid_sums, ('dp', 'rows'))]
    psum x1 -> x2, waiting for transfers between devices: 0.02 us -> 40.1 us  [the longest x1 25.1 us: body(): contract_first = lax.psum(contract_sum[:contract_half], 'dp')]
    ppermute x12, starting transfers between devices: 69.3 us -> 37 us  [step(): self.up = lax.ppermute(up, 'dp', [(i, i + 1) for i in ends])]
    ppermute x4, waiting for transfers between devices: 0.01 us -> 32.1 us  [small_sum(): lax.ppermute(value, axis, [(i, i ^ hop) for i in range(size)])]
    ppermute x12, waiting for transfers between devices: 59.8 us -> 32.7 us  [step(): lax.ppermute(down, 'dp', [(last - i, last - i - 1) for i in ends])]
    ppermute x12, waiting for transfers between devices: 59.2 us -> 81.5 us  [step(): self.up = lax.ppermute(up, 'dp', [(i, i + 1) for i in ends])]
    ppermute x2, waiting for transfers between devices: 6.08 us -> 23.3 us  [beside(): return lax.ppermute(value, 'dp', [(i, i ^ 1) for i in range(n_dp)])]
  transfers between devices with their start and end apart: 80 -> 79, of which waited for: 27 -> 32; matrix products, arithmetic and copies ran while one was open for 15% -> 16% of each run, Pallas kernels for 28% -> 31%
where the time goes in v2:
time: 1050 us; the launch traced here: 1040 us
  Pallas kernels  364 us (35%)
  waiting for transfers between devices  352 us (34%)
  starting transfers between devices  118 us (11%)
  other arithmetic  93.8 us (9%)
  local copies, waits for them, and re-layouts  78.9 us (8%)
  matrix products  19.8 us (2%)
  between operations  16.2 us (2%)
    pallas_call x19, Pallas kernels, call(): pl.pallas_call(kernel, grid_spec=pltpu.PrefetchScalarGridSpec(num_scalar_...  291 us
    ppermute x11, waiting for transfers between devices, far(): return lax.ppermute(value, 'rows', [(i, i ^ 2) for i in range(n_rows)])  113 us
    ppermute x12, waiting for transfers between devices, step(): self.up = lax.ppermute(up, 'dp', [(i, i + 1) for i in ends])  81.5 us
    pallas_call x4, Pallas kernels, feed_far(): pl.pallas_call(functools.partial(feed_far_kernel, steps), grid_spec=pltpu...  73.5 us
    convert_element_type x17, other arithmetic, add(): functools.reduce(lambda u, v: u + v, (t.astype(F32) for t in terms))  38.2 us
    ppermute x12, starting transfers between devices, step(): self.up = lax.ppermute(up, 'dp', [(i, i + 1) for i in ends])  37 us
    ppermute x11, starting transfers between devices, far(): return lax.ppermute(value, 'rows', [(i, i ^ 2) for i in range(n_rows)])  32.9 us
    ppermute x12, waiting for transfers between devices, step(): lax.ppermute(down, 'dp', [(last - i, last - i - 1) for i in ends])  32.7 us
  transfers between devices with their start and end apart: 79, of which 32 were waited for; matrix products, arithmetic and copies ran while one was open for 16% of the time, Pallas kernels for 31%

profile of v2, /device:TPU:0, one launch (start us, length us, event | category | flops | bytes accessed | tf_op | source)
XLA Modules:
  0.0 1042.8 jit_solution(1166873271172742882)
XLA Ops:
  10.5 5.6 shard_map.288
  21.4 7.8 shard_map.289
  29.7 4.9 constant_dynamic-slice_fusion.11
  46.4 15.8 %shard_map.290 = (bf16[1024,256]{1,0:T(8,128)(2,1)S(1)}, bf16[1024,256]{1,0:T(8,128)(2,1)S(1)}, f32[2,2048]{1,0:T(2,128)S(1)}) custom-call(s32[5,4]{1,0:T(8,128)S(1)} %stack.5.info, bf16[1024,512]{1,0:T(8,128)(2,1)S(1)} %get-tuple-element.174.qa_ref, bf16[1024,512]{1,0:T(8,128)(2,1)} %collective-permute-done.1.qb_ref, bf16[4096,256]{1,0:T(8,128)(2,1)S(1)} %copy-done.1, ...), custom_call_target="tpu_custom_call" | custom-call | flops 8589934592 | bytes 2097152 | tf_op jit(solution)/shard_map/pallas_call | solution.py:41
  64.3 23.9 %collective-permute-done.8.rest_0_.rest_2_ = bf16[2048,512]{1,0:T(8,128)(2,1)} collective-permute-done((bf16[2048,512]{1,0:T(8,128)(2,1)}, bf16[2048,512]{1,0:T(8,128)(2,1)}, u32[]{:S(2)}, u32[]{:S(2)}) %collective-permute-start.8) | collective-permute-done | bytes 2097184 | tf_op jit(solution)/shard_map/ppermute | solution.py:545
  91.2 15.7 %shard_map.291 = (bf16[1024,256]{1,0:T(8,128)(2,1)S(1)}, bf16[1024,256]{1,0:T(8,128)(2,1)S(1)}, f32[2,2048]{1,0:T(2,128)S(1)}) custom-call(s32[5,4]{1,0:T(8,128)S(1)} %stack.5.info, bf16[1024,512]{1,0:T(8,128)(2,1)S(1)} %get-tuple-element.174.qa_ref, bf16[1024,512]{1,0:T(8,128)(2,1)} %collective-permute-done.1.qb_ref, bf16[4096,256]{1,0:T(8,128)(2,1)S(1)} %copy-done.1, ...), custom_call_target="tpu_custom_call" | custom-call | flops 8589934592 | bytes 2097152 | tf_op jit(solution)/shard_map/pallas_call | solution.py:41
  106.9 5.9 collective-permute-done.9.refs_1_
  115.3 20.6 %collective-permute-done.12.rest_4_.refs_13_ = bf16[512,2048]{1,0:T(8,128)(2,1)} collective-permute-done((bf16[512,2048]{1,0:T(8,128)(2,1)S(1)}, bf16[512,2048]{1,0:T(8,128)(2,1)}, u32[]{:S(2)}, u32[]{:S(2)}) %collective-permute-start.12) | collective-permute-done | bytes 2097184 | tf_op jit(solution)/shard_map/ppermute | solution.py:545
  141.0 12.1 %shard_map.293 = (f32[512,2048]{1,0:T(8,128)}, bf16[512,2048]{1,0:T(8,128)(2,1)}) custom-call(bf16[1024,512]{1,0:T(8,128)(2,1)} %copy-done.29, bf16[1024,512]{1,0:T(8,128)(2,1)} %copy-done.41, bf16[1024,512]{1,0:T(8,128)(2,1)} %copy-done.34, bf16[1024,512]{1,0:T(8,128)(2,1)} %copy-done.42, bf16[512,2048]{1,0:T(8,128)(2,1)} %get-tuple-element.349.refs_4_.refs_7_, ...), custom_call_target="tpu_custom_call" | custom-call | flops 4294967296 | bytes 20971520 | tf_op jit(solution)/shard_map/pallas_call | solution.py:41
  154.7 6.0 collective-permute-start
  162.0 16.3 %shard_map.294 = (bf16[512,1024]{1,0:T(8,128)(2,1)}, bf16[512,1024]{1,0:T(8,128)(2,1)}, bf16[512,1024]{1,0:T(8,128)(2,1)}, bf16[512,1024]{1,0:T(8,128)(2,1)}, f32[8,1024]{1,0:T(8,128)}) custom-call(bf16[512,2048]{1,0:T(8,128)(2,1)} %get-tuple-element.200.xa_ref.refs_0_, bf16[512,2048]{1,0:T(8,128)(2,1)} %copy-done.50, bf16[1024,2048]{1,0:T(8,128)(2,1)} %refs_5_.7, ...), custom_call_target="tpu_custom_call" | custom-call | flops 8589934592 | bytes 25165824 | tf_op jit(solution)/shard_map/pallas_call | solution.py:41
  178.3 23.0 %collective-permute-done.17.rest_5_.refs_14_ = bf16[512,2048]{1,0:T(8,128)(2,1)S(1)} collective-permute-done((bf16[512,2048]{1,0:T(8,128)(2,1)}, bf16[512,2048]{1,0:T(8,128)(2,1)S(1)}, u32[]{:S(2)}, u32[]{:S(2)}) %collective-permute-start.17) | collective-permute-done | bytes 2097184 | tf_op jit(solution)/shard_map/ppermute | solution.py:551
  202.7 18.2 %shard_map.295 = (bf16[256,2048]{1,0:T(8,128)(2,1)}, bf16[256,2048]{1,0:T(8,128)(2,1)}, bf16[512,1024]{1,0:T(8,128)(2,1)}, bf16[512,1024]{1,0:T(8,128)(2,1)}, bf...) custom-call(s32[1]{0:T(128)} %bitcast.3.order.parity, ...), custom_call_target="tpu_custom_call" | custom-call | flops 8589934592 | bytes 29360128 | tf_op jit(solution)/shard_map/pallas_call | solution.py:411
  221.0 12.1 %shard_map.292 = (f32[512,2048]{1,0:T(8,128)}, bf16[512,2048]{1,0:T(8,128)(2,1)}) custom-call(bf16[1024,512]{1,0:T(8,128)(2,1)} %copy-done.29, bf16[1024,512]{1,0:T(8,128)(2,1)} %copy-done.41, bf16[1024,512]{1,0:T(8,128)(2,1)} %copy-done.34, bf16[1024,512]{1,0:T(8,128)(2,1)} %copy-done.42, bf16[512,2048]{1,0:T(8,128)(2,1)} %get-tuple-element.349.refs_4_.refs_7_, ...), custom_call_target="tpu_custom_call" | custom-call | flops 4294967296 | bytes 20971520 | tf_op jit(solution)/shard_map/pallas_call | solution.py:41
  233.8 4.6 constant_dynamic-slice_fusion.6
  241.1 18.3 %shard_map.296 = (bf16[256,2048]{1,0:T(8,128)(2,1)}, bf16[256,2048]{1,0:T(8,128)(2,1)}, bf16[512,1024]{1,0:T(8,128)(2,1)}, bf16[512,1024]{1,0:T(8,128)(2,1)}, bf...) custom-call(s32[1]{0:T(128)} %bitcast.3.order.parity, ...), custom_call_target="tpu_custom_call", output_to_operand_aliasing={{2}: (15, {}), {3}: (16, {}), {4}: (17, {}), {5}: (18, {})} | custom-call | flops 8589934592 | bytes 29360128 | tf_op jit(solution)/shard_map/pallas_call | solution.py:411
  259.6 16.2 %shard_map.297 = (bf16[512,1024]{1,0:T(8,128)(2,1)}, bf16[512,1024]{1,0:T(8,128)(2,1)}, bf16[512,1024]{1,0:T(8,128)(2,1)}, bf16[512,1024]{1,0:T(8,128)(2,1)}, f32[8,1024]{1,0:T(8,128)}) custom-call(bf16[512,2048]{1,0:T(8,128)(2,1)} %get-tuple-element.198.xa_ref.refs_1_, bf16[512,2048]{1,0:T(8,128)(2,1)} %collective-permute-done.15.xb_ref.refs_3_, ...), custom_call_target="tpu_custom_call" | custom-call | flops 8589934592 | bytes 25165824 | tf_op jit(solution)/shard_map/pallas_call | solution.py:41
  278.0 18.3 %shard_map.298 = (bf16[256,2048]{1,0:T(8,128)(2,1)}, bf16[256,2048]{1,0:T(8,128)(2,1)}, bf16[512,1024]{1,0:T(8,128)(2,1)}, bf16[512,1024]{1,0:T(8,128)(2,1)}, bf...) custom-call(s32[1]{0:T(128)} %bitcast.3.order.parity, ...), custom_call_target="tpu_custom_call" | custom-call | flops 8589934592 | bytes 29360128 | tf_op jit(solution)/shard_map/pallas_call | solution.py:411
  296.6 15.2 %shard_map.299 = bf16[1024,2048]{1,0:T(8,128)(2,1)} custom-call(bf16[512,1024]{1,0:T(8,128)(2,1)} %get-tuple-element.263.refs_0_, bf16[512,1024]{1,0:T(8,128)(2,1)} %get-tuple-element.223.refs_1_, bf16[512,1024]{1,0:T(8,128)(2,1)} %get-tuple-element.224.refs_2_, bf16[512,1024]{1,0:T(8,128)(2,1)} %get-tuple-element.225.refs_3_, bf16[1024,2048]{1,0:T(8,128)(2,1)} %refs_5_.7, ...), custom_call_target="tpu_custom_call" | custom-call | flops 17179869184 | bytes 16777216 | tf_op jit(solution)/shard_map/pallas_call | solution.py:41
  313.8 18.7 %shard_map.300 = (bf16[256,2048]{1,0:T(8,128)(2,1)}, bf16[256,2048]{1,0:T(8,128)(2,1)}, bf16[512,1024]{1,0:T(8,128)(2,1)}, bf16[512,1024]{1,0:T(8,128)(2,1)}, bf...) custom-call(s32[1]{0:T(128)} %bitcast.3.order.parity, ...), custom_call_target="tpu_custom_call", output_to_operand_aliasing={{2}: (15, {}), {3}: (16, {}), {4}: (17, {}), {5}: (18, {})} | custom-call | flops 8589934592 | bytes 29360128 | tf_op jit(solution)/shard_map/pallas_call | solution.py:411
  332.6 4.7 collective-permute-done.22.refs_3_
  338.8 14.7 %shard_map.303 = bf16[1024,2048]{1,0:T(8,128)(2,1)} custom-call(bf16[512,1024]{1,0:T(8,128)(2,1)} %get-tuple-element.241.refs_0_.refs_4_.refs_5_, bf16[512,1024]{1,0:T(8,128)(2,1)} %get-tuple-element.242.refs_1_.refs_6_.refs_7_, bf16[512,1024]{1,0:T(8,128)(2,1)} %get-tuple-element.243.refs_2_.refs_8_.refs_9_, ...), custom_call_target="tpu_custom_call" | custom-call | flops 17179869184 | bytes 16777216 | tf_op jit(solution)/shard_map/pallas_call | solution.py:41
  353.5 5.8 collective-permute-start.24
  359.3 13.6 %shard_map.301 = bf16[2048,1024]{1,0:T(8,128)(2,1)} custom-call(bf16[512,2048]{1,0:T(8,128)(2,1)} %get-tuple-element.200.xa_ref.refs_0_, bf16[512,2048]{1,0:T(8,128)(2,1)} %get-tuple-element.198.xa_ref.refs_1_, bf16[512,2048]{1,0:T(8,128)(2,1)} %copy-done.50, bf16[512,2048]{1,0:T(8,128)(2,1)} %collective-permute-done.15.xb_ref.refs_3_, ...), custom_call_target="tpu_custom_call" | custom-call | flops 17179869184 | bytes 16777216 | tf_op jit(solution)/shard_map/pallas_call | solution.py:41
  375.9 14.1 %shard_map.302 = bf16[2048,1024]{1,0:T(8,128)(2,1)} custom-call(bf16[512,2048]{1,0:T(8,128)(2,1)} %get-tuple-element.200.xa_ref.refs_0_, bf16[512,2048]{1,0:T(8,128)(2,1)} %get-tuple-element.198.xa_ref.refs_1_, bf16[512,2048]{1,0:T(8,128)(2,1)} %copy-done.50, bf16[512,2048]{1,0:T(8,128)(2,1)} %collective-permute-done.15.xb_ref.refs_3_, ...), custom_call_target="tpu_custom_call" | custom-call | flops 17179869184 | bytes 16777216 | tf_op jit(solution)/shard_map/pallas_call | solution.py:41
  390.0 12.8 %shard_map.304 = (f32[512,2048]{1,0:T(8,128)}, bf16[512,2048]{1,0:T(8,128)(2,1)}, bf16[512,512]{1,0:T(8,128)(2,1)}, bf16[512,512]{1,0:T(8,128)(2,1)}, f32[8,2048]{1,0:T(8,128)}) custom-call(bf16[256,2048]{1,0:T(8,128)(2,1)} %copy-done.45, bf16[256,2048]{1,0:T(8,128)(2,1)} %copy-done.47, bf16[256,2048]{1,0:T(8,128)(2,1)} %copy-done.61, ...), custom_call_target="tpu_custom_call" | custom-call | flops 2147483648 | bytes 20971520 | tf_op jit(solution)/shard_map/pallas_call | solution.py:41
  407.1 12.7 %shard_map.305 = (f32[512,2048]{1,0:T(8,128)}, bf16[512,2048]{1,0:T(8,128)(2,1)}, bf16[512,512]{1,0:T(8,128)(2,1)}, bf16[512,512]{1,0:T(8,128)(2,1)}, f32[8,2048]{1,0:T(8,128)}) custom-call(bf16[256,2048]{1,0:T(8,128)(2,1)} %copy-done.46, bf16[256,2048]{1,0:T(8,128)(2,1)} %add_convert_fusion.12.refs_1_, bf16[256,2048]{1,0:T(8,128)(2,1)} %copy-done.62, ...), custom_call_target="tpu_custom_call" | custom-call | flops 2147483648 | bytes 20971520 | tf_op jit(solution)/shard_map/pallas_call | solution.py:41
  424.1 6.3 convolution_convert_fusion.2
  434.3 15.3 %collective-permute-done.24 = bf16[1024,2048]{1,0:T(8,128)(2,1)} collective-permute-done((bf16[1024,2048]{1,0:T(8,128)(2,1)}, bf16[1024,2048]{1,0:T(8,128)(2,1)}, u32[]{:S(2)}, u32[]{:S(2)}) %collective-permute-start.24) | collective-permute-done | bytes 4194336 | tf_op jit(solution)/shard_map/ppermute | solution.py:545
  455.5 25.7 %shard_map.306 = (bf16[1024,256]{1,0:T(8,128)(2,1)S(1)}, bf16[1024,256]{1,0:T(8,128)(2,1)}, f32[4096,256]{1,0:T(8,128)}) custom-call(s32[5,8]{1,0:T(8,128)S(1)} %stack.4.info, bf16[1024,512]{1,0:T(8,128)(2,1)S(1)} %get-tuple-element.174.qa_ref, bf16[1024,512]{1,0:T(8,128)(2,1)} %collective-permute-done.1.qb_ref, ...), custom_call_target="tpu_custom_call" | custom-call | flops 2097152 | bytes 1024 | tf_op jit(solution)/shard_map/pallas_call | solution.py:41
  482.0 23.5 %shard_map.307 = (bf16[1024,2048]{1,0:T(8,128)(2,1)}, bf16[1024,2048]{1,0:T(8,128)(2,1)}) custom-call(s32[1]{0:T(128)} %bitcast.3.order.parity, bf16[512,1024]{1,0:T(8,128)(2,1)} %get-tuple-element.263.refs_0_, bf16[512,1024]{1,0:T(8,128)(2,1)} %get-tuple-element.223.refs_1_, bf16[512,1024]{1,0:T(8,128)(2,1)} %get-tuple-element.224.refs_2_, ...), custom_call_target="tpu_custom_call" | custom-call | flops 1024 | bytes 1024 | tf_op jit(solution)/shard_map/pallas_call | solution.py:41
  511.7 25.8 %shard_map.308 = (bf16[1024,256]{1,0:T(8,128)(2,1)S(1)}, bf16[1024,256]{1,0:T(8,128)(2,1)S(1)}, f32[4096,256]{1,0:T(8,128)}) custom-call(s32[5,8]{1,0:T(8,128)S(1)} %stack.4.info, bf16[1024,512]{1,0:T(8,128)(2,1)S(1)} %get-tuple-element.174.qa_ref, bf16[1024,512]{1,0:T(8,128)(2,1)} %collective-permute-done.1.qb_ref, ...), custom_call_target="tpu_custom_call" | custom-call | flops 2097152 | bytes 1024 | tf_op jit(solution)/shard_map/pallas_call | solution.py:41
  547.5 11.7 %collective-permute-start.33 = (bf16[256,2048]{1,0:T(8,128)(2,1)S(1)}, bf16[256,2048]{1,0:T(8,128)(2,1)}, u32[]{:S(2)}, u32[]{:S(2)}) collective-permute-start(bf16[256,2048]{1,0:T(8,128)(2,1)S(1)} %constant_dynamic-slice_fusion.9), channel_id=1, source_target_pairs={{0,2},{1,3},{2,0},{3,1},{4,6},{5,7},{6,4},{7,5},{8,10},{9,11},{10,... | collective-permute-start | bytes 3145736 | tf_op jit(solution)/shard_map/ppermute | solution.py:545
  564.0 19.3 %collective-permute-done.33 = bf16[256,2048]{1,0:T(8,128)(2,1)} collective-permute-done((bf16[256,2048]{1,0:T(8,128)(2,1)S(1)}, bf16[256,2048]{1,0:T(8,128)(2,1)}, u32[]{:S(2)}, u32[]{:S(2)}) %collective-permute-start.33) | collective-permute-done | bytes 1048608 | tf_op jit(solution)/shard_map/ppermute | solution.py:545
  585.3 25.1 %all-reduce.4.cloned.1.call-done = bf16[512,2048]{1,0:T(8,128)(2,1)} async-done(((bf16[512,2048]{1,0:T(8,128)(2,1)}), bf16[512,2048]{1,0:T(8,128)(2,1)}) %all-reduce.4.cloned.1.call-update) | async-done | bytes 2097168 | tf_op jit(solution)/shard_map/psum | solution.py:1050
  613.5 5.6 add_convert_fusion.1
  620.1 5.5 collective-permute-done.36
  632.7 6.0 convolution_convert_fusion
  644.6 16.9 %collective-permute-done.37 = bf16[640,1024]{1,0:T(8,128)(2,1)} collective-permute-done((bf16[640,1024]{1,0:T(8,128)(2,1)}, bf16[640,1024]{1,0:T(8,128)(2,1)}, u32[]{:S(2)}, u32[]{:S(2)}) %collective-permute-start.37) | collective-permute-done | bytes 1310752 | tf_op jit(solution)/shard_map/ppermute | solution.py:602
  665.4 4.5 collective-permute-start.38
  675.7 6.2 add_convert_fusion
  681.9 36.6 %collective-permute-done.38 = bf16[640,1024]{1,0:T(8,128)(2,1)S(1)} collective-permute-done((bf16[640,1024]{1,0:T(8,128)(2,1)S(1)}, bf16[640,1024]{1,0:T(8,128)(2,1)S(1)}, u32[]{:S(2)}, u32[]{:S(2)}) %collective-permute-start.38) | collective-permute-done | bytes 1310752 | tf_op jit(solution)/shard_map/ppermute | solution.py:602
  722.9 7.6 collective-permute-start.41
  742.1 25.1 %shard_map.309 = (bf16[1024,2048]{1,0:T(8,128)(2,1)}, f32[8,2048]{1,0:T(8,128)}) custom-call(bf16[1024,512]{1,0:T(8,128)(2,1)} %pad_maximum_fusion.5.refs_0_, bf16[1024,512]{1,0:T(8,128)(2,1)} %collective-permute-done.42.refs_1_, bf16[1024,512]{1,0:T(8,128)(2,1)} %copy-done.69, bf16[1024,512]{1,0:T(8,128)(2,1)} %copy-done.74, ...), custom_call_target="tpu_custom_call" | custom-call | flops 9663676416 | bytes 41943040 | tf_op jit(solution)/shard_map/pallas_call | solution.py:41
  769.7 15.0 %all-reduce.6.cloned.1.call-done = bf16[512,2048]{1,0:T(8,128)(2,1)} async-done(((bf16[512,2048]{1,0:T(8,128)(2,1)}), bf16[512,2048]{1,0:T(8,128)(2,1)}) %all-reduce.6.cloned.1.call-update) | async-done | bytes 2097168 | tf_op jit(solution)/shard_map/psum | solution.py:1059
  787.3 6.4 broadcast_in_dim.48
  797.7 5.6 collective-permute-start.49
  807.5 4.6 collective-permute-start.51
  812.9 24.4 %collective-permute-done.51 = bf16[256,640]{1,0:T(8,128)(2,1)S(1)} collective-permute-done((bf16[256,640]{1,0:T(8,128)(2,1)S(1)}, bf16[256,640]{1,0:T(8,128)(2,1)S(1)}, u32[]{:S(2)}, u32[]{:S(2)}) %collective-permute-start.51) | collective-permute-done | bytes 327712 | tf_op jit(solution)/shard_map/ppermute | solution.py:602
  846.1 8.7 collective-permute-start.64
  854.9 22.9 %collective-permute-done.64 = f32[17536]{0:T(1024)S(1)} collective-permute-done((f32[17536]{0:T(1024)S(1)}, f32[17536]{0:T(1024)S(1)}, u32[]{:S(2)}, u32[]{:S(2)}) %collective-permute-start.64) | collective-permute-done | bytes 70176 | tf_op jit(solution)/shard_map/ppermute | solution.py:636
  877.9 5.2 collective-permute-done.65
  886.0 7.3 maximum_convert_fusion
  898.5 7.2 fusion.1
  905.9 4.7 collective-permute-start.57
  913.6 15.7 %collective-permute-done.59 = bf16[640,1024]{1,0:T(8,128)(2,1)S(1)} collective-permute-done((bf16[640,1024]{1,0:T(8,128)(2,1)S(1)}, bf16[640,1024]{1,0:T(8,128)(2,1)S(1)}, u32[]{:S(2)}, u32[]{:S(2)}) %collective-permute-start.59) | collective-permute-done | bytes 1310752 | tf_op jit(solution)/shard_map/ppermute | solution.py:603
  932.4 4.7 bitcast_convert_fusion
  945.9 5.5 collective-permute-done.68
  954.9 6.3 collective-permute-done.70
  965.1 5.1 collective-permute-done.72
  977.1 25.9 %collective-permute-done.73 = bf16[1024,640]{1,0:T(8,128)(2,1)} collective-permute-done((bf16[1024,640]{1,0:T(8,128)(2,1)S(1)}, bf16[1024,640]{1,0:T(8,128)(2,1)}, u32[]{:S(2)}, u32[]{:S(2)}) %collective-permute-start.73) | collective-permute-done | bytes 1310752 | tf_op jit(solution)/shard_map/ppermute | solution.py:545
  1006.4 7.8 collective-permute-done.75
  1022.4 6.8 fusion.2
  1029.2 6.2 shard_map.310
  (409 shorter events, 206.4 us)
Async XLA Ops:
  7.2 603.3 %all-reduce.4.cloned.1.call-start = ((), (), s32[]{:S(2)}) async-start(), calls=%async_computation | async-start | bytes 4194304 | tf_op jit(solution)/shard_map/psum | solution.py:1050
  18.3 18.4 %collective-permute-start.3 = (bf16[1024,256]{0,1:T(8,128)(2,1)S(1)}, bf16[1024,256]{0,1:T(8,128)(2,1)S(1)}, u32[]{:S(2)}, u32[]{:S(2)}) collective-permute-start(bf16[1024,256]{0,1:T(8,128)(2,1)S(1)} %copy.86), channel_id=1, source_target_pairs={{0,2},{1,3},{2,0},{3,1},{4,6},{5,7},{6,4},{7,5},{8,10},{9,11},{10,... | collective-permute-start | bytes 1572872 | tf_op jit(solution)/shard_map/ppermute | solution.py:545
  21.4 18.7 %collective-permute-start.2 = (bf16[1024,256]{0,1:T(8,128)(2,1)S(1)}, bf16[1024,256]{0,1:T(8,128)(2,1)S(1)}, u32[]{:S(2)}, u32[]{:S(2)}) collective-permute-start(bf16[1024,256]{0,1:T(8,128)(2,1)S(1)} %copy.86), channel_id=1, source_target_pairs={{0,1},{1,0},{2,3},{3,2},{4,5},{5,4},{6,7},{7,6},{8,9},{9,8},{10,11... | collective-permute-start | bytes 1572872 | tf_op jit(solution)/shard_map/ppermute | solution.py:542
  29.2 15.7 %collective-permute-start.1 = (bf16[1024,512]{1,0:T(8,128)(2,1)}, bf16[1024,512]{1,0:T(8,128)(2,1)}, u32[]{:S(2)}, u32[]{:S(2)}) collective-permute-start(bf16[1024,512]{1,0:T(8,128)(2,1)} %get-tuple-element.175), channel_id=1, source_target_pairs={{0,1},{1,0},{2,3},{3,2},{4,5},{5,4},{6,7},{7,6},{8,9},{9,8},{10,11... | collective-permute-start | bytes 3145736 | tf_op jit(solution)/shard_map/ppermute | solution.py:542
  29.6 58.5 %collective-permute-start.6 = (bf16[1024,2048]{1,0:T(8,128)(2,1)}, bf16[1024,2048]{1,0:T(8,128)(2,1)}, u32[]{:S(2)}, u32[]{:S(2)}) collective-permute-start(bf16[1024,2048]{1,0:T(8,128)(2,1)} %refs_5_.7), channel_id=1, source_target_pairs={{0,1},{1,0},{2,3},{3,2},{4,5},{5,4},{6,7},{7,6},{8,9},{9,8},{10,11... | collective-permute-start | bytes 12582920 | tf_op jit(solution)/shard_map/ppermute | solution.py:542
  34.6 54.8 %collective-permute-start.7 = (bf16[512,2048]{1,0:T(8,128)(2,1)}, bf16[512,2048]{1,0:T(8,128)(2,1)}, u32[]{:S(2)}, u32[]{:S(2)}) collective-permute-start(bf16[512,2048]{1,0:T(8,128)(2,1)} %get-tuple-element.349.refs_4_.refs_7_), channel_id=1, source_target_pairs={{0,4},{4,0},{1,5},{5,1},{2,6},{6,2},{3,7},{7,3},{8,12},{12,8},{9,1... | collective-permute-start | bytes 6291464 | tf_op jit(solution)/shard_map/ppermute | solution.py:548
  40.0 48.2 %collective-permute-start.8 = (bf16[2048,512]{1,0:T(8,128)(2,1)}, bf16[2048,512]{1,0:T(8,128)(2,1)}, u32[]{:S(2)}, u32[]{:S(2)}) collective-permute-start(bf16[2048,512]{1,0:T(8,128)(2,1)} %constant_dynamic-slice_fusion.13), channel_id=1, source_target_pairs={{0,2},{1,3},{2,0},{3,1},{4,6},{5,7},{6,4},{7,5},{8,10},{9,11},{10,... | collective-permute-start | bytes 6291464 | tf_op jit(solution)/shard_map/ppermute | solution.py:545
  88.2 24.6 %collective-permute-start.9 = (bf16[1024,512]{1,0:T(8,128)(2,1)S(1)}, bf16[1024,512]{1,0:T(8,128)(2,1)S(1)}, u32[]{:S(2)}, u32[]{:S(2)}) collective-permute-start(bf16[1024,512]{1,0:T(8,128)(2,1)S(1)} %pad_maximum_fusion.3.refs_0_), channel_id=1, source_target_pairs={{0,4},{4,0},{1,5},{5,1},{2,6},{6,2},{3,7},{7,3},{8,12},{12,8},{9,1... | collective-permute-start | bytes 3145736 | tf_op jit(solution)/shard_map/ppermute | solution.py:548
  89.0 46.9 %collective-permute-start.12 = (bf16[512,2048]{1,0:T(8,128)(2,1)S(1)}, bf16[512,2048]{1,0:T(8,128)(2,1)}, u32[]{:S(2)}, u32[]{:S(2)}) collective-permute-start(bf16[512,2048]{1,0:T(8,128)(2,1)S(1)} %constant_dynamic-slice_fusion.12), channel_id=1, source_target_pairs={{0,2},{1,3},{2,0},{3,1},{4,6},{5,7},{6,4},{7,5},{8,10},{9,11},{10,... | collective-permute-start | bytes 6291464 | tf_op jit(solution)/shard_map/ppermute | solution.py:545
  89.3 46.9 %collective-permute-start.13 = (bf16[2048,512]{1,0:T(8,128)(2,1)}, bf16[2048,512]{1,0:T(8,128)(2,1)}, u32[]{:S(2)}, u32[]{:S(2)}) collective-permute-start(bf16[2048,512]{1,0:T(8,128)(2,1)} %collective-permute-done.8.rest_0_.rest_2_), channel_id=1, source_target_pairs={{0,8},{8,0},{16,24},{24,16},{1,9},{9,1},{17,25},{25,17},{2,10},{10... | collective-permute-start | bytes 6291464 | tf_op jit(solution)/shard_map/ppermute | solution.py:551
  91.1 48.8 %collective-permute-start.14 = (bf16[512,2048]{1,0:T(8,128)(2,1)}, bf16[512,2048]{1,0:T(8,128)(2,1)}, u32[]{:S(2)}, u32[]{:S(2)}) collective-permute-start(bf16[512,2048]{1,0:T(8,128)(2,1)} %collective-permute-done.7.refs_6_), channel_id=1, source_target_pairs={{0,1},{1,0},{2,3},{3,2},{4,5},{5,4},{6,7},{7,6},{8,9},{9,8},{10,11... | collective-permute-start | bytes 6291464 | tf_op jit(solution)/shard_map/ppermute | solution.py:542
  114.7 25.3 %collective-permute-start.11 = (bf16[1024,512]{1,0:T(8,128)(2,1)S(1)}, bf16[1024,512]{1,0:T(8,128)(2,1)S(1)}, u32[]{:S(2)}, u32[]{:S(2)}) collective-permute-start(bf16[1024,512]{1,0:T(8,128)(2,1)S(1)} %constant_dynamic-update-slice_fusion.refs_2_), channel_id=1, source_target_pairs={{0,4},{4,0},{1,5},{5,1},{2,6},{6,2},{3,7},{7,3},{8,12},{12,8},{9,1... | collective-permute-start | bytes 3145736 | tf_op jit(solution)/shard_map/ppermute | solution.py:548
  153.1 48.3 %collective-permute-start.17 = (bf16[512,2048]{1,0:T(8,128)(2,1)}, bf16[512,2048]{1,0:T(8,128)(2,1)S(1)}, u32[]{:S(2)}, u32[]{:S(2)}) collective-permute-start(bf16[512,2048]{1,0:T(8,128)(2,1)} %collective-permute-done.12.rest_4_.refs_13_), channel_id=1, source_target_pairs={{0,8},{8,0},{16,24},{24,16},{1,9},{9,1},{17,25},{25,17},{2,10},{10... | collective-permute-start | bytes 6291464 | tf_op jit(solution)/shard_map/ppermute | solution.py:551
  154.7 23.6 %collective-permute-start = (f32[1024]{0:T(1024)S(1)}, f32[1024]{0:T(1024)S(1)}, u32[]{:S(2)}, u32[]{:S(2)}) collective-permute-start(f32[1024]{0:T(1024)S(1)} %copy-done.75), channel_id=1, source_target_pairs={{0,2},{1,3},{2,0},{3,1},{4,6},{5,7},{6,4},{7,5},{8,10},{9,11},{10,... | collective-permute-start | bytes 12296 | tf_op jit(solution)/shard_map/ppermute | solution.py:545
  221.0 17.5 %collective-permute-start.18 = (bf16[256,2048]{1,0:T(8,128)(2,1)}, bf16[256,2048]{1,0:T(8,128)(2,1)S(1)}, u32[]{:S(2)}, u32[]{:S(2)}) collective-permute-start(bf16[256,2048]{1,0:T(8,128)(2,1)} %get-tuple-element.206), channel_id=1, source_target_pairs={{0,1},{1,0},{2,3},{3,2},{4,5},{5,4},{6,7},{7,6},{8,9},{9,8},{10,11... | collective-permute-start | bytes 3145736 | tf_op jit(solution)/shard_map/ppermute | solution.py:542
  233.2 26.4 %collective-permute-start.15 = (bf16[512,2048]{1,0:T(8,128)(2,1)}, bf16[512,2048]{1,0:T(8,128)(2,1)}, u32[]{:S(2)}, u32[]{:S(2)}) collective-permute-start(bf16[512,2048]{1,0:T(8,128)(2,1)} %get-tuple-element.198.xa_ref.refs_1_), channel_id=1, source_target_pairs={{0,1},{1,0},{2,3},{3,2},{4,5},{5,4},{6,7},{7,6},{8,9},{9,8},{10,11... | collective-permute-start | bytes 6291464 | tf_op jit(solution)/shard_map/ppermute | solution.py:542
  259.4 17.0 %collective-permute-start.19 = (bf16[256,2048]{1,0:T(8,128)(2,1)}, bf16[256,2048]{1,0:T(8,128)(2,1)}, u32[]{:S(2)}, u32[]{:S(2)}) collective-permute-start(bf16[256,2048]{1,0:T(8,128)(2,1)} %get-tuple-element.213), channel_id=1, source_target_pairs={{0,1},{1,0},{2,3},{3,2},{4,5},{5,4},{6,7},{7,6},{8,9},{9,8},{10,11... | collective-permute-start | bytes 3145736 | tf_op jit(solution)/shard_map/ppermute | solution.py:542
  275.8 38.0 %collective-permute-start.21 = (bf16[256,2048]{1,0:T(8,128)(2,1)S(1)}, bf16[256,2048]{1,0:T(8,128)(2,1)S(1)}, u32[]{:S(2)}, u32[]{:S(2)}) collective-permute-start(bf16[256,2048]{1,0:T(8,128)(2,1)S(1)} %add_convert_fusion.15.refs_0_), channel_id=1, source_target_pairs={{0,4},{4,0},{1,5},{5,1},{2,6},{6,2},{3,7},{7,3},{8,12},{12,8},{9,1... | collective-permute-start | bytes 3145736 | tf_op jit(solution)/shard_map/ppermute | solution.py:548
  296.3 17.1 %collective-permute-start.20 = (bf16[256,2048]{1,0:T(8,128)(2,1)}, bf16[256,2048]{1,0:T(8,128)(2,1)S(1)}, u32[]{:S(2)}, u32[]{:S(2)}) collective-permute-start(bf16[256,2048]{1,0:T(8,128)(2,1)} %get-tuple-element.218), channel_id=1, source_target_pairs={{0,1},{1,0},{2,3},{3,2},{4,5},{5,4},{6,7},{7,6},{8,9},{9,8},{10,11... | collective-permute-start | bytes 3145736 | tf_op jit(solution)/shard_map/ppermute | solution.py:542
  311.8 25.5 %collective-permute-start.22 = (bf16[256,2048]{1,0:T(8,128)(2,1)S(1)}, bf16[256,2048]{1,0:T(8,128)(2,1)}, u32[]{:S(2)}, u32[]{:S(2)}) collective-permute-start(bf16[256,2048]{1,0:T(8,128)(2,1)S(1)} %add_convert_fusion.14.refs_1_), channel_id=1, source_target_pairs={{0,4},{4,0},{1,5},{5,1},{2,6},{6,2},{3,7},{7,3},{8,12},{12,8},{9,1... | collective-permute-start | bytes 3145736 | tf_op jit(solution)/shard_map/ppermute | solution.py:548
  332.5 40.5 %collective-permute-start.25 = (bf16[256,2048]{1,0:T(8,128)(2,1)}, bf16[256,2048]{1,0:T(8,128)(2,1)S(1)}, u32[]{:S(2)}, u32[]{:S(2)}) collective-permute-start(bf16[256,2048]{1,0:T(8,128)(2,1)} %get-tuple-element.255), channel_id=1, source_target_pairs={{0,1},{1,0},{2,3},{3,2},{4,5},{5,4},{6,7},{7,6},{8,9},{9,8},{10,11... | collective-permute-start | bytes 3145736 | tf_op jit(solution)/shard_map/ppermute | solution.py:542
  337.3 38.6 %collective-permute-start.23 = (bf16[256,2048]{1,0:T(8,128)(2,1)S(1)}, bf16[256,2048]{1,0:T(8,128)(2,1)S(1)}, u32[]{:S(2)}, u32[]{:S(2)}) collective-permute-start(bf16[256,2048]{1,0:T(8,128)(2,1)S(1)} %add_convert_fusion.13.refs_0_), channel_id=1, source_target_pairs={{0,4},{4,0},{1,5},{5,1},{2,6},{6,2},{3,7},{7,3},{8,12},{12,8},{9,1... | collective-permute-start | bytes 3145736 | tf_op jit(solution)/shard_map/ppermute | solution.py:548
  353.5 96.1 %collective-permute-start.24 = (bf16[1024,2048]{1,0:T(8,128)(2,1)}, bf16[1024,2048]{1,0:T(8,128)(2,1)}, u32[]{:S(2)}, u32[]{:S(2)}) collective-permute-start(bf16[1024,2048]{1,0:T(8,128)(2,1)} %shard_map.303), channel_id=1, source_target_pairs={{0,2},{1,3},{2,0},{3,1},{4,6},{5,7},{6,4},{7,5},{8,10},{9,11},{10,... | collective-permute-start | bytes 12582920 | tf_op jit(solution)/shard_map/ppermute | solution.py:545
  374.3 32.7 %collective-permute-start.26 = (bf16[256,2048]{1,0:T(8,128)(2,1)}, bf16[256,2048]{1,0:T(8,128)(2,1)}, u32[]{:S(2)}, u32[]{:S(2)}) collective-permute-start(bf16[256,2048]{1,0:T(8,128)(2,1)} %add_convert_fusion.12.refs_1_), channel_id=1, source_target_pairs={{0,4},{4,0},{1,5},{5,1},{2,6},{6,2},{3,7},{7,3},{8,12},{12,8},{9,1... | collective-permute-start | bytes 3145736 | tf_op jit(solution)/shard_map/ppermute | solution.py:548
  419.8 14.4 %collective-permute-start.28 = (bf16[512,512]{1,0:T(8,128)(2,1)}, bf16[512,512]{1,0:T(8,128)(2,1)S(1)}, u32[]{:S(2)}, u32[]{:S(2)}) collective-permute-start(bf16[512,512]{1,0:T(8,128)(2,1)} %get-tuple-element.260), channel_id=1, source_target_pairs={{0,1},{1,0},{2,3},{3,2},{4,5},{5,4},{6,7},{7,6},{8,9},{9,8},{10,11... | collective-permute-start | bytes 1572872 | tf_op jit(solution)/shard_map/ppermute | solution.py:542
  420.4 85.1 %collective-permute-start.29 = (bf16[2048,512]{1,0:T(8,128)(2,1)}, bf16[2048,512]{1,0:T(8,128)(2,1)}, u32[]{:S(2)}, u32[]{:S(2)}) collective-permute-start(bf16[2048,512]{1,0:T(8,128)(2,1)} %get-tuple-element.266.refs_4_), channel_id=1, source_target_pairs={{0,4},{4,0},{1,5},{5,1},{2,6},{6,2},{3,7},{7,3},{8,12},{12,8},{9,1... | collective-permute-start | bytes 6291464 | tf_op jit(solution)/shard_map/ppermute | solution.py:548
  430.4 110.9 %collective-permute-start.32 = (bf16[512,2048]{1,0:T(8,128)(2,1)}, bf16[512,2048]{1,0:T(8,128)(2,1)}, u32[]{:S(2)}, u32[]{:S(2)}) collective-permute-start(bf16[512,2048]{1,0:T(8,128)(2,1)} %convolution_convert_fusion.2), channel_id=1, source_target_pairs={{0,1},{1,0},{2,3},{3,2},{4,5},{5,4},{6,7},{7,6},{8,9},{9,8},{10,11... | collective-permute-start | bytes 6291464 | tf_op jit(solution)/shard_map/ppermute | solution.py:542
  449.6 163.9 %collective-permute-start.31 = (bf16[2048,1024]{1,0:T(8,128)(2,1)}, bf16[2048,1024]{1,0:T(8,128)(2,1)}, u32[]{:S(2)}, u32[]{:S(2)}) collective-permute-start(bf16[2048,1024]{1,0:T(8,128)(2,1)} %shard_map.301), channel_id=1, source_target_pairs={{0,2},{1,3},{2,0},{3,1},{4,6},{5,7},{6,4},{7,5},{8,10},{9,11},{10,... | collective-permute-start | bytes 12582920 | tf_op jit(solution)/shard_map/ppermute | solution.py:545
  482.0 26.6 %collective-permute-start.30 = (bf16[1024,256]{1,0:T(8,128)(2,1)}, bf16[1024,256]{1,0:T(8,128)(2,1)}, u32[]{:S(2)}, u32[]{:S(2)}) collective-permute-start(bf16[1024,256]{1,0:T(8,128)(2,1)} %get-tuple-element.269), channel_id=1, source_target_pairs={{0,1},{1,0},{2,3},{3,2},{4,5},{5,4},{6,7},{7,6},{8,9},{9,8},{10,11... | collective-permute-start | bytes 1572872 | tf_op jit(solution)/shard_map/ppermute | solution.py:542
  508.1 276.6 %all-reduce.6.cloned.1.call-start = ((), (), s32[]{:S(2)}) async-start(), calls=%async_computation.1 | async-start | bytes 4194304 | tf_op jit(solution)/shard_map/psum | solution.py:1059
  540.7 18.5 %collective-permute-start.34 = (bf16[2,1024,256]{2,1,0:T(8,128)(2,1)S(1)}, bf16[2,1024,256]{2,1,0:T(8,128)(2,1)}, u32[]{:S(2)}, u32[]{:S(2)}) collective-permute-start(bf16[2,1024,256]{2,1,0:T(8,128)(2,1)S(1)} %fusion.13), channel_id=1, source_target_pairs={{0,1},{1,0},{2,3},{3,2},{4,5},{5,4},{6,7},{7,6},{8,9},{9,8},{10,11... | collective-permute-start | bytes 3145736 | tf_op jit(solution)/shard_map/ppermute | solution.py:542
  547.5 35.8 %collective-permute-start.33 = (bf16[256,2048]{1,0:T(8,128)(2,1)S(1)}, bf16[256,2048]{1,0:T(8,128)(2,1)}, u32[]{:S(2)}, u32[]{:S(2)}) collective-permute-start(bf16[256,2048]{1,0:T(8,128)(2,1)S(1)} %constant_dynamic-slice_fusion.9), channel_id=1, source_target_pairs={{0,2},{1,3},{2,0},{3,1},{4,6},{5,7},{6,4},{7,5},{8,10},{9,11},{10,... | collective-permute-start | bytes 3145736 | tf_op jit(solution)/shard_map/ppermute | solution.py:545
  562.9 47.6 %collective-permute-start.35 = (bf16[1024,256]{1,0:T(8,128)(2,1)S(1)}, bf16[1024,256]{1,0:T(8,128)(2,1)}, u32[]{:S(2)}, u32[]{:S(2)}) collective-permute-start(bf16[1024,256]{1,0:T(8,128)(2,1)S(1)} %fusion.19), channel_id=1, source_target_pairs={{0,2},{1,3},{2,0},{3,1},{4,6},{5,7},{6,4},{7,5},{8,10},{9,11},{10,... | collective-permute-start | bytes 1572872 | tf_op jit(solution)/shard_map/ppermute | solution.py:545
  563.8 110.6 %collective-permute-start.60 = (bf16[1024,2048]{1,0:T(8,128)(2,1)}, bf16[1024,2048]{1,0:T(8,128)(2,1)}, u32[]{:S(2)}, u32[]{:S(2)}) collective-permute-start(bf16[1024,2048]{1,0:T(8,128)(2,1)} %get-tuple-element.309), channel_id=1, source_target_pairs={{0,1},{1,0},{2,3},{3,2},{4,5},{5,4},{6,7},{7,6},{8,9},{9,8},{10,11... | collective-permute-start | bytes 12582920 | tf_op jit(solution)/shard_map/ppermute | solution.py:542
  611.9 13.7 %collective-permute-start.36 = (bf16[1024,256]{1,0:T(8,128)(2,1)S(1)}, bf16[1024,256]{1,0:T(8,128)(2,1)S(1)}, u32[]{:S(2)}, u32[]{:S(2)}) collective-permute-start(bf16[1024,256]{1,0:T(8,128)(2,1)S(1)} %fusion.18), channel_id=1, source_target_pairs={{0,4},{4,0},{1,5},{5,1},{2,6},{6,2},{3,7},{7,3},{8,12},{12,8},{9,1... | collective-permute-start | bytes 1572872 | tf_op jit(solution)/shard_map/ppermute | solution.py:548
  620.1 12.5 %collective-permute-start.43 = (bf16[1024,256]{1,0:T(8,128)(2,1)S(1)}, bf16[1024,256]{1,0:T(8,128)(2,1)S(1)}, u32[]{:S(2)}, u32[]{:S(2)}) collective-permute-start(bf16[1024,256]{1,0:T(8,128)(2,1)S(1)} %copy-done.20), channel_id=1, source_target_pairs={{0,1},{1,0},{2,3},{3,2},{4,5},{5,4},{6,7},{7,6},{8,9},{9,8},{10,11... | collective-permute-start | bytes 1572872 | tf_op jit(solution)/shard_map/ppermute | solution.py:542
  627.7 33.8 %collective-permute-start.37 = (bf16[640,1024]{1,0:T(8,128)(2,1)}, bf16[640,1024]{1,0:T(8,128)(2,1)}, u32[]{:S(2)}, u32[]{:S(2)}) collective-permute-start(bf16[640,1024]{1,0:T(8,128)(2,1)} %get-tuple-element.343), channel_id=1, source_target_pairs={{0,8},{1,9},{2,10},{3,11},{4,12},{5,13},{6,14},{7,15}} | collective-permute-start | bytes 3932168 | tf_op jit(solution)/shard_map/ppermute | solution.py:602
  630.6 30.8 %collective-permute-start.39 = (bf16[640,1024]{1,0:T(8,128)(2,1)}, bf16[640,1024]{1,0:T(8,128)(2,1)}, u32[]{:S(2)}, u32[]{:S(2)}) collective-permute-start(bf16[640,1024]{1,0:T(8,128)(2,1)} %get-tuple-element.342), channel_id=1, source_target_pairs={{24,16},{25,17},{26,18},{27,19},{28,20},{29,21},{30,22},{31,23}} | collective-permute-start | bytes 3932168 | tf_op jit(solution)/shard_map/ppermute | solution.py:603
  638.7 91.7 %collective-permute-start.47 = (bf16[2048,640]{1,0:T(8,128)(2,1)}, bf16[2048,640]{1,0:T(8,128)(2,1)}, u32[]{:S(2)}, u32[]{:S(2)}) collective-permute-start(bf16[2048,640]{1,0:T(8,128)(2,1)} %convolution_convert_fusion), channel_id=1, source_target_pairs={{0,1},{1,0},{2,3},{3,2},{4,5},{5,4},{6,7},{7,6},{8,9},{9,8},{10,11... | collective-permute-start | bytes 7864328 | tf_op jit(solution)/shard_map/ppermute | solution.py:542
  643.2 94.3 %collective-permute-start.45 = (bf16[2048,512]{1,0:T(8,128)(2,1)}, bf16[2048,512]{1,0:T(8,128)(2,1)}, u32[]{:S(2)}, u32[]{:S(2)}) collective-permute-start(bf16[2048,512]{1,0:T(8,128)(2,1)} %collective-permute-done.29.refs_6_), channel_id=1, source_target_pairs={{0,1},{1,0},{2,3},{3,2},{4,5},{5,4},{6,7},{7,6},{8,9},{9,8},{10,11... | collective-permute-start | bytes 6291464 | tf_op jit(solution)/shard_map/ppermute | solution.py:542
  665.4 53.2 %collective-permute-start.38 = (bf16[640,1024]{1,0:T(8,128)(2,1)S(1)}, bf16[640,1024]{1,0:T(8,128)(2,1)S(1)}, u32[]{:S(2)}, u32[]{:S(2)}) collective-permute-start(bf16[640,1024]{1,0:T(8,128)(2,1)S(1)} %get-tuple-element.341), channel_id=1, source_target_pairs={{0,8},{8,16},{1,9},{9,17},{2,10},{10,18},{3,11},{11,19},{4,12},{12... | collective-permute-start | bytes 3932168 | tf_op jit(solution)/shard_map/ppermute | solution.py:602
  669.8 50.2 %collective-permute-start.40 = (bf16[640,1024]{1,0:T(8,128)(2,1)S(1)}, bf16[640,1024]{1,0:T(8,128)(2,1)S(1)}, u32[]{:S(2)}, u32[]{:S(2)}) collective-permute-start(bf16[640,1024]{1,0:T(8,128)(2,1)S(1)} %get-tuple-element.340), channel_id=1, source_target_pairs={{24,16},{16,8},{25,17},{17,9},{26,18},{18,10},{27,19},{19,11},{28,... | collective-permute-start | bytes 3932168 | tf_op jit(solution)/shard_map/ppermute | solution.py:603
  674.4 61.7 %collective-permute-start.42 = (bf16[1024,512]{1,0:T(8,128)(2,1)S(1)}, bf16[1024,512]{1,0:T(8,128)(2,1)}, u32[]{:S(2)}, u32[]{:S(2)}) collective-permute-start(bf16[1024,512]{1,0:T(8,128)(2,1)S(1)} %copy-done.60), channel_id=1, source_target_pairs={{0,4},{4,0},{1,5},{5,1},{2,6},{6,2},{3,7},{7,3},{8,12},{12,8},{9,1... | collective-permute-start | bytes 3145736 | tf_op jit(solution)/shard_map/ppermute | solution.py:548
  718.5 22.6 %collective-permute-start.44 = (bf16[1024,512]{1,0:T(8,128)(2,1)S(1)}, bf16[1024,512]{1,0:T(8,128)(2,1)S(1)}, u32[]{:S(2)}, u32[]{:S(2)}) collective-permute-start(bf16[1024,512]{1,0:T(8,128)(2,1)S(1)} %constant_dynamic-update-slice_fusion.8.refs_2_), channel_id=1, source_target_pairs={{0,4},{4,0},{1,5},{5,1},{2,6},{6,2},{3,7},{7,3},{8,12},{12,8},{9,1... | collective-permute-start | bytes 3145736 | tf_op jit(solution)/shard_map/ppermute | solution.py:548
  722.9 62.3 %collective-permute-start.41 = (bf16[640,1024]{1,0:T(8,128)(2,1)}, bf16[640,1024]{1,0:T(8,128)(2,1)}, u32[]{:S(2)}, u32[]{:S(2)}) collective-permute-start(bf16[640,1024]{1,0:T(8,128)(2,1)} %get-tuple-element.339), channel_id=1, source_target_pairs={{0,8},{8,16},{16,24},{1,9},{9,17},{17,25},{2,10},{10,18},{18,26},{... | collective-permute-start | bytes 3932168 | tf_op jit(solution)/shard_map/ppermute | solution.py:602
  730.5 56.8 %collective-permute-start.46 = (bf16[640,1024]{1,0:T(8,128)(2,1)}, bf16[640,1024]{1,0:T(8,128)(2,1)}, u32[]{:S(2)}, u32[]{:S(2)}) collective-permute-start(bf16[640,1024]{1,0:T(8,128)(2,1)} %get-tuple-element.338), channel_id=1, source_target_pairs={{24,16},{16,8},{8,0},{25,17},{17,9},{9,1},{26,18},{18,10},{10,2},{... | collective-permute-start | bytes 3932168 | tf_op jit(solution)/shard_map/ppermute | solution.py:603
  736.1 49.0 %collective-permute-start.48 = (bf16[1024,640]{1,0:T(8,128)(2,1)S(1)}, bf16[1024,640]{1,0:T(8,128)(2,1)}, u32[]{:S(2)}, u32[]{:S(2)}) collective-permute-start(bf16[1024,640]{1,0:T(8,128)(2,1)S(1)} %constant_dynamic-slice_fusion.3), channel_id=1, source_target_pairs={{0,2},{1,3},{2,0},{3,1},{4,6},{5,7},{6,4},{7,5},{8,10},{9,11},{10,... | collective-permute-start | bytes 3932168 | tf_op jit(solution)/shard_map/ppermute | solution.py:545
  767.2 131.3 %collective-permute-start.61 = (bf16[1024,2048]{1,0:T(8,128)(2,1)}, bf16[1024,2048]{1,0:T(8,128)(2,1)}, u32[]{:S(2)}, u32[]{:S(2)}) collective-permute-start(bf16[1024,2048]{1,0:T(8,128)(2,1)} %add_convert_fusion), channel_id=1, source_target_pairs={{0,4},{4,0},{1,5},{5,1},{2,6},{6,2},{3,7},{7,3},{8,12},{12,8},{9,1... | collective-permute-start | bytes 12582920 | tf_op jit(solution)/shard_map/ppermute | solution.py:548
  797.7 39.6 %collective-permute-start.49 = (bf16[640,1024]{1,0:T(8,128)(2,1)S(1)}, bf16[640,1024]{1,0:T(8,128)(2,1)}, u32[]{:S(2)}, u32[]{:S(2)}) collective-permute-start(bf16[640,1024]{1,0:T(8,128)(2,1)S(1)} %get-tuple-element.337), channel_id=1, source_target_pairs={{0,8},{8,16},{16,24},{1,9},{9,17},{17,25},{2,10},{10,18},{18,26},{... | collective-permute-start | bytes 3932168 | tf_op jit(solution)/shard_map/ppermute | solution.py:602
  803.4 34.0 %collective-permute-start.50 = (bf16[640,1024]{1,0:T(8,128)(2,1)S(1)}, bf16[640,1024]{1,0:T(8,128)(2,1)}, u32[]{:S(2)}, u32[]{:S(2)}) collective-permute-start(bf16[640,1024]{1,0:T(8,128)(2,1)S(1)} %get-tuple-element.337), channel_id=1, source_target_pairs={{24,16},{16,8},{8,0},{25,17},{17,9},{9,1},{26,18},{18,10},{10,2},{... | collective-permute-start | bytes 3932168 | tf_op jit(solution)/shard_map/ppermute | solution.py:603
  807.5 29.8 %collective-permute-start.51 = (bf16[256,640]{1,0:T(8,128)(2,1)S(1)}, bf16[256,640]{1,0:T(8,128)(2,1)S(1)}, u32[]{:S(2)}, u32[]{:S(2)}) collective-permute-start(bf16[256,640]{1,0:T(8,128)(2,1)S(1)} %get-tuple-element.355), channel_id=1, source_target_pairs={{0,8},{1,9},{2,10},{3,11},{4,12},{5,13},{6,14},{7,15}} | collective-permute-start | bytes 983048 | tf_op jit(solution)/shard_map/ppermute | solution.py:602
  812.1 25.3 %collective-permute-start.52 = (bf16[256,640]{1,0:T(8,128)(2,1)S(1)}, bf16[256,640]{1,0:T(8,128)(2,1)S(1)}, u32[]{:S(2)}, u32[]{:S(2)}) collective-permute-start(bf16[256,640]{1,0:T(8,128)(2,1)S(1)} %get-tuple-element.354), channel_id=1, source_target_pairs={{24,16},{25,17},{26,18},{27,19},{28,20},{29,21},{30,22},{31,23}} | collective-permute-start | bytes 983048 | tf_op jit(solution)/shard_map/ppermute | solution.py:603
  837.3 59.1 %collective-permute-start.53 = (bf16[640,1024]{1,0:T(8,128)(2,1)}, bf16[640,1024]{1,0:T(8,128)(2,1)}, u32[]{:S(2)}, u32[]{:S(2)}) collective-permute-start(bf16[640,1024]{1,0:T(8,128)(2,1)} %collective-permute-done.49), channel_id=1, source_target_pairs={{8,16},{16,24},{9,17},{17,25},{10,18},{18,26},{11,19},{19,27},{12,... | collective-permute-start | bytes 3932168 | tf_op jit(solution)/shard_map/ppermute | solution.py:602
  839.1 57.4 %collective-permute-start.54 = (bf16[640,1024]{1,0:T(8,128)(2,1)}, bf16[640,1024]{1,0:T(8,128)(2,1)S(1)}, u32[]{:S(2)}, u32[]{:S(2)}) collective-permute-start(bf16[640,1024]{1,0:T(8,128)(2,1)} %collective-permute-done.50), channel_id=1, source_target_pairs={{16,8},{8,0},{17,9},{9,1},{18,10},{10,2},{19,11},{11,3},{20,12},{1... | collective-permute-start | bytes 3932168 | tf_op jit(solution)/shard_map/ppermute | solution.py:603
  846.1 31.6 %collective-permute-start.64 = (f32[17536]{0:T(1024)S(1)}, f32[17536]{0:T(1024)S(1)}, u32[]{:S(2)}, u32[]{:S(2)}) collective-permute-start(f32[17536]{0:T(1024)S(1)} %add.644), channel_id=1, source_target_pairs={{0,8},{8,0},{16,24},{24,16},{1,9},{9,1},{17,25},{25,17},{2,10},{10... | collective-permute-start | bytes 210440 | tf_op jit(solution)/shard_map/ppermute | solution.py:636
  883.3 13.1 %collective-permute-start.55 = (bf16[256,640]{1,0:T(8,128)(2,1)S(1)}, bf16[256,640]{1,0:T(8,128)(2,1)S(1)}, u32[]{:S(2)}, u32[]{:S(2)}) collective-permute-start(bf16[256,640]{1,0:T(8,128)(2,1)S(1)} %get-tuple-element.353), channel_id=1, source_target_pairs={{0,8},{8,16},{1,9},{9,17},{2,10},{10,18},{3,11},{11,19},{4,12},{12... | collective-permute-start | bytes 983048 | tf_op jit(solution)/shard_map/ppermute | solution.py:602
  885.2 11.2 %collective-permute-start.56 = (bf16[256,640]{1,0:T(8,128)(2,1)S(1)}, bf16[256,640]{1,0:T(8,128)(2,1)S(1)}, u32[]{:S(2)}, u32[]{:S(2)}) collective-permute-start(bf16[256,640]{1,0:T(8,128)(2,1)S(1)} %get-tuple-element.352), channel_id=1, source_target_pairs={{24,16},{16,8},{25,17},{17,9},{26,18},{18,10},{27,19},{19,11},{28,... | collective-permute-start | bytes 983048 | tf_op jit(solution)/shard_map/ppermute | solution.py:603
  896.4 17.0 %collective-permute-start.58 = (bf16[640,1024]{1,0:T(8,128)(2,1)}, bf16[640,1024]{1,0:T(8,128)(2,1)S(1)}, u32[]{:S(2)}, u32[]{:S(2)}) collective-permute-start(bf16[640,1024]{1,0:T(8,128)(2,1)} %collective-permute-done.53), channel_id=1, source_target_pairs={{16,24},{17,25},{18,26},{19,27},{20,28},{21,29},{22,30},{23,31}} | collective-permute-start | bytes 3932168 | tf_op jit(solution)/shard_map/ppermute | solution.py:602
  897.2 32.1 %collective-permute-start.59 = (bf16[640,1024]{1,0:T(8,128)(2,1)S(1)}, bf16[640,1024]{1,0:T(8,128)(2,1)S(1)}, u32[]{:S(2)}, u32[]{:S(2)}) collective-permute-start(bf16[640,1024]{1,0:T(8,128)(2,1)S(1)} %collective-permute-done.54), channel_id=1, source_target_pairs={{8,0},{9,1},{10,2},{11,3},{12,4},{13,5},{14,6},{15,7}} | collective-permute-start | bytes 3932168 | tf_op jit(solution)/shard_map/ppermute | solution.py:603
  905.9 31.2 %collective-permute-start.57 = (bf16[256,640]{1,0:T(8,128)(2,1)S(1)}, bf16[256,640]{1,0:T(8,128)(2,1)S(1)}, u32[]{:S(2)}, u32[]{:S(2)}) collective-permute-start(bf16[256,640]{1,0:T(8,128)(2,1)S(1)} %get-tuple-element.351), channel_id=1, source_target_pairs={{0,8},{8,16},{16,24},{1,9},{9,17},{17,25},{2,10},{10,18},{18,26},{... | collective-permute-start | bytes 983048 | tf_op jit(solution)/shard_map/ppermute | solution.py:602
  910.5 26.6 %collective-permute-start.66 = (bf16[256,640]{1,0:T(8,128)(2,1)S(1)}, bf16[256,640]{1,0:T(8,128)(2,1)S(1)}, u32[]{:S(2)}, u32[]{:S(2)}) collective-permute-start(bf16[256,640]{1,0:T(8,128)(2,1)S(1)} %get-tuple-element.350), channel_id=1, source_target_pairs={{24,16},{16,8},{8,0},{25,17},{17,9},{9,1},{26,18},{18,10},{10,2},{... | collective-permute-start | bytes 983048 | tf_op jit(solution)/shard_map/ppermute | solution.py:603
  972.4 30.7 %collective-permute-start.73 = (bf16[1024,640]{1,0:T(8,128)(2,1)S(1)}, bf16[1024,640]{1,0:T(8,128)(2,1)}, u32[]{:S(2)}, u32[]{:S(2)}) collective-permute-start(bf16[1024,640]{1,0:T(8,128)(2,1)S(1)} %slice.144), channel_id=1, source_target_pairs={{0,2},{1,3},{2,0},{3,1},{4,6},{5,7},{6,4},{7,5},{8,10},{9,11},{10,... | collective-permute-start | bytes 3932168 | tf_op jit(solution)/shard_map/ppermute | solution.py:545
  976.7 37.4 %collective-permute-start.75 = (bf16[256,2048]{1,0:T(8,128)(2,1)}, bf16[256,2048]{1,0:T(8,128)(2,1)S(1)}, u32[]{:S(2)}, u32[]{:S(2)}) collective-permute-start(bf16[256,2048]{1,0:T(8,128)(2,1)} %reshape.699), channel_id=1, source_target_pairs={{0,2},{1,3},{2,0},{3,1},{4,6},{5,7},{6,4},{7,5},{8,10},{9,11},{10,... | collective-permute-start | bytes 3145736 | tf_op jit(solution)/shard_map/ppermute | solution.py:545
  1006.3 22.9 %collective-permute-start.74 = (bf16[2048,640]{1,0:T(8,128)(2,1)S(1)}, bf16[2048,640]{1,0:T(8,128)(2,1)}, u32[]{:S(2)}, u32[]{:S(2)}) collective-permute-start(bf16[2048,640]{1,0:T(8,128)(2,1)S(1)} %maximum_select_fusion.1.mine_ref), channel_id=1, source_target_pairs={{0,1},{1,0},{2,3},{3,2},{4,5},{5,4},{6,7},{7,6},{8,9},{9,8},{10,11... | collective-permute-start | bytes 7864328 | tf_op jit(solution)/shard_map/ppermute | solution.py:542
  (94 other events, 1219.8 us)
Sparse Core Ops, SparseCore 0:
  508.2 102.1 all-reduce.3
  644.7 140.0 all-reduce.5

commit v3 on v2

--- a/solution.py
+++ b/solution.py
@@ -310,10 +310,10 @@
     add_to(sum_ref, jnp.concatenate(sums, 1), pl.program_id(0) == 0)
 
 
-def feed_far_kernel(steps, order, xa_ref, xb_ref, ca_ref, cb_ref, b_ref, ea_ref, eb_ref, u_ref, *rest):
+def feed_far_kernel(steps, back, order, xa_ref, xb_ref, ca_ref, cb_ref, b_ref, ea_ref, eb_ref, u_ref, *rest):
     w_refs, z_refs, v_refs = rest[:steps], rest[steps : 2 * steps], rest[2 * steps : 3 * steps]
     ga_ref, gb_ref, ha_ref, hb_ref, da_ref, db_ref, sum_ref, x_ref, c_ref, e_ref, low_ref = rest[-11:]
-    i = pl.program_id(0)
+    i = lax.rem(pl.program_id(0), steps + back)
     rows = xa_ref.shape[0]
 
     @pl.when(i == 0)
@@ -370,19 +370,22 @@
     )
 
 
-def feed_far(chunk, index, first_row, x_own, x_other, c_own, c_other, w, v, bias, near_own, near_other, w_near, kept, parity):
+def feed_far(chunk, first_row, x_own, x_other, c_own, c_other, w, v, bias, near_own, near_other, w_near, parity):
     rows, width = x_own.shape
     hid = w_near.shape[1]
     steps = len(w)
     blk = hid // steps
     out_blk = min(512, width)
     back = width // out_blk
+    per = steps + back
+    count = rows // chunk
     base = first_row // chunk
-    at = lambda i, p: (index, 0)
-    at_all = lambda i, p: (base + index, 0)
-    tile = lambda i, p: lax.rem(jnp.minimum(i, steps - 1) + p[0], steps)
-    after = lambda i: jnp.maximum(i - steps, 0)
+    at = lambda i, p: (i // per, 0)
+    at_all = lambda i, p: (base + i // per, 0)
+    tile = lambda i, p: lax.rem(jnp.minimum(lax.rem(i, per), steps - 1) + p[0], steps)
+    after = lambda i: jnp.maximum(lax.rem(i, per) - steps, 0)
     ins = [
+        (parity.reshape(1), None, None),
         (x_own, (chunk, width), at),
         (x_other, (chunk, width), at),
         (c_own, (chunk, width), at_all),
@@ -395,41 +398,26 @@
     ins += [whole(p) for p in w]
     ins += [(u, (out_blk, blk), lambda i, p: (after(i), 0)) for u in w]
     ins += [whole(p) for p in v]
-    outs = [((chunk, width), BF16, (chunk, out_blk), lambda i, p: (0, after(i)))] * 2
-    outs += [((rows, hid), BF16, (chunk, blk), lambda i, p: (index, tile(i, p)))] * 4
-    outs += [((8, hid), F32, (8, blk), lambda i, p: (0, tile(i, p)))]
-    alias = {}
-    arrays = [a for a, _, _ in ins]
-    specs = [
-        pl.BlockSpec(b, m, pipeline_mode=pl.Buffered(1)) if b == a.shape else pl.BlockSpec(b, m) for a, b, m in ins
-    ]
-    if kept is not None:
-        for place, array in enumerate(kept):
-            alias[len(arrays) + 1] = 2 + place
-            arrays.append(array)
-            specs.append(pl.BlockSpec(memory_space=pl.ANY))
-    result = pl.pallas_call(
-        functools.partial(feed_far_kernel, steps),
-        grid_spec=pltpu.PrefetchScalarGridSpec(
-            num_scalar_prefetch=1,
-            grid=(steps + back,),
-            in_specs=specs,
-            out_specs=[pl.BlockSpec(b, m) for _, _, b, m in outs],
-            scratch_shapes=[
-                pltpu.VMEM((2 * chunk, width), BF16),
-                pltpu.VMEM((2 * chunk, width), BF16),
-                pltpu.VMEM((2 * chunk, hid), BF16),
-                pltpu.VMEM((steps, 2 * chunk, blk), BF16),
-            ],
-        ),
-        out_shape=[jax.ShapeDtypeStruct(s, d) for s, d, _, _ in outs],
-        input_output_aliases=alias,
-        compiler_params=pltpu.CompilerParams(vmem_limit_bytes=56 * MIB),
-        cost_estimate=pl.CostEstimate(
-            flops=8 * 2 * chunk * width * hid, bytes_accessed=8 * width * hid + 24 * chunk * width, transcendentals=0
-        ),
-    )(parity.reshape(1), *arrays)
-    return result[:2], result[2:6], result[6]
+    outs = [((rows, width), BF16, (chunk, out_blk), lambda i, p: (i // per, after(i)))] * 2
+    outs += [((rows, hid), BF16, (chunk, blk), lambda i, p: (i // per, tile(i, p)))] * 4
+    outs += [((8 * count, hid), F32, (8, blk), lambda i, p: (i // per, tile(i, p)))]
+    result = call(
+        functools.partial(feed_far_kernel, steps, back),
+        (count * per,),
+        ins,
+        outs,
+        scratch=[
+            pltpu.VMEM((2 * chunk, width), BF16),
+            pltpu.VMEM((2 * chunk, width), BF16),
+            pltpu.VMEM((2 * chunk, hid), BF16),
+            pltpu.VMEM((steps, 2 * chunk, blk), BF16),
+        ],
+        prefetch=1,
+        vmem=56,
+        flops=rows,
+        moved=rows,
+    )
+    return result[:2], result[2:6], jnp.sum(result[6].reshape(count, 8, hid)[:, 0], 0)
 
 
 def contract_kernel(count, pieces, parity, *refs):
@@ -577,6 +565,9 @@
             self.up = self.down = self.out = None
             self.t = 0
 
+        def prepare(self):
+            self.out = jnp.zeros(((3 * n_dp - 2) * self.size,) + self.value.shape[1:], BF16)
+
         def piece(self, index):
             return lax.dynamic_slice_in_dim(self.value, jnp.clip(index, 0, last) * self.size, self.size, 0)
 
@@ -593,7 +584,8 @@
             else:
                 if t == last:
                     own = add(self.piece(dp_index), self.up, self.down)
-                    self.out = jnp.zeros(((3 * n_dp - 2) * self.size,) + own.shape[1:], BF16)
+                    if self.out is None:
+                        self.prepare()
                     self.put(own, dp_index)
                     up = down = own
                 else:
@@ -629,13 +621,13 @@
             chain.up, chain.down, *values = tie(chain.up, chain.down, *values)
         return values
 
-    def small_sum(value):
-        for axis, size in (("rows", n_rows), ("dp", n_dp)):
-            hop = 1
-            while hop < size:
-                value = value + lax.ppermute(value, axis, [(i, i ^ hop) for i in range(size)])
-                hop *= 2
-        return value
+    hops = [(axis, size, 1 << k) for axis, size in (("rows", n_rows), ("dp", n_dp)) for k in range(size.bit_length() - 1)]
+
+    def hop_sum(value):
+        if not hops:
+            return value
+        axis, size, hop = hops.pop(0)
+        return value + lax.ppermute(value, axis, [(i, i ^ hop) for i in range(size)])
 
     keep_at, send_at = core * cols, (1 - core) * cols
     query_keep = lax.dynamic_slice_in_dim(query_weight, keep_at, cols, 1)
@@ -838,41 +830,31 @@
         ))
         for j in range(halves)
     ]
-    far_parts, far_sums, grads, sums_own = [], [], [], []
+    far_parts, far_sums, grads = [], [], []
+    far_bias = line(expand_bias_far)
+    far_bias, near_parts[1][0] = tie(far_bias, near_parts[1][0])
     for j in range(halves):
-        kept = None
-        for k in range(sub):
-            far_bias = line(expand_bias_far)
-            if sums_own:
-                far_bias, sums_own[-1] = tie(far_bias, sums_own[-1])
-            if len(grads) >= 3:
-                far_bias, *grads[-3] = tie(far_bias, *grads[-3])
-            (g_own, g_near), kept, bias_sum = feed_far(
-                chunk,
-                k,
-                j * part_rows,
-                seconds[j],
-                others[j],
-                cotangent,
-                cot_near,
-                expand_far,
-                contract_far,
-                far_bias,
-                near_parts[j][2],
-                near_parts[j][3],
-                expand_weight,
-                kept,
-                parity,
-            )
-            far_sums.append(bias_sum[0])
-            sums_own.append(add(g_own, near(g_near)))
-            grads.append(None)
-            for m in range(len(grads)):
-                if grads[m] is None and m < len(sums_own) - 1:
-                    grads[m] = list(heads_sum(sums_own[m]))
+        (g_own, g_near), kept, bias_sum = feed_far(
+            chunk,
+            j * part_rows,
+            seconds[j],
+            others[j],
+            cotangent,
+            cot_near,
+            expand_far,
+            contract_far,
+            far_bias,
+            near_parts[j][2],
+            near_parts[j][3],
+            expand_weight,
+            parity,
+        )
+        far_sums.append(bias_sum)
         far_parts.append(list(kept))
-
-    grads[-1] = list(heads_sum(sums_own[-1]))
+        g_sum = add(g_own, near(g_near))
+        if j == 0:
+            far_bias, g_sum = tie(far_bias, g_sum)
+        grads.append(list(heads_sum(g_sum)))
 
     hblk = min(512, hid)
     n_blk = hid // hblk
@@ -885,8 +867,8 @@
             (count,),
             lefts + rights,
             [((count * hblk, width), BF16, (hblk, width), down)],
-            flops=4 * 2 * rows * width * hblk * count,
-            moved=8 * width * rows,
+            flops=rows,
+            moved=rows,
             vmem=56,
         )[0]
 
@@ -898,16 +880,18 @@
             (count,),
             lefts + rights,
             [((count * hblk, hid), BF16, (hblk, hid), down)],
-            flops=4 * 2 * rows * hblk * hid * count,
-            moved=8 * width * rows,
+            flops=rows,
+            moved=rows,
             vmem=56,
         )[0]
 
-    far_parts[1][3], *grads[1] = tie(far_parts[1][3], *grads[1])
     contract_send = contract_grad(far_parts, 0, n_blk)
     contract_moved = far(contract_send)
+    far_parts[1][3], *grads[0] = tie(far_parts[1][3], *grads[0])
     expand_send = expand_grad(far_parts, 0, width // hblk)
-    near_parts[1][3], expand_send, *grads[2] = tie(near_parts[1][3], expand_send, *grads[2])
+    near_parts[1][0], contract_send, expand_send = tie(near_parts[1][0], contract_send, expand_send)
+    near_parts[1][3], *grads[1] = tie(near_parts[1][3], *grads[1])
+    query_late, *grads[1] = tie(query_keep, *grads[1])
     contract_own = contract_grad(near_parts, 0, n_blk)
     expand_own = expand_grad(near_parts, 0, width // hblk)
     bias_near = near_parts[0][4][0] + near_parts[1][4][0]
@@ -918,10 +902,10 @@
 
     gms, lows, keeps, sends, sums = [], [], [], [], []
     for j in range(halves):
-        terms = grads[j * sub : (j + 1) * sub]
+        terms = grads[j : j + 1]
         at = lambda i, j=j: (j, 0)
         gm, low, keep, send, part = call(
-            functools.partial(second_back_kernel, sub),
+            functools.partial(second_back_kernel, 1),
             (1,),
             [whole(t[0]) for t in terms]
             + [whole(t[1]) for t in terms]
@@ -953,7 +937,6 @@
     mid_sums = functools.reduce(lambda u, v: u + v, sums)
 
     if n_heads == 2:
-        query_late, lows[-1] = tie(query_keep, lows[-1])
         query_other = across(query_late)
         query_all = [query_keep, query_send, query_other, near(query_other)]
     else:
@@ -1010,14 +993,9 @@
 
     own_all = jnp.concatenate([a[0] for a in attn], 1)
     other_all = jnp.concatenate([a[1] for a in attn], 1)
-    out_half = add(*chips_half(add(dot_left(own_all, grad_low), near(dot_left(other_all, grad_low)))))
+    out_sum = add(dot_left(own_all, grad_low), near(dot_left(other_all, grad_low)))
     expand_size = width // n_dp
-    out_size = out_half.shape[0] * width // hid // n_dp
-    joined = jnp.concatenate(
-        [add(expand_own, expand_moved).reshape(n_dp, expand_size, hid), out_half.reshape(n_dp, out_size, hid)], 1
-    )
-    joined = joined.reshape(-1, hid)
-
+    out_size = out_sum.shape[0] // chips * width // hid // n_dp
     def feed_output(first_input):
         count = 2 * halves
         out_cols = min(512, width)
@@ -1045,21 +1023,28 @@
     info = scalars[0]
     for n in range(calls):
         if n == 0:
-            info, contract_sum = tie(info, contract_sum)
+            info, contract_sum, out_sum = tie(info, contract_sum, out_sum)
+            out_half = add(*chips_half(out_sum))
             contract_half = contract_sum.shape[0] // 2
             contract_first = lax.psum(contract_sum[:contract_half], "dp")
         own, for_near, dkv_part = attn_backward(n, info)
         if n == 0:
             mlp_start, dkv_part = tie(near_parts[0][0], dkv_part)
             mlp_own, mlp_near = feed_output(mlp_start)
-            info, mlp_own, query_all[-2] = tie(info, mlp_own, query_all[-2])
+            info, mlp_own, query_all[-1] = tie(info, mlp_own, query_all[-1])
         if n == calls - 1:
             for_near, contract_first = tie(for_near, contract_first)
             contract_rest, contract_first = tie(contract_sum[contract_half:], contract_first)
             contract_second = lax.psum(contract_rest, "dp")
+            joined = jnp.concatenate(
+                [add(expand_own, expand_moved).reshape(n_dp, expand_size, hid), out_half.reshape(n_dp, out_size, hid)], 1
+            )
+            joined = joined.reshape(-1, hid)
             for_near, joined = tie(for_near, joined)
             expand_chain = Chain(joined)
             expand_chain.step()
+            expand_chain.prepare()
+            expand_chain.up, expand_chain.out = tie(expand_chain.up, expand_chain.out)
         other = near(for_near)
         dq_own.append(own)
         dq_other.append(other)
@@ -1112,12 +1097,6 @@
     expand_chain.step()
     expand_chain.up, input_grad, contract_second = tie(expand_chain.up, input_grad, contract_second)
     contract_weight_grad = jnp.concatenate([contract_first, contract_second]).astype(F32)
-    for k in range(3):
-        if k == 2:
-            expand_chain.up, contract_weight_grad = tie(expand_chain.up, contract_weight_grad)
-        together([expand_chain, query_chain], [])
-    joined = expand_chain.result().reshape(n_dp, -1, hid)
-    expand_weight_grad = joined[:, :expand_size].reshape(width, hid).astype(F32)
     dq_bias_keep = jnp.concatenate([jnp.sum(v.astype(F32), 0) for v in dq_own])
     dq_bias_send = jnp.concatenate([jnp.sum(v.astype(F32), 0) for v in dq_other])
     query_bias_part = ordered(core, dq_bias_keep, dq_bias_send, 0)
@@ -1128,11 +1107,28 @@
         places_of_units == jnp.bitwise_xor(row_index, 2), bias_far, 0.0
     )
     shorts = [mid_sums, first_sums[:2], query_bias_part, value_bias_part, units]
-    short_sums = small_sum(jnp.concatenate([v.reshape(-1) for v in shorts]))
+    short_sums = jnp.concatenate([v.reshape(-1) for v in shorts])
+    for k in range(3):
+        if k == 2:
+            expand_chain.up, contract_weight_grad = tie(expand_chain.up, contract_weight_grad)
+        expand_chain.up, short_sums = tie(expand_chain.up, short_sums)
+        together([expand_chain, query_chain], [])
+        short_sums = hop_sum(short_sums)
+    joined = expand_chain.result().reshape(n_dp, -1, hid)
+    expand_weight_grad = joined[:, :expand_size].reshape(width, hid).astype(F32)
     query_chain.up, expand_weight_grad, layer_output, short_sums = tie(
         query_chain.up, expand_weight_grad, layer_output, short_sums
     )
-    out_block, out_block_near = all_blocks(joined[:, expand_size:].reshape(out_half.shape))
+    query_chain.step()
+    short_sums = hop_sum(short_sums)
+    while hops:
+        short_sums = hop_sum(short_sums)
+    query_chain.up, short_sums = tie(query_chain.up, short_sums)
+    out_total = joined[:, expand_size:].reshape(out_half.shape)
+    out_block = ordered(chip, out_total, far(out_total), 0)
+    query_chain.step()
+    query_chain.up, out_block = tie(query_chain.up, out_block)
+    out_block_near = near(out_block)
     output_weight_grad = ordered(core, out_block, out_block_near, 0).astype(F32)
     query_block, query_block_near = all_blocks(query_chain.result())
     query_weight_grad, key_value_weight_grad = call(

time: 1050 us -> 1000 us (0.952)
  waiting for transfers between devices: 352 us -> 286 us
  starting transfers between devices: 118 us -> 143 us
  local copies, waits for them, and re-layouts: 78.9 us -> 65.7 us
    pallas_call x4 -> x0, Pallas kernels: 73.5 us -> none  [feed_far(): pl.pallas_call(functools.partial(feed_far_kernel, steps), grid_spec=pltpu...]
    pallas_call x19 -> x21, Pallas kernels: 291 us -> 356 us  [call(): pl.pallas_call(kernel, grid_spec=pltpu.PrefetchScalarGridSpec(num_scalar_...]
    ppermute x11, waiting for transfers between devices: 113 us -> 81.9 us  [far(): return lax.ppermute(value, 'rows', [(i, i ^ 2) for i in range(n_rows)])]
    ppermute x11, starting transfers between devices: 32.9 us -> 58.8 us  [far(): return lax.ppermute(value, 'rows', [(i, i ^ 2) for i in range(n_rows)])]
    psum x1, waiting for transfers between devices: 25.1 us -> 0.02 us  [body(): contract_first = lax.psum(contract_sum[:contract_half], 'dp')]
    ppermute x2, waiting for transfers between devices: 23.3 us -> 6.07 us  [beside(): return lax.ppermute(value, 'dp', [(i, i ^ 1) for i in range(n_dp)])]
    ppermute x12 -> x10, waiting for transfers between devices: 23.6 us -> 39.9 us  [across(): return lax.ppermute(value, 'heads', [(0, 1), (1, 0)])]
    ppermute x4, waiting for transfers between devices: 32.1 us -> 16.5 us  [hop_sum(): lax.ppermute(value, axis, [(i, i ^ hop) for i in range(size)])]
  transfers between devices with their start and end apart: 79 -> 75, of which waited for: 32 -> 29; matrix products, arithmetic and copies ran while one was open for 16% -> 16% of each run, Pallas kernels for 31% -> 27%
where the time goes in v3:
time: 1000 us; the launch traced here: 984 us
  Pallas kernels  356 us (36%)
  waiting for transfers between devices  286 us (29%)
  starting transfers between devices  143 us (14%)
  other arithmetic  102 us (10%)
  local copies, waits for them, and re-layouts  65.7 us (7%)
  matrix products  16.3 us (2%)
  between operations  15.9 us (2%)
    pallas_call x21, Pallas kernels, call(): pl.pallas_call(kernel, grid_spec=pltpu.PrefetchScalarGridSpec(num_scalar_...  356 us
    ppermute x12, waiting for transfers between devices, step(): self.up = lax.ppermute(up, 'dp', [(i, i + 1) for i in ends])  82.6 us
    ppermute x11, waiting for transfers between devices, far(): return lax.ppermute(value, 'rows', [(i, i ^ 2) for i in range(n_rows)])  81.9 us
    ppermute x11, starting transfers between devices, far(): return lax.ppermute(value, 'rows', [(i, i ^ 2) for i in range(n_rows)])  58.8 us
    ppermute x12, starting transfers between devices, step(): self.up = lax.ppermute(up, 'dp', [(i, i + 1) for i in ends])  49.8 us
    convert_element_type x15, other arithmetic, add(): functools.reduce(lambda u, v: u + v, (t.astype(F32) for t in terms))  42.6 us
    ppermute x10, waiting for transfers between devices, across(): return lax.ppermute(value, 'heads', [(0, 1), (1, 0)])  39.9 us
    ppermute x12, waiting for transfers between devices, step(): lax.ppermute(down, 'dp', [(last - i, last - i - 1) for i in ends])  28.1 us
  transfers between devices with their start and end apart: 75, of which 29 were waited for; matrix products, arithmetic and copies ran while one was open for 16% of the time, Pallas kernels for 27%

profile of v3, /device:TPU:0, one launch (start us, length us, event | category | flops | bytes accessed | tf_op | source)
XLA Modules:
  0.0 984.1 jit_solution(11310952874046333620)
XLA Ops:
  10.5 5.6 shard_map.288
  21.4 7.8 shard_map.289
  29.7 4.9 constant_dynamic-slice_fusion.11
  46.4 16.2 %shard_map.290 = (bf16[1024,256]{1,0:T(8,128)(2,1)S(1)}, bf16[1024,256]{1,0:T(8,128)(2,1)S(1)}, f32[2,2048]{1,0:T(2,128)S(1)}) custom-call(s32[5,4]{1,0:T(8,128)S(1)} %stack.5.info, bf16[1024,512]{1,0:T(8,128)(2,1)S(1)} %get-tuple-element.170.qa_ref, bf16[1024,512]{1,0:T(8,128)(2,1)} %collective-permute-done.qb_ref, bf16[4096,256]{1,0:T(8,128)(2,1)S(1)} %copy-done.1, ...), custom_call_target="tpu_custom_call" | custom-call | flops 8589934592 | bytes 2097152 | tf_op jit(solution)/shard_map/pallas_call | solution.py:41
  64.7 23.5 %collective-permute-done.7.rest_0_.rest_2_ = bf16[2048,512]{1,0:T(8,128)(2,1)} collective-permute-done((bf16[2048,512]{1,0:T(8,128)(2,1)}, bf16[2048,512]{1,0:T(8,128)(2,1)}, u32[]{:S(2)}, u32[]{:S(2)}) %collective-permute-start.7) | collective-permute-done | bytes 2097184 | tf_op jit(solution)/shard_map/ppermute | solution.py:533
  91.2 16.1 %shard_map.291 = (bf16[1024,256]{1,0:T(8,128)(2,1)S(1)}, bf16[1024,256]{1,0:T(8,128)(2,1)S(1)}, f32[2,2048]{1,0:T(2,128)S(1)}) custom-call(s32[5,4]{1,0:T(8,128)S(1)} %stack.5.info, bf16[1024,512]{1,0:T(8,128)(2,1)S(1)} %get-tuple-element.170.qa_ref, bf16[1024,512]{1,0:T(8,128)(2,1)} %collective-permute-done.qb_ref, bf16[4096,256]{1,0:T(8,128)(2,1)S(1)} %copy-done.1, ...), custom_call_target="tpu_custom_call" | custom-call | flops 8589934592 | bytes 2097152 | tf_op jit(solution)/shard_map/pallas_call | solution.py:41
  107.3 5.5 collective-permute-done.8.refs_1_
  115.3 20.6 %collective-permute-done.11.rest_4_.refs_13_ = bf16[512,2048]{1,0:T(8,128)(2,1)} collective-permute-done((bf16[512,2048]{1,0:T(8,128)(2,1)S(1)}, bf16[512,2048]{1,0:T(8,128)(2,1)}, u32[]{:S(2)}, u32[]{:S(2)}) %collective-permute-start.11) | collective-permute-done | bytes 2097184 | tf_op jit(solution)/shard_map/ppermute | solution.py:533
  141.0 12.1 %shard_map.292 = (f32[512,2048]{1,0:T(8,128)}, bf16[512,2048]{1,0:T(8,128)(2,1)}) custom-call(bf16[1024,512]{1,0:T(8,128)(2,1)} %copy-done.29, bf16[1024,512]{1,0:T(8,128)(2,1)} %copy-done.39, bf16[1024,512]{1,0:T(8,128)(2,1)} %copy-done.34, bf16[1024,512]{1,0:T(8,128)(2,1)} %copy-done.40, bf16[512,2048]{1,0:T(8,128)(2,1)} %get-tuple-element.341.refs_4_.refs_5_, ...), custom_call_target="tpu_custom_call" | custom-call | flops 4294967296 | bytes 20971520 | tf_op jit(solution)/shard_map/pallas_call | solution.py:41
  153.1 12.1 %shard_map.294 = (f32[512,2048]{1,0:T(8,128)}, bf16[512,2048]{1,0:T(8,128)(2,1)}) custom-call(bf16[1024,512]{1,0:T(8,128)(2,1)} %copy-done.29, bf16[1024,512]{1,0:T(8,128)(2,1)} %copy-done.39, bf16[1024,512]{1,0:T(8,128)(2,1)} %copy-done.34, bf16[1024,512]{1,0:T(8,128)(2,1)} %copy-done.40, bf16[512,2048]{1,0:T(8,128)(2,1)} %get-tuple-element.341.refs_4_.refs_5_, ...), custom_call_target="tpu_custom_call" | custom-call | flops 4294967296 | bytes 20971520 | tf_op jit(solution)/shard_map/pallas_call | solution.py:41
  167.3 5.6 collective-permute-start.15
  174.2 16.3 %shard_map.293 = (bf16[512,1024]{1,0:T(8,128)(2,1)}, bf16[512,1024]{1,0:T(8,128)(2,1)}, bf16[512,1024]{1,0:T(8,128)(2,1)}, bf16[512,1024]{1,0:T(8,128)(2,1)}, f32[8,1024]{1,0:T(8,128)}) custom-call(bf16[512,2048]{1,0:T(8,128)(2,1)} %get-tuple-element.194.xa_ref.refs_1_, bf16[512,2048]{1,0:T(8,128)(2,1)} %copy-done.24, bf16[1024,2048]{1,0:T(8,128)(2,1)} %refs_3_.3, ...), custom_call_target="tpu_custom_call" | custom-call | flops 8589934592 | bytes 25165824 | tf_op jit(solution)/shard_map/pallas_call | solution.py:41
  191.9 15.8 %shard_map.295 = (bf16[512,1024]{1,0:T(8,128)(2,1)}, bf16[512,1024]{1,0:T(8,128)(2,1)}, bf16[512,1024]{1,0:T(8,128)(2,1)}, bf16[512,1024]{1,0:T(8,128)(2,1)}, f32[8,1024]{1,0:T(8,128)}) custom-call(bf16[512,2048]{1,0:T(8,128)(2,1)} %get-tuple-element.198.xa_ref.refs_0_, bf16[512,2048]{1,0:T(8,128)(2,1)} %copy-done.25, bf16[1024,2048]{1,0:T(8,128)(2,1)} %refs_3_.3, ...), custom_call_target="tpu_custom_call" | custom-call | flops 8589934592 | bytes 25165824 | tf_op jit(solution)/shard_map/pallas_call | solution.py:41
  207.7 5.8 collective-permute-done.17.rest_5_.refs_14_
  214.9 32.0 %shard_map.296 = (bf16[512,2048]{1,0:T(8,128)(2,1)}, bf16[512,2048]{1,0:T(8,128)(2,1)}, bf16[512,1024]{1,0:T(8,128)(2,1)}, bf16[512,1024]{1,0:T(8,128)(2,1)}, bf...) custom-call(s32[1]{0:T(128)} %bitcast.2.order.parity, ...), custom_call_target="tpu_custom_call" | custom-call | flops 512 | bytes 512 | tf_op jit(solution)/shard_map/pallas_call | solution.py:41
  246.9 4.4 collective-permute-done.18
  253.6 32.5 %shard_map.297 = (bf16[512,2048]{1,0:T(8,128)(2,1)}, bf16[512,2048]{1,0:T(8,128)(2,1)}, bf16[512,1024]{1,0:T(8,128)(2,1)}, bf16[512,1024]{1,0:T(8,128)(2,1)}, bf...) custom-call(s32[1]{0:T(128)} %bitcast.2.order.parity, ...), custom_call_target="tpu_custom_call" | custom-call | flops 512 | bytes 512 | tf_op jit(solution)/shard_map/pallas_call | solution.py:41
  294.8 14.7 %shard_map.298 = bf16[1024,2048]{1,0:T(8,128)(2,1)} custom-call(bf16[512,1024]{1,0:T(8,128)(2,1)} %get-tuple-element.213.refs_0_.refs_4_.refs_5_, bf16[512,1024]{1,0:T(8,128)(2,1)} %get-tuple-element.214.refs_1_.refs_6_.refs_7_, bf16[512,1024]{1,0:T(8,128)(2,1)} %get-tuple-element.215.refs_2_.refs_8_.refs_9_, ...), custom_call_target="tpu_custom_call" | custom-call | flops 1024 | bytes 1024 | tf_op jit(solution)/shard_map/pallas_call | solution.py:41
  309.5 8.2 collective-permute-start.22
  321.9 13.1 %collective-permute-done.19.refs_1_ = bf16[512,2048]{1,0:T(8,128)(2,1)} collective-permute-done((bf16[512,2048]{1,0:T(8,128)(2,1)S(1)}, bf16[512,2048]{1,0:T(8,128)(2,1)}, u32[]{:S(2)}, u32[]{:S(2)}) %collective-permute-start.19) | collective-permute-done | bytes 2097184 | tf_op jit(solution)/shard_map/ppermute | solution.py:536
  335.0 13.5 %shard_map.299 = bf16[2048,1024]{1,0:T(8,128)(2,1)} custom-call(bf16[512,2048]{1,0:T(8,128)(2,1)} %get-tuple-element.198.xa_ref.refs_0_, bf16[512,2048]{1,0:T(8,128)(2,1)} %get-tuple-element.194.xa_ref.refs_1_, bf16[512,2048]{1,0:T(8,128)(2,1)} %copy-done.25, bf16[512,2048]{1,0:T(8,128)(2,1)} %copy-done.24, bf16[512,1024]{1,0:T(8,128)(2,1)} %get-tuple-element.217.refs_4_, ...), custom_call_target="tpu_custom_call" | custom-call | flops 1024 | bytes 1024 | tf_op jit(solution)/shard_map/pallas_call | solution.py:41
  348.5 14.7 %shard_map.300 = bf16[1024,2048]{1,0:T(8,128)(2,1)} custom-call(bf16[512,1024]{1,0:T(8,128)(2,1)} %get-tuple-element.247.refs_0_, bf16[512,1024]{1,0:T(8,128)(2,1)} %get-tuple-element.221.refs_1_, bf16[512,1024]{1,0:T(8,128)(2,1)} %get-tuple-element.222.refs_2_, bf16[512,1024]{1,0:T(8,128)(2,1)} %get-tuple-element.223.refs_3_, bf16[1024,2048]{1,0:T(8,128)(2,1)} %refs_3_.3, ...), custom_call_target="tpu_custom_call" | custom-call | flops 1024 | bytes 1024 | tf_op jit(solution)/shard_map/pallas_call | solution.py:41
  363.2 16.1 %collective-permute-done.21.refs_1_ = bf16[512,2048]{1,0:T(8,128)(2,1)} collective-permute-done((bf16[512,2048]{1,0:T(8,128)(2,1)}, bf16[512,2048]{1,0:T(8,128)(2,1)}, u32[]{:S(2)}, u32[]{:S(2)}) %collective-permute-start.21) | collective-permute-done | bytes 2097184 | tf_op jit(solution)/shard_map/ppermute | solution.py:536
  379.3 13.9 %shard_map.301 = bf16[2048,1024]{1,0:T(8,128)(2,1)} custom-call(bf16[512,2048]{1,0:T(8,128)(2,1)} %get-tuple-element.198.xa_ref.refs_0_, bf16[512,2048]{1,0:T(8,128)(2,1)} %get-tuple-element.194.xa_ref.refs_1_, bf16[512,2048]{1,0:T(8,128)(2,1)} %copy-done.25, bf16[512,2048]{1,0:T(8,128)(2,1)} %copy-done.24, ...), custom_call_target="tpu_custom_call" | custom-call | flops 1024 | bytes 1024 | tf_op jit(solution)/shard_map/pallas_call | solution.py:41
  393.8 12.6 %shard_map.302 = (f32[512,2048]{1,0:T(8,128)}, bf16[512,2048]{1,0:T(8,128)(2,1)}, bf16[512,512]{1,0:T(8,128)(2,1)}, bf16[512,512]{1,0:T(8,128)(2,1)}, f32[8,2048]{1,0:T(8,128)}) custom-call(bf16[512,2048]{1,0:T(8,128)(2,1)} %copy-done.32, bf16[512,2048]{1,0:T(8,128)(2,1)} %collective-permute-done.19.refs_1_, f32[512,2048]{1,0:T(8,128)} %get-tuple-element.232.refs_2_, ...), custom_call_target="tpu_custom_call" | custom-call | flops 2147483648 | bytes 20971520 | tf_op jit(solution)/shard_map/pallas_call | solution.py:41
  406.5 12.8 %shard_map.303 = (f32[512,2048]{1,0:T(8,128)}, bf16[512,2048]{1,0:T(8,128)(2,1)}, bf16[512,512]{1,0:T(8,128)(2,1)}, bf16[512,512]{1,0:T(8,128)(2,1)}, f32[8,2048]{1,0:T(8,128)}) custom-call(bf16[512,2048]{1,0:T(8,128)(2,1)} %add_convert_fusion.5.refs_0_, bf16[512,2048]{1,0:T(8,128)(2,1)} %collective-permute-done.21.refs_1_, ...), custom_call_target="tpu_custom_call" | custom-call | flops 2147483648 | bytes 20971520 | tf_op jit(solution)/shard_map/pallas_call | solution.py:41
  430.9 8.2 collective-permute-start.29
  440.5 4.5 add_convert_fusion.2
  449.4 26.2 %shard_map.304 = (bf16[1024,256]{1,0:T(8,128)(2,1)S(1)}, bf16[1024,256]{1,0:T(8,128)(2,1)}, f32[4096,256]{1,0:T(8,128)}) custom-call(s32[5,8]{1,0:T(8,128)S(1)} %stack.4.info, bf16[1024,512]{1,0:T(8,128)(2,1)S(1)} %get-tuple-element.170.qa_ref, bf16[1024,512]{1,0:T(8,128)(2,1)} %collective-permute-done.qb_ref, ...), custom_call_target="tpu_custom_call" | custom-call | flops 2097152 | bytes 1024 | tf_op jit(solution)/shard_map/pallas_call | solution.py:41
  478.8 23.8 %shard_map.305 = (bf16[1024,2048]{1,0:T(8,128)(2,1)}, bf16[1024,2048]{1,0:T(8,128)(2,1)}) custom-call(s32[1]{0:T(128)} %bitcast.2.order.parity, bf16[512,1024]{1,0:T(8,128)(2,1)} %get-tuple-element.247.refs_0_, bf16[512,1024]{1,0:T(8,128)(2,1)} %get-tuple-element.221.refs_1_, bf16[512,1024]{1,0:T(8,128)(2,1)} %get-tuple-element.222.refs_2_, ...), custom_call_target="tpu_custom_call" | custom-call | flops 1024 | bytes 1024 | tf_op jit(solution)/shard_map/pallas_call | solution.py:41
  504.7 26.1 %shard_map.306 = (bf16[1024,256]{1,0:T(8,128)(2,1)S(1)}, bf16[1024,256]{1,0:T(8,128)(2,1)S(1)}, f32[4096,256]{1,0:T(8,128)}) custom-call(s32[5,8]{1,0:T(8,128)S(1)} %stack.4.info, bf16[1024,512]{1,0:T(8,128)(2,1)S(1)} %get-tuple-element.170.qa_ref, bf16[1024,512]{1,0:T(8,128)(2,1)} %collective-permute-done.qb_ref, ...), custom_call_target="tpu_custom_call" | custom-call | flops 2097152 | bytes 1024 | tf_op jit(solution)/shard_map/pallas_call | solution.py:41
  536.8 27.9 %collective-permute-start.30 = (bf16[256,2048]{1,0:T(8,128)(2,1)S(1)}, bf16[256,2048]{1,0:T(8,128)(2,1)}, u32[]{:S(2)}, u32[]{:S(2)}) collective-permute-start(bf16[256,2048]{1,0:T(8,128)(2,1)S(1)} %constant_dynamic-slice_fusion.9), channel_id=1, source_target_pairs={{0,2},{1,3},{2,0},{3,1},{4,6},{5,7},{6,4},{7,5},{8,10},{9,11},{10,... | collective-permute-start | bytes 3145736 | tf_op jit(solution)/shard_map/ppermute | solution.py:533
  564.7 6.7 pad_maximum_fusion.refs_11_
  574.7 14.1 %collective-permute-done.30 = bf16[256,2048]{1,0:T(8,128)(2,1)} collective-permute-done((bf16[256,2048]{1,0:T(8,128)(2,1)S(1)}, bf16[256,2048]{1,0:T(8,128)(2,1)}, u32[]{:S(2)}, u32[]{:S(2)}) %collective-permute-start.30) | collective-permute-done | bytes 1048608 | tf_op jit(solution)/shard_map/ppermute | solution.py:533
  593.2 6.1 collective-permute-done.32
  602.2 5.6 add_convert_fusion.1
  616.5 6.1 convolution_convert_fusion
  624.7 27.1 %collective-permute-done.34 = bf16[640,1024]{1,0:T(8,128)(2,1)} collective-permute-done((bf16[640,1024]{1,0:T(8,128)(2,1)}, bf16[640,1024]{1,0:T(8,128)(2,1)}, u32[]{:S(2)}, u32[]{:S(2)}) %collective-permute-start.34) | collective-permute-done | bytes 1310752 | tf_op jit(solution)/shard_map/ppermute | solution.py:594
  655.6 4.5 collective-permute-start.35
  664.7 6.2 add_convert_fusion
  670.9 34.9 %collective-permute-done.35 = bf16[640,1024]{1,0:T(8,128)(2,1)S(1)} collective-permute-done((bf16[640,1024]{1,0:T(8,128)(2,1)S(1)}, bf16[640,1024]{1,0:T(8,128)(2,1)S(1)}, u32[]{:S(2)}, u32[]{:S(2)}) %collective-permute-start.35) | collective-permute-done | bytes 1310752 | tf_op jit(solution)/shard_map/ppermute | solution.py:594
  708.7 6.6 collective-permute-start.38
  721.3 25.3 %shard_map.307 = (bf16[1024,2048]{1,0:T(8,128)(2,1)}, f32[8,2048]{1,0:T(8,128)}) custom-call(bf16[1024,512]{1,0:T(8,128)(2,1)} %pad_maximum_fusion.5.refs_0_, bf16[1024,512]{1,0:T(8,128)(2,1)} %collective-permute-done.39.refs_1_, bf16[1024,512]{1,0:T(8,128)(2,1)} %copy-done.56, bf16[1024,512]{1,0:T(8,128)(2,1)} %collective-permute-done.41.refs_3_, ...), custom_call_target="tpu_custom_call" | custom-call | flops 9663676416 | bytes 41943040 | tf_op jit(solution)/shard_map/pallas_call | solution.py:41
  749.2 13.3 %all-reduce.6.cloned.1.call-done = bf16[512,2048]{1,0:T(8,128)(2,1)} async-done(((bf16[512,2048]{1,0:T(8,128)(2,1)}), bf16[512,2048]{1,0:T(8,128)(2,1)}) %all-reduce.6.cloned.1.call-update) | async-done | bytes 2097168 | tf_op jit(solution)/shard_map/psum | solution.py:1038
  767.7 8.9 collective-permute-done.43
  776.6 6.4 broadcast_in_dim.48
  783.0 4.6 constant_dynamic-update-slice_fusion.24
  787.6 4.9 collective-permute-start.46
  794.0 5.3 collective-permute-start.49
  800.7 14.7 %collective-permute-done.46 = bf16[640,1024]{1,0:T(8,128)(2,1)} collective-permute-done((bf16[640,1024]{1,0:T(8,128)(2,1)}, bf16[640,1024]{1,0:T(8,128)(2,1)}, u32[]{:S(2)}, u32[]{:S(2)}) %collective-permute-start.46) | collective-permute-done | bytes 1310752 | tf_op jit(solution)/shard_map/ppermute | solution.py:594
  823.6 9.4 collective-permute-start.54
  833.9 6.9 maximum_convert_fusion
  840.9 7.9 collective-permute-done.53
  850.9 7.2 fusion.1
  862.0 11.4 %collective-permute-start.56 = (bf16[256,640]{1,0:T(8,128)(2,1)}, bf16[256,640]{1,0:T(8,128)(2,1)}, u32[]{:S(2)}, u32[]{:S(2)}) collective-permute-start(bf16[256,640]{1,0:T(8,128)(2,1)} %get-tuple-element.343), channel_id=1, source_target_pairs={{0,8},{8,16},{16,24},{1,9},{9,17},{17,25},{2,10},{10,18},{18,26},{... | collective-permute-start | bytes 983048 | tf_op jit(solution)/shard_map/ppermute | solution.py:594
  877.6 6.2 collective-permute-done.60
  890.3 6.6 bitcast_convert_fusion
  903.6 4.8 collective-permute-start.63
  908.4 10.2 %collective-permute-done.63 = f32[17536]{0:T(1024)S(1)} collective-permute-done((f32[17536]{0:T(1024)S(1)}, f32[17536]{0:T(1024)S(1)}, u32[]{:S(2)}, u32[]{:S(2)}) %collective-permute-start.63) | collective-permute-done | bytes 70176 | tf_op jit(solution)/shard_map/ppermute | solution.py:630
  929.8 7.5 collective-permute-done.69
  937.5 17.6 %collective-permute-done.70 = bf16[1024,640]{1,0:T(8,128)(2,1)S(1)} collective-permute-done((bf16[1024,640]{1,0:T(8,128)(2,1)S(1)}, bf16[1024,640]{1,0:T(8,128)(2,1)S(1)}, u32[]{:S(2)}, u32[]{:S(2)}) %collective-permute-start.70) | collective-permute-done | bytes 1310752 | tf_op jit(solution)/shard_map/ppermute | solution.py:533
  958.7 5.4 collective-permute-done.72
  964.1 6.8 fusion.2
  970.9 6.2 shard_map.308
  (380 shorter events, 180.2 us)
Async XLA Ops:
  7.2 586.0 %all-reduce.4.cloned.1.call-start = ((), (), s32[]{:S(2)}) async-start(), calls=%async_computation | async-start | bytes 4194304 | tf_op jit(solution)/shard_map/psum | solution.py:1029
  18.4 18.3 %collective-permute-start.2 = (bf16[1024,256]{0,1:T(8,128)(2,1)S(1)}, bf16[1024,256]{0,1:T(8,128)(2,1)S(1)}, u32[]{:S(2)}, u32[]{:S(2)}) collective-permute-start(bf16[1024,256]{0,1:T(8,128)(2,1)S(1)} %copy.78), channel_id=1, source_target_pairs={{0,2},{1,3},{2,0},{3,1},{4,6},{5,7},{6,4},{7,5},{8,10},{9,11},{10,... | collective-permute-start | bytes 1572872 | tf_op jit(solution)/shard_map/ppermute | solution.py:533
  21.4 18.7 %collective-permute-start.1 = (bf16[1024,256]{0,1:T(8,128)(2,1)S(1)}, bf16[1024,256]{0,1:T(8,128)(2,1)S(1)}, u32[]{:S(2)}, u32[]{:S(2)}) collective-permute-start(bf16[1024,256]{0,1:T(8,128)(2,1)S(1)} %copy.78), channel_id=1, source_target_pairs={{0,1},{1,0},{2,3},{3,2},{4,5},{5,4},{6,7},{7,6},{8,9},{9,8},{10,11... | collective-permute-start | bytes 1572872 | tf_op jit(solution)/shard_map/ppermute | solution.py:530
  29.2 15.7 %collective-permute-start = (bf16[1024,512]{1,0:T(8,128)(2,1)}, bf16[1024,512]{1,0:T(8,128)(2,1)}, u32[]{:S(2)}, u32[]{:S(2)}) collective-permute-start(bf16[1024,512]{1,0:T(8,128)(2,1)} %get-tuple-element.171), channel_id=1, source_target_pairs={{0,1},{1,0},{2,3},{3,2},{4,5},{5,4},{6,7},{7,6},{8,9},{9,8},{10,11... | collective-permute-start | bytes 3145736 | tf_op jit(solution)/shard_map/ppermute | solution.py:530
  29.7 58.5 %collective-permute-start.5 = (bf16[1024,2048]{1,0:T(8,128)(2,1)}, bf16[1024,2048]{1,0:T(8,128)(2,1)}, u32[]{:S(2)}, u32[]{:S(2)}) collective-permute-start(bf16[1024,2048]{1,0:T(8,128)(2,1)} %refs_3_.3), channel_id=1, source_target_pairs={{0,1},{1,0},{2,3},{3,2},{4,5},{5,4},{6,7},{7,6},{8,9},{9,8},{10,11... | collective-permute-start | bytes 12582920 | tf_op jit(solution)/shard_map/ppermute | solution.py:530
  34.6 54.8 %collective-permute-start.6 = (bf16[512,2048]{1,0:T(8,128)(2,1)}, bf16[512,2048]{1,0:T(8,128)(2,1)}, u32[]{:S(2)}, u32[]{:S(2)}) collective-permute-start(bf16[512,2048]{1,0:T(8,128)(2,1)} %get-tuple-element.341.refs_4_.refs_5_), channel_id=1, source_target_pairs={{0,4},{4,0},{1,5},{5,1},{2,6},{6,2},{3,7},{7,3},{8,12},{12,8},{9,1... | collective-permute-start | bytes 6291464 | tf_op jit(solution)/shard_map/ppermute | solution.py:536
  40.1 48.2 %collective-permute-start.7 = (bf16[2048,512]{1,0:T(8,128)(2,1)}, bf16[2048,512]{1,0:T(8,128)(2,1)}, u32[]{:S(2)}, u32[]{:S(2)}) collective-permute-start(bf16[2048,512]{1,0:T(8,128)(2,1)} %constant_dynamic-slice_fusion.13), channel_id=1, source_target_pairs={{0,2},{1,3},{2,0},{3,1},{4,6},{5,7},{6,4},{7,5},{8,10},{9,11},{10,... | collective-permute-start | bytes 6291464 | tf_op jit(solution)/shard_map/ppermute | solution.py:533
  88.2 24.6 %collective-permute-start.8 = (bf16[1024,512]{1,0:T(8,128)(2,1)S(1)}, bf16[1024,512]{1,0:T(8,128)(2,1)S(1)}, u32[]{:S(2)}, u32[]{:S(2)}) collective-permute-start(bf16[1024,512]{1,0:T(8,128)(2,1)S(1)} %pad_maximum_fusion.3.refs_0_), channel_id=1, source_target_pairs={{0,4},{4,0},{1,5},{5,1},{2,6},{6,2},{3,7},{7,3},{8,12},{12,8},{9,1... | collective-permute-start | bytes 3145736 | tf_op jit(solution)/shard_map/ppermute | solution.py:536
  89.0 46.9 %collective-permute-start.11 = (bf16[512,2048]{1,0:T(8,128)(2,1)S(1)}, bf16[512,2048]{1,0:T(8,128)(2,1)}, u32[]{:S(2)}, u32[]{:S(2)}) collective-permute-start(bf16[512,2048]{1,0:T(8,128)(2,1)S(1)} %constant_dynamic-slice_fusion.12), channel_id=1, source_target_pairs={{0,2},{1,3},{2,0},{3,1},{4,6},{5,7},{6,4},{7,5},{8,10},{9,11},{10,... | collective-permute-start | bytes 6291464 | tf_op jit(solution)/shard_map/ppermute | solution.py:533
  89.3 46.9 %collective-permute-start.12 = (bf16[2048,512]{1,0:T(8,128)(2,1)}, bf16[2048,512]{1,0:T(8,128)(2,1)}, u32[]{:S(2)}, u32[]{:S(2)}) collective-permute-start(bf16[2048,512]{1,0:T(8,128)(2,1)} %collective-permute-done.7.rest_0_.rest_2_), channel_id=1, source_target_pairs={{0,8},{8,0},{16,24},{24,16},{1,9},{9,1},{17,25},{25,17},{2,10},{10... | collective-permute-start | bytes 6291464 | tf_op jit(solution)/shard_map/ppermute | solution.py:539
  91.2 48.8 %collective-permute-start.13 = (bf16[512,2048]{1,0:T(8,128)(2,1)}, bf16[512,2048]{1,0:T(8,128)(2,1)}, u32[]{:S(2)}, u32[]{:S(2)}) collective-permute-start(bf16[512,2048]{1,0:T(8,128)(2,1)} %collective-permute-done.6.refs_6_), channel_id=1, source_target_pairs={{0,1},{1,0},{2,3},{3,2},{4,5},{5,4},{6,7},{7,6},{8,9},{9,8},{10,11... | collective-permute-start | bytes 6291464 | tf_op jit(solution)/shard_map/ppermute | solution.py:530
  114.7 25.3 %collective-permute-start.10 = (bf16[1024,512]{1,0:T(8,128)(2,1)S(1)}, bf16[1024,512]{1,0:T(8,128)(2,1)S(1)}, u32[]{:S(2)}, u32[]{:S(2)}) collective-permute-start(bf16[1024,512]{1,0:T(8,128)(2,1)S(1)} %constant_dynamic-update-slice_fusion.refs_2_), channel_id=1, source_target_pairs={{0,4},{4,0},{1,5},{5,1},{2,6},{6,2},{3,7},{7,3},{8,12},{12,8},{9,1... | collective-permute-start | bytes 3145736 | tf_op jit(solution)/shard_map/ppermute | solution.py:536
  153.1 19.8 %collective-permute-start.14 = (bf16[512,2048]{1,0:T(8,128)(2,1)}, bf16[512,2048]{1,0:T(8,128)(2,1)S(1)}, u32[]{:S(2)}, u32[]{:S(2)}) collective-permute-start(bf16[512,2048]{1,0:T(8,128)(2,1)} %get-tuple-element.194.xa_ref.refs_1_), channel_id=1, source_target_pairs={{0,1},{1,0},{2,3},{3,2},{4,5},{5,4},{6,7},{7,6},{8,9},{9,8},{10,11... | collective-permute-start | bytes 6291464 | tf_op jit(solution)/shard_map/ppermute | solution.py:530
  165.2 25.2 %collective-permute-start.16 = (bf16[512,2048]{1,0:T(8,128)(2,1)}, bf16[512,2048]{1,0:T(8,128)(2,1)S(1)}, u32[]{:S(2)}, u32[]{:S(2)}) collective-permute-start(bf16[512,2048]{1,0:T(8,128)(2,1)} %get-tuple-element.198.xa_ref.refs_0_), channel_id=1, source_target_pairs={{0,1},{1,0},{2,3},{3,2},{4,5},{5,4},{6,7},{7,6},{8,9},{9,8},{10,11... | collective-permute-start | bytes 6291464 | tf_op jit(solution)/shard_map/ppermute | solution.py:530
  165.7 47.8 %collective-permute-start.17 = (bf16[512,2048]{1,0:T(8,128)(2,1)}, bf16[512,2048]{1,0:T(8,128)(2,1)S(1)}, u32[]{:S(2)}, u32[]{:S(2)}) collective-permute-start(bf16[512,2048]{1,0:T(8,128)(2,1)} %collective-permute-done.11.rest_4_.refs_13_), channel_id=1, source_target_pairs={{0,8},{8,0},{16,24},{24,16},{1,9},{9,1},{17,25},{25,17},{2,10},{10... | collective-permute-start | bytes 6291464 | tf_op jit(solution)/shard_map/ppermute | solution.py:539
  167.3 23.2 %collective-permute-start.15 = (f32[1024]{0:T(1024)S(1)}, f32[1024]{0:T(1024)S(1)}, u32[]{:S(2)}, u32[]{:S(2)}) collective-permute-start(f32[1024]{0:T(1024)S(1)} %copy-done.61), channel_id=1, source_target_pairs={{0,2},{1,3},{2,0},{3,1},{4,6},{5,7},{6,4},{7,5},{8,10},{9,11},{10,... | collective-permute-start | bytes 12296 | tf_op jit(solution)/shard_map/ppermute | solution.py:533
  286.4 48.6 %collective-permute-start.19 = (bf16[512,2048]{1,0:T(8,128)(2,1)S(1)}, bf16[512,2048]{1,0:T(8,128)(2,1)}, u32[]{:S(2)}, u32[]{:S(2)}) collective-permute-start(bf16[512,2048]{1,0:T(8,128)(2,1)S(1)} %add_convert_fusion.6.refs_0_), channel_id=1, source_target_pairs={{0,4},{4,0},{1,5},{5,1},{2,6},{6,2},{3,7},{7,3},{8,12},{12,8},{9,1... | collective-permute-start | bytes 6291464 | tf_op jit(solution)/shard_map/ppermute | solution.py:536
  294.3 85.0 %collective-permute-start.21 = (bf16[512,2048]{1,0:T(8,128)(2,1)}, bf16[512,2048]{1,0:T(8,128)(2,1)}, u32[]{:S(2)}, u32[]{:S(2)}) collective-permute-start(bf16[512,2048]{1,0:T(8,128)(2,1)} %add_convert_fusion.5.refs_0_), channel_id=1, source_target_pairs={{0,4},{4,0},{1,5},{5,1},{2,6},{6,2},{3,7},{7,3},{8,12},{12,8},{9,1... | collective-permute-start | bytes 6291464 | tf_op jit(solution)/shard_map/ppermute | solution.py:536
  309.5 121.4 %collective-permute-start.22 = (bf16[1024,2048]{1,0:T(8,128)(2,1)}, bf16[1024,2048]{1,0:T(8,128)(2,1)}, u32[]{:S(2)}, u32[]{:S(2)}) collective-permute-start(bf16[1024,2048]{1,0:T(8,128)(2,1)} %shard_map.298), channel_id=1, source_target_pairs={{0,2},{1,3},{2,0},{3,1},{4,6},{5,7},{6,4},{7,5},{8,10},{9,11},{10,... | collective-permute-start | bytes 12582920 | tf_op jit(solution)/shard_map/ppermute | solution.py:533
  393.2 47.3 %collective-permute-start.26 = (bf16[2048,512]{1,0:T(8,128)(2,1)S(1)}, bf16[2048,512]{1,0:T(8,128)(2,1)}, u32[]{:S(2)}, u32[]{:S(2)}) collective-permute-start(bf16[2048,512]{1,0:T(8,128)(2,1)S(1)} %get-tuple-element.249.refs_4_), channel_id=1, source_target_pairs={{0,4},{4,0},{1,5},{5,1},{2,6},{6,2},{3,7},{7,3},{8,12},{12,8},{9,1... | collective-permute-start | bytes 6291464 | tf_op jit(solution)/shard_map/ppermute | solution.py:536
  425.2 22.0 %collective-permute-start.23 = (bf16[512,2048]{1,0:T(8,128)(2,1)}, bf16[512,2048]{1,0:T(8,128)(2,1)S(1)}, u32[]{:S(2)}, u32[]{:S(2)}) collective-permute-start(bf16[512,2048]{1,0:T(8,128)(2,1)} %convolution_convert_fusion.2), channel_id=1, source_target_pairs={{0,1},{1,0},{2,3},{3,2},{4,5},{5,4},{6,7},{7,6},{8,9},{9,8},{10,11... | collective-permute-start | bytes 6291464 | tf_op jit(solution)/shard_map/ppermute | solution.py:530
  427.7 17.3 %collective-permute-start.24 = (bf16[512,512]{1,0:T(8,128)(2,1)}, bf16[512,512]{1,0:T(8,128)(2,1)}, u32[]{:S(2)}, u32[]{:S(2)}) collective-permute-start(bf16[512,512]{1,0:T(8,128)(2,1)} %get-tuple-element.243), channel_id=1, source_target_pairs={{0,1},{1,0},{2,3},{3,2},{4,5},{5,4},{6,7},{7,6},{8,9},{9,8},{10,11... | collective-permute-start | bytes 1572872 | tf_op jit(solution)/shard_map/ppermute | solution.py:530
  428.2 17.8 %collective-permute-start.25 = (bf16[512,512]{1,0:T(8,128)(2,1)}, bf16[512,512]{1,0:T(8,128)(2,1)}, u32[]{:S(2)}, u32[]{:S(2)}) collective-permute-start(bf16[512,512]{1,0:T(8,128)(2,1)} %get-tuple-element.244), channel_id=1, source_target_pairs={{0,1},{1,0},{2,3},{3,2},{4,5},{5,4},{6,7},{7,6},{8,9},{9,8},{10,11... | collective-permute-start | bytes 1572872 | tf_op jit(solution)/shard_map/ppermute | solution.py:530
  430.9 171.3 %collective-permute-start.29 = (bf16[2048,1024]{1,0:T(8,128)(2,1)}, bf16[2048,1024]{1,0:T(8,128)(2,1)}, u32[]{:S(2)}, u32[]{:S(2)}) collective-permute-start(bf16[2048,1024]{1,0:T(8,128)(2,1)} %shard_map.299), channel_id=1, source_target_pairs={{0,2},{1,3},{2,0},{3,1},{4,6},{5,7},{6,4},{7,5},{8,10},{9,11},{10,... | collective-permute-start | bytes 12582920 | tf_op jit(solution)/shard_map/ppermute | solution.py:533
  440.5 64.2 %collective-permute-start.27 = (bf16[2048,512]{1,0:T(8,128)(2,1)}, bf16[2048,512]{1,0:T(8,128)(2,1)}, u32[]{:S(2)}, u32[]{:S(2)}) collective-permute-start(bf16[2048,512]{1,0:T(8,128)(2,1)} %collective-permute-done.26.refs_6_), channel_id=1, source_target_pairs={{0,1},{1,0},{2,3},{3,2},{4,5},{5,4},{6,7},{7,6},{8,9},{9,8},{10,11... | collective-permute-start | bytes 6291464 | tf_op jit(solution)/shard_map/ppermute | solution.py:530
  475.6 27.0 %collective-permute-start.28 = (bf16[1024,256]{1,0:T(8,128)(2,1)}, bf16[1024,256]{1,0:T(8,128)(2,1)}, u32[]{:S(2)}, u32[]{:S(2)}) collective-permute-start(bf16[1024,256]{1,0:T(8,128)(2,1)} %get-tuple-element.252), channel_id=1, source_target_pairs={{0,1},{1,0},{2,3},{3,2},{4,5},{5,4},{6,7},{7,6},{8,9},{9,8},{10,11... | collective-permute-start | bytes 1572872 | tf_op jit(solution)/shard_map/ppermute | solution.py:530
  478.7 283.7 %all-reduce.6.cloned.1.call-start = ((), (), s32[]{:S(2)}) async-start(), calls=%async_computation.1 | async-start | bytes 4194304 | tf_op jit(solution)/shard_map/psum | solution.py:1038
  535.2 36.2 %collective-permute-start.31 = (bf16[2,1024,256]{2,1,0:T(8,128)(2,1)S(1)}, bf16[2,1024,256]{2,1,0:T(8,128)(2,1)}, u32[]{:S(2)}, u32[]{:S(2)}) collective-permute-start(bf16[2,1024,256]{2,1,0:T(8,128)(2,1)S(1)} %fusion.13), channel_id=1, source_target_pairs={{0,1},{1,0},{2,3},{3,2},{4,5},{5,4},{6,7},{7,6},{8,9},{9,8},{10,11... | collective-permute-start | bytes 3145736 | tf_op jit(solution)/shard_map/ppermute | solution.py:530
  536.8 52.0 %collective-permute-start.30 = (bf16[256,2048]{1,0:T(8,128)(2,1)S(1)}, bf16[256,2048]{1,0:T(8,128)(2,1)}, u32[]{:S(2)}, u32[]{:S(2)}) collective-permute-start(bf16[256,2048]{1,0:T(8,128)(2,1)S(1)} %constant_dynamic-slice_fusion.9), channel_id=1, source_target_pairs={{0,2},{1,3},{2,0},{3,1},{4,6},{5,7},{6,4},{7,5},{8,10},{9,11},{10,... | collective-permute-start | bytes 3145736 | tf_op jit(solution)/shard_map/ppermute | solution.py:533
  574.3 25.0 %collective-permute-start.32 = (bf16[1024,256]{1,0:T(8,128)(2,1)S(1)}, bf16[1024,256]{1,0:T(8,128)(2,1)S(1)}, u32[]{:S(2)}, u32[]{:S(2)}) collective-permute-start(bf16[1024,256]{1,0:T(8,128)(2,1)S(1)} %fusion.19), channel_id=1, source_target_pairs={{0,2},{1,3},{2,0},{3,1},{4,6},{5,7},{6,4},{7,5},{8,10},{9,11},{10,... | collective-permute-start | bytes 1572872 | tf_op jit(solution)/shard_map/ppermute | solution.py:533
  574.6 90.0 %collective-permute-start.42 = (bf16[1024,2048]{1,0:T(8,128)(2,1)}, bf16[1024,2048]{1,0:T(8,128)(2,1)}, u32[]{:S(2)}, u32[]{:S(2)}) collective-permute-start(bf16[1024,2048]{1,0:T(8,128)(2,1)} %get-tuple-element.280), channel_id=1, source_target_pairs={{0,1},{1,0},{2,3},{3,2},{4,5},{5,4},{6,7},{7,6},{8,9},{9,8},{10,11... | collective-permute-start | bytes 12582920 | tf_op jit(solution)/shard_map/ppermute | solution.py:530
  600.6 15.7 %collective-permute-start.33 = (bf16[1024,256]{1,0:T(8,128)(2,1)S(1)}, bf16[1024,256]{1,0:T(8,128)(2,1)S(1)}, u32[]{:S(2)}, u32[]{:S(2)}) collective-permute-start(bf16[1024,256]{1,0:T(8,128)(2,1)S(1)} %fusion.18), channel_id=1, source_target_pairs={{0,4},{4,0},{1,5},{5,1},{2,6},{6,2},{3,7},{7,3},{8,12},{12,8},{9,1... | collective-permute-start | bytes 1572872 | tf_op jit(solution)/shard_map/ppermute | solution.py:536
  612.1 39.7 %collective-permute-start.34 = (bf16[640,1024]{1,0:T(8,128)(2,1)}, bf16[640,1024]{1,0:T(8,128)(2,1)}, u32[]{:S(2)}, u32[]{:S(2)}) collective-permute-start(bf16[640,1024]{1,0:T(8,128)(2,1)} %get-tuple-element.335), channel_id=1, source_target_pairs={{0,8},{1,9},{2,10},{3,11},{4,12},{5,13},{6,14},{7,15}} | collective-permute-start | bytes 3932168 | tf_op jit(solution)/shard_map/ppermute | solution.py:594
  614.6 37.2 %collective-permute-start.36 = (bf16[640,1024]{1,0:T(8,128)(2,1)}, bf16[640,1024]{1,0:T(8,128)(2,1)}, u32[]{:S(2)}, u32[]{:S(2)}) collective-permute-start(bf16[640,1024]{1,0:T(8,128)(2,1)} %get-tuple-element.334), channel_id=1, source_target_pairs={{24,16},{25,17},{26,18},{27,19},{28,20},{29,21},{30,22},{31,23}} | collective-permute-start | bytes 3932168 | tf_op jit(solution)/shard_map/ppermute | solution.py:595
  622.7 92.6 %collective-permute-start.44 = (bf16[2048,640]{1,0:T(8,128)(2,1)}, bf16[2048,640]{1,0:T(8,128)(2,1)}, u32[]{:S(2)}, u32[]{:S(2)}) collective-permute-start(bf16[2048,640]{1,0:T(8,128)(2,1)} %convolution_convert_fusion), channel_id=1, source_target_pairs={{0,1},{1,0},{2,3},{3,2},{4,5},{5,4},{6,7},{7,6},{8,9},{9,8},{10,11... | collective-permute-start | bytes 7864328 | tf_op jit(solution)/shard_map/ppermute | solution.py:530
  623.9 97.4 %collective-permute-start.39 = (bf16[1024,512]{1,0:T(8,128)(2,1)}, bf16[1024,512]{1,0:T(8,128)(2,1)}, u32[]{:S(2)}, u32[]{:S(2)}) collective-permute-start(bf16[1024,512]{1,0:T(8,128)(2,1)} %pad_maximum_fusion.5.refs_0_), channel_id=1, source_target_pairs={{0,4},{4,0},{1,5},{5,1},{2,6},{6,2},{3,7},{7,3},{8,12},{12,8},{9,1... | collective-permute-start | bytes 3145736 | tf_op jit(solution)/shard_map/ppermute | solution.py:536
  655.6 50.2 %collective-permute-start.35 = (bf16[640,1024]{1,0:T(8,128)(2,1)S(1)}, bf16[640,1024]{1,0:T(8,128)(2,1)S(1)}, u32[]{:S(2)}, u32[]{:S(2)}) collective-permute-start(bf16[640,1024]{1,0:T(8,128)(2,1)S(1)} %get-tuple-element.333), channel_id=1, source_target_pairs={{0,8},{8,16},{1,9},{9,17},{2,10},{10,18},{3,11},{11,19},{4,12},{12... | collective-permute-start | bytes 3932168 | tf_op jit(solution)/shard_map/ppermute | solution.py:594
  660.0 45.7 %collective-permute-start.37 = (bf16[640,1024]{1,0:T(8,128)(2,1)S(1)}, bf16[640,1024]{1,0:T(8,128)(2,1)S(1)}, u32[]{:S(2)}, u32[]{:S(2)}) collective-permute-start(bf16[640,1024]{1,0:T(8,128)(2,1)S(1)} %get-tuple-element.332), channel_id=1, source_target_pairs={{24,16},{16,8},{25,17},{17,9},{26,18},{18,10},{27,19},{19,11},{28,... | collective-permute-start | bytes 3932168 | tf_op jit(solution)/shard_map/ppermute | solution.py:595
  664.6 56.6 %collective-permute-start.41 = (bf16[1024,512]{1,0:T(8,128)(2,1)S(1)}, bf16[1024,512]{1,0:T(8,128)(2,1)}, u32[]{:S(2)}, u32[]{:S(2)}) collective-permute-start(bf16[1024,512]{1,0:T(8,128)(2,1)S(1)} %constant_dynamic-update-slice_fusion.8.refs_2_), channel_id=1, source_target_pairs={{0,4},{4,0},{1,5},{5,1},{2,6},{6,2},{3,7},{7,3},{8,12},{12,8},{9,1... | collective-permute-start | bytes 3145736 | tf_op jit(solution)/shard_map/ppermute | solution.py:536
  708.7 56.3 %collective-permute-start.38 = (bf16[640,1024]{1,0:T(8,128)(2,1)}, bf16[640,1024]{1,0:T(8,128)(2,1)}, u32[]{:S(2)}, u32[]{:S(2)}) collective-permute-start(bf16[640,1024]{1,0:T(8,128)(2,1)} %get-tuple-element.331), channel_id=1, source_target_pairs={{0,8},{8,16},{16,24},{1,9},{9,17},{17,25},{2,10},{10,18},{18,26},{... | collective-permute-start | bytes 3932168 | tf_op jit(solution)/shard_map/ppermute | solution.py:594
  719.0 46.0 %collective-permute-start.45 = (bf16[1024,640]{1,0:T(8,128)(2,1)}, bf16[1024,640]{1,0:T(8,128)(2,1)}, u32[]{:S(2)}, u32[]{:S(2)}) collective-permute-start(bf16[1024,640]{1,0:T(8,128)(2,1)} %constant_dynamic-slice_fusion.3), channel_id=1, source_target_pairs={{0,2},{1,3},{2,0},{3,1},{4,6},{5,7},{6,4},{7,5},{8,10},{9,11},{10,... | collective-permute-start | bytes 3932168 | tf_op jit(solution)/shard_map/ppermute | solution.py:533
  746.6 30.0 %collective-permute-start.43 = (bf16[640,1024]{1,0:T(8,128)(2,1)}, bf16[640,1024]{1,0:T(8,128)(2,1)}, u32[]{:S(2)}, u32[]{:S(2)}) collective-permute-start(bf16[640,1024]{1,0:T(8,128)(2,1)} %get-tuple-element.330), channel_id=1, source_target_pairs={{24,16},{16,8},{8,0},{25,17},{17,9},{9,1},{26,18},{18,10},{10,2},{... | collective-permute-start | bytes 3932168 | tf_op jit(solution)/shard_map/ppermute | solution.py:595
  747.9 103.0 %collective-permute-start.59 = (bf16[1024,2048]{1,0:T(8,128)(2,1)}, bf16[1024,2048]{1,0:T(8,128)(2,1)}, u32[]{:S(2)}, u32[]{:S(2)}) collective-permute-start(bf16[1024,2048]{1,0:T(8,128)(2,1)} %add_convert_fusion), channel_id=1, source_target_pairs={{0,4},{4,0},{1,5},{5,1},{2,6},{6,2},{3,7},{7,3},{8,12},{12,8},{9,1... | collective-permute-start | bytes 12582920 | tf_op jit(solution)/shard_map/ppermute | solution.py:536
  787.6 27.8 %collective-permute-start.46 = (bf16[640,1024]{1,0:T(8,128)(2,1)}, bf16[640,1024]{1,0:T(8,128)(2,1)}, u32[]{:S(2)}, u32[]{:S(2)}) collective-permute-start(bf16[640,1024]{1,0:T(8,128)(2,1)} %get-tuple-element.329), channel_id=1, source_target_pairs={{0,8},{8,16},{16,24},{1,9},{9,17},{17,25},{2,10},{10,18},{18,26},{... | collective-permute-start | bytes 3932168 | tf_op jit(solution)/shard_map/ppermute | solution.py:594
  792.5 26.2 %collective-permute-start.48 = (bf16[640,1024]{1,0:T(8,128)(2,1)}, bf16[640,1024]{1,0:T(8,128)(2,1)}, u32[]{:S(2)}, u32[]{:S(2)}) collective-permute-start(bf16[640,1024]{1,0:T(8,128)(2,1)} %get-tuple-element.329), channel_id=1, source_target_pairs={{24,16},{16,8},{8,0},{25,17},{17,9},{9,1},{26,18},{18,10},{10,2},{... | collective-permute-start | bytes 3932168 | tf_op jit(solution)/shard_map/ppermute | solution.py:595
  794.0 24.8 %collective-permute-start.49 = (bf16[256,640]{1,0:T(8,128)(2,1)S(1)}, bf16[256,640]{1,0:T(8,128)(2,1)}, u32[]{:S(2)}, u32[]{:S(2)}) collective-permute-start(bf16[256,640]{1,0:T(8,128)(2,1)S(1)} %get-tuple-element.347), channel_id=1, source_target_pairs={{0,8},{1,9},{2,10},{3,11},{4,12},{5,13},{6,14},{7,15}} | collective-permute-start | bytes 983048 | tf_op jit(solution)/shard_map/ppermute | solution.py:594
  799.3 19.5 %collective-permute-start.50 = (bf16[256,640]{1,0:T(8,128)(2,1)S(1)}, bf16[256,640]{1,0:T(8,128)(2,1)}, u32[]{:S(2)}, u32[]{:S(2)}) collective-permute-start(bf16[256,640]{1,0:T(8,128)(2,1)S(1)} %get-tuple-element.346), channel_id=1, source_target_pairs={{24,16},{25,17},{26,18},{27,19},{28,20},{29,21},{30,22},{31,23}} | collective-permute-start | bytes 983048 | tf_op jit(solution)/shard_map/ppermute | solution.py:595
  818.8 22.1 %collective-permute-start.51 = (bf16[640,1024]{1,0:T(8,128)(2,1)}, bf16[640,1024]{1,0:T(8,128)(2,1)}, u32[]{:S(2)}, u32[]{:S(2)}) collective-permute-start(bf16[640,1024]{1,0:T(8,128)(2,1)} %collective-permute-done.46), channel_id=1, source_target_pairs={{8,16},{16,24},{9,17},{17,25},{10,18},{18,26},{11,19},{19,27},{12,... | collective-permute-start | bytes 3932168 | tf_op jit(solution)/shard_map/ppermute | solution.py:594
  820.6 28.2 %collective-permute-start.53 = (bf16[640,1024]{1,0:T(8,128)(2,1)}, bf16[640,1024]{1,0:T(8,128)(2,1)}, u32[]{:S(2)}, u32[]{:S(2)}) collective-permute-start(bf16[640,1024]{1,0:T(8,128)(2,1)} %collective-permute-done.48), channel_id=1, source_target_pairs={{16,8},{8,0},{17,9},{9,1},{18,10},{10,2},{19,11},{11,3},{20,12},{1... | collective-permute-start | bytes 3932168 | tf_op jit(solution)/shard_map/ppermute | solution.py:595
  821.9 11.1 %collective-permute-start.52 = (f32[17536]{0:T(1024)S(1)}, f32[17536]{0:T(1024)S(1)}, u32[]{:S(2)}, u32[]{:S(2)}) collective-permute-start(f32[17536]{0:T(1024)S(1)} %add.600), channel_id=1, source_target_pairs={{0,2},{1,3},{2,0},{3,1},{4,6},{5,7},{6,4},{7,5},{8,10},{9,11},{10,... | collective-permute-start | bytes 210440 | tf_op jit(solution)/shard_map/ppermute | solution.py:630
  823.6 17.3 %collective-permute-start.54 = (bf16[256,640]{1,0:T(8,128)(2,1)S(1)}, bf16[256,640]{1,0:T(8,128)(2,1)S(1)}, u32[]{:S(2)}, u32[]{:S(2)}) collective-permute-start(bf16[256,640]{1,0:T(8,128)(2,1)S(1)} %get-tuple-element.345), channel_id=1, source_target_pairs={{0,8},{8,16},{1,9},{9,17},{2,10},{10,18},{3,11},{11,19},{4,12},{12... | collective-permute-start | bytes 983048 | tf_op jit(solution)/shard_map/ppermute | solution.py:594
  848.8 35.0 %collective-permute-start.57 = (bf16[640,1024]{1,0:T(8,128)(2,1)}, bf16[640,1024]{1,0:T(8,128)(2,1)S(1)}, u32[]{:S(2)}, u32[]{:S(2)}) collective-permute-start(bf16[640,1024]{1,0:T(8,128)(2,1)} %collective-permute-done.51), channel_id=1, source_target_pairs={{16,24},{17,25},{18,26},{19,27},{20,28},{21,29},{22,30},{23,31}} | collective-permute-start | bytes 3932168 | tf_op jit(solution)/shard_map/ppermute | solution.py:594
  849.6 34.4 %collective-permute-start.58 = (bf16[640,1024]{1,0:T(8,128)(2,1)}, bf16[640,1024]{1,0:T(8,128)(2,1)S(1)}, u32[]{:S(2)}, u32[]{:S(2)}) collective-permute-start(bf16[640,1024]{1,0:T(8,128)(2,1)} %collective-permute-done.53), channel_id=1, source_target_pairs={{8,0},{9,1},{10,2},{11,3},{12,4},{13,5},{14,6},{15,7}} | collective-permute-start | bytes 3932168 | tf_op jit(solution)/shard_map/ppermute | solution.py:595
  862.0 34.9 %collective-permute-start.56 = (bf16[256,640]{1,0:T(8,128)(2,1)}, bf16[256,640]{1,0:T(8,128)(2,1)}, u32[]{:S(2)}, u32[]{:S(2)}) collective-permute-start(bf16[256,640]{1,0:T(8,128)(2,1)} %get-tuple-element.343), channel_id=1, source_target_pairs={{0,8},{8,16},{16,24},{1,9},{9,17},{17,25},{2,10},{10,18},{18,26},{... | collective-permute-start | bytes 983048 | tf_op jit(solution)/shard_map/ppermute | solution.py:594
  873.4 10.4 %collective-permute-start.60 = (f32[17536]{0:T(1024)S(1)}, f32[17536]{0:T(1024)S(1)}, u32[]{:S(2)}, u32[]{:S(2)}) collective-permute-start(f32[17536]{0:T(1024)S(1)} %add.603), channel_id=1, source_target_pairs={{0,8},{8,0},{16,24},{24,16},{1,9},{9,1},{17,25},{25,17},{2,10},{10... | collective-permute-start | bytes 210440 | tf_op jit(solution)/shard_map/ppermute | solution.py:630
  873.4 23.5 %collective-permute-start.61 = (bf16[256,640]{1,0:T(8,128)(2,1)}, bf16[256,640]{1,0:T(8,128)(2,1)}, u32[]{:S(2)}, u32[]{:S(2)}) collective-permute-start(bf16[256,640]{1,0:T(8,128)(2,1)} %get-tuple-element.342), channel_id=1, source_target_pairs={{24,16},{16,8},{8,0},{25,17},{17,9},{9,1},{26,18},{18,10},{10,2},{... | collective-permute-start | bytes 983048 | tf_op jit(solution)/shard_map/ppermute | solution.py:595
  887.7 33.7 %collective-permute-start.67 = (bf16[256,2048]{1,0:T(8,128)(2,1)S(1)}, bf16[256,2048]{1,0:T(8,128)(2,1)S(1)}, u32[]{:S(2)}, u32[]{:S(2)}) collective-permute-start(bf16[256,2048]{1,0:T(8,128)(2,1)S(1)} %reshape.699), channel_id=1, source_target_pairs={{0,2},{1,3},{2,0},{3,1},{4,6},{5,7},{6,4},{7,5},{8,10},{9,11},{10,... | collective-permute-start | bytes 3145736 | tf_op jit(solution)/shard_map/ppermute | solution.py:533
  900.8 17.8 %collective-permute-start.62 = (bf16[256,640]{1,0:T(8,128)(2,1)}, bf16[256,640]{1,0:T(8,128)(2,1)S(1)}, u32[]{:S(2)}, u32[]{:S(2)}) collective-permute-start(bf16[256,640]{1,0:T(8,128)(2,1)} %get-tuple-element.327), channel_id=1, source_target_pairs={{0,8},{8,16},{16,24},{1,9},{9,17},{17,25},{2,10},{10,18},{18,26},{... | collective-permute-start | bytes 983048 | tf_op jit(solution)/shard_map/ppermute | solution.py:594
  902.3 17.0 %collective-permute-start.64 = (bf16[256,640]{1,0:T(8,128)(2,1)}, bf16[256,640]{1,0:T(8,128)(2,1)S(1)}, u32[]{:S(2)}, u32[]{:S(2)}) collective-permute-start(bf16[256,640]{1,0:T(8,128)(2,1)} %get-tuple-element.327), channel_id=1, source_target_pairs={{24,16},{16,8},{8,0},{25,17},{17,9},{9,1},{26,18},{18,10},{10,2},{... | collective-permute-start | bytes 983048 | tf_op jit(solution)/shard_map/ppermute | solution.py:595
  903.6 15.0 %collective-permute-start.63 = (f32[17536]{0:T(1024)S(1)}, f32[17536]{0:T(1024)S(1)}, u32[]{:S(2)}, u32[]{:S(2)}) collective-permute-start(f32[17536]{0:T(1024)S(1)} %add.623), channel_id=1, source_target_pairs={{0,16},{8,24},{16,0},{24,8},{1,17},{9,25},{17,1},{25,9},{2,18},{10... | collective-permute-start | bytes 210440 | tf_op jit(solution)/shard_map/ppermute | solution.py:630
  919.3 9.0 collective-permute-start.66
  928.3 9.0 collective-permute-start.69
  937.4 17.7 %collective-permute-start.70 = (bf16[1024,640]{1,0:T(8,128)(2,1)S(1)}, bf16[1024,640]{1,0:T(8,128)(2,1)S(1)}, u32[]{:S(2)}, u32[]{:S(2)}) collective-permute-start(bf16[1024,640]{1,0:T(8,128)(2,1)S(1)} %slice.139), channel_id=1, source_target_pairs={{0,2},{1,3},{2,0},{3,1},{4,6},{5,7},{6,4},{7,5},{8,10},{9,11},{10,... | collective-permute-start | bytes 3932168 | tf_op jit(solution)/shard_map/ppermute | solution.py:533
  955.8 15.1 %collective-permute-start.71 = (bf16[2048,640]{1,0:T(8,128)(2,1)S(1)}, bf16[2048,640]{1,0:T(8,128)(2,1)}, u32[]{:S(2)}, u32[]{:S(2)}) collective-permute-start(bf16[2048,640]{1,0:T(8,128)(2,1)S(1)} %maximum_select_fusion.1.mine_ref), channel_id=1, source_target_pairs={{0,1},{1,0},{2,3},{3,2},{4,5},{5,4},{6,7},{7,6},{8,9},{9,8},{10,11... | collective-permute-start | bytes 7864328 | tf_op jit(solution)/shard_map/ppermute | solution.py:530
  (80 other events, 1121.6 us)
Sparse Core Ops, SparseCore 0:
  478.8 102.7 all-reduce.3
  624.6 137.8 all-reduce.5

commit v4 on v3

--- a/solution.py
+++ b/solution.py
@@ -1095,8 +1095,7 @@
     layer_output = (jnp.concatenate(middles) + mlp_total + contract_bias).astype(BF16)
 
     expand_chain.step()
-    expand_chain.up, input_grad, contract_second = tie(expand_chain.up, input_grad, contract_second)
-    contract_weight_grad = jnp.concatenate([contract_first, contract_second]).astype(F32)
+    expand_chain.up, input_grad = tie(expand_chain.up, input_grad)
     dq_bias_keep = jnp.concatenate([jnp.sum(v.astype(F32), 0) for v in dq_own])
     dq_bias_send = jnp.concatenate([jnp.sum(v.astype(F32), 0) for v in dq_other])
     query_bias_part = ordered(core, dq_bias_keep, dq_bias_send, 0)
@@ -1109,6 +1108,9 @@
     shorts = [mid_sums, first_sums[:2], query_bias_part, value_bias_part, units]
     short_sums = jnp.concatenate([v.reshape(-1) for v in shorts])
     for k in range(3):
+        if k == 1:
+            expand_chain.up, contract_second = tie(expand_chain.up, contract_second)
+            contract_weight_grad = jnp.concatenate([contract_first, contract_second]).astype(F32)
         if k == 2:
             expand_chain.up, contract_weight_grad = tie(expand_chain.up, contract_weight_grad)
         expand_chain.up, short_sums = tie(expand_chain.up, short_sums)

time: 1000 us -> 996 us (level)
    ppermute x12, waiting for transfers between devices: 82.6 us -> 99.2 us  [step(): self.up = lax.ppermute(up, 'dp', [(i, i + 1) for i in ends])]
    psum x1, waiting for transfers between devices: 13.3 us -> 0.02 us  [body(): contract_second = lax.psum(contract_rest, 'dp')]
    unnamed x149 -> x143, local copies, waits for them, and re-layouts: 21.3 us -> 22 us
  transfers between devices with their start and end apart: 75 -> 75, of which waited for: 29 -> 28; matrix products, arithmetic and copies ran while one was open for 16% -> 16% of each run, Pallas kernels for 27% -> 27%
where the time goes in v4:
time: 996 us; the launch traced here: 984 us
  Pallas kernels  356 us (36%)
  waiting for transfers between devices  290 us (29%)
  starting transfers between devices  138 us (14%)
  other arithmetic  100 us (10%)
  local copies, waits for them, and re-layouts  67.9 us (7%)
  matrix products  16.1 us (2%)
  between operations  15.9 us (2%)
    pallas_call x21, Pallas kernels, call(): pl.pallas_call(kernel, grid_spec=pltpu.PrefetchScalarGridSpec(num_scalar_...  356 us
    ppermute x12, waiting for transfers between devices, step(): self.up = lax.ppermute(up, 'dp', [(i, i + 1) for i in ends])  99.2 us
    ppermute x11, waiting for transfers between devices, far(): return lax.ppermute(value, 'rows', [(i, i ^ 2) for i in range(n_rows)])  81.3 us
    ppermute x11, starting transfers between devices, far(): return lax.ppermute(value, 'rows', [(i, i ^ 2) for i in range(n_rows)])  57.9 us
    ppermute x12, starting transfers between devices, step(): self.up = lax.ppermute(up, 'dp', [(i, i + 1) for i in ends])  46.4 us
    ppermute x10, waiting for transfers between devices, across(): return lax.ppermute(value, 'heads', [(0, 1), (1, 0)])  40 us
    convert_element_type x15, other arithmetic, add(): functools.reduce(lambda u, v: u + v, (t.astype(F32) for t in terms))  39.6 us
    ppermute x12, waiting for transfers between devices, step(): lax.ppermute(down, 'dp', [(last - i, last - i - 1) for i in ends])  28 us
  transfers between devices with their start and end apart: 75, of which 28 were waited for; matrix products, arithmetic and copies ran while one was open for 16% of the time, Pallas kernels for 27%

profile of v4, /device:TPU:0, one launch (start us, length us, event | category | flops | bytes accessed | tf_op | source)
XLA Modules:
  0.0 984.2 jit_solution(6625876395427583309)
XLA Ops:
  10.5 5.6 shard_map.288
  21.4 7.8 shard_map.289
  29.7 4.9 constant_dynamic-slice_fusion.11
  46.4 16.2 %shard_map.290 = (bf16[1024,256]{1,0:T(8,128)(2,1)S(1)}, bf16[1024,256]{1,0:T(8,128)(2,1)S(1)}, f32[2,2048]{1,0:T(2,128)S(1)}) custom-call(s32[5,4]{1,0:T(8,128)S(1)} %stack.5.info, bf16[1024,512]{1,0:T(8,128)(2,1)S(1)} %get-tuple-element.171.qa_ref, bf16[1024,512]{1,0:T(8,128)(2,1)} %collective-permute-done.qb_ref, bf16[4096,256]{1,0:T(8,128)(2,1)S(1)} %copy-done.1, ...), custom_call_target="tpu_custom_call" | custom-call | flops 8589934592 | bytes 2097152 | tf_op jit(solution)/shard_map/pallas_call | solution.py:41
  64.7 23.5 %collective-permute-done.7.rest_0_.rest_2_ = bf16[2048,512]{1,0:T(8,128)(2,1)} collective-permute-done((bf16[2048,512]{1,0:T(8,128)(2,1)}, bf16[2048,512]{1,0:T(8,128)(2,1)}, u32[]{:S(2)}, u32[]{:S(2)}) %collective-permute-start.7) | collective-permute-done | bytes 2097184 | tf_op jit(solution)/shard_map/ppermute | solution.py:533
  91.2 16.0 %shard_map.291 = (bf16[1024,256]{1,0:T(8,128)(2,1)S(1)}, bf16[1024,256]{1,0:T(8,128)(2,1)S(1)}, f32[2,2048]{1,0:T(2,128)S(1)}) custom-call(s32[5,4]{1,0:T(8,128)S(1)} %stack.5.info, bf16[1024,512]{1,0:T(8,128)(2,1)S(1)} %get-tuple-element.171.qa_ref, bf16[1024,512]{1,0:T(8,128)(2,1)} %collective-permute-done.qb_ref, bf16[4096,256]{1,0:T(8,128)(2,1)S(1)} %copy-done.1, ...), custom_call_target="tpu_custom_call" | custom-call | flops 8589934592 | bytes 2097152 | tf_op jit(solution)/shard_map/pallas_call | solution.py:41
  107.3 5.5 collective-permute-done.8.refs_1_
  115.3 20.6 %collective-permute-done.11.rest_4_.refs_13_ = bf16[512,2048]{1,0:T(8,128)(2,1)} collective-permute-done((bf16[512,2048]{1,0:T(8,128)(2,1)S(1)}, bf16[512,2048]{1,0:T(8,128)(2,1)}, u32[]{:S(2)}, u32[]{:S(2)}) %collective-permute-start.11) | collective-permute-done | bytes 2097184 | tf_op jit(solution)/shard_map/ppermute | solution.py:533
  141.0 12.1 %shard_map.292 = (f32[512,2048]{1,0:T(8,128)}, bf16[512,2048]{1,0:T(8,128)(2,1)}) custom-call(bf16[1024,512]{1,0:T(8,128)(2,1)} %copy-done.28, bf16[1024,512]{1,0:T(8,128)(2,1)} %copy-done.38, bf16[1024,512]{1,0:T(8,128)(2,1)} %copy-done.33, bf16[1024,512]{1,0:T(8,128)(2,1)} %copy-done.39, bf16[512,2048]{1,0:T(8,128)(2,1)} %get-tuple-element.343.refs_4_.refs_5_, ...), custom_call_target="tpu_custom_call" | custom-call | flops 4294967296 | bytes 20971520 | tf_op jit(solution)/shard_map/pallas_call | solution.py:41
  153.1 12.1 %shard_map.294 = (f32[512,2048]{1,0:T(8,128)}, bf16[512,2048]{1,0:T(8,128)(2,1)}) custom-call(bf16[1024,512]{1,0:T(8,128)(2,1)} %copy-done.28, bf16[1024,512]{1,0:T(8,128)(2,1)} %copy-done.38, bf16[1024,512]{1,0:T(8,128)(2,1)} %copy-done.33, bf16[1024,512]{1,0:T(8,128)(2,1)} %copy-done.39, bf16[512,2048]{1,0:T(8,128)(2,1)} %get-tuple-element.343.refs_4_.refs_5_, ...), custom_call_target="tpu_custom_call" | custom-call | flops 4294967296 | bytes 20971520 | tf_op jit(solution)/shard_map/pallas_call | solution.py:41
  167.3 6.0 collective-permute-start.15
  174.7 16.3 %shard_map.293 = (bf16[512,1024]{1,0:T(8,128)(2,1)}, bf16[512,1024]{1,0:T(8,128)(2,1)}, bf16[512,1024]{1,0:T(8,128)(2,1)}, bf16[512,1024]{1,0:T(8,128)(2,1)}, f32[8,1024]{1,0:T(8,128)}) custom-call(bf16[512,2048]{1,0:T(8,128)(2,1)} %get-tuple-element.195.xa_ref.refs_1_, bf16[512,2048]{1,0:T(8,128)(2,1)} %copy-done.24, bf16[1024,2048]{1,0:T(8,128)(2,1)} %refs_3_.3, ...), custom_call_target="tpu_custom_call" | custom-call | flops 8589934592 | bytes 25165824 | tf_op jit(solution)/shard_map/pallas_call | solution.py:41
  192.4 15.8 %shard_map.295 = (bf16[512,1024]{1,0:T(8,128)(2,1)}, bf16[512,1024]{1,0:T(8,128)(2,1)}, bf16[512,1024]{1,0:T(8,128)(2,1)}, bf16[512,1024]{1,0:T(8,128)(2,1)}, f32[8,1024]{1,0:T(8,128)}) custom-call(bf16[512,2048]{1,0:T(8,128)(2,1)} %get-tuple-element.199.xa_ref.refs_0_, bf16[512,2048]{1,0:T(8,128)(2,1)} %copy-done.25, bf16[1024,2048]{1,0:T(8,128)(2,1)} %refs_3_.3, ...), custom_call_target="tpu_custom_call" | custom-call | flops 8589934592 | bytes 25165824 | tf_op jit(solution)/shard_map/pallas_call | solution.py:41
  208.2 5.3 collective-permute-done.17.rest_5_.refs_14_
  214.9 32.0 %shard_map.296 = (bf16[512,2048]{1,0:T(8,128)(2,1)}, bf16[512,2048]{1,0:T(8,128)(2,1)}, bf16[512,1024]{1,0:T(8,128)(2,1)}, bf16[512,1024]{1,0:T(8,128)(2,1)}, bf...) custom-call(s32[1]{0:T(128)} %bitcast.2.order.parity, ...), custom_call_target="tpu_custom_call" | custom-call | flops 512 | bytes 512 | tf_op jit(solution)/shard_map/pallas_call | solution.py:41
  246.9 4.4 collective-permute-done.18
  253.7 32.5 %shard_map.297 = (bf16[512,2048]{1,0:T(8,128)(2,1)}, bf16[512,2048]{1,0:T(8,128)(2,1)}, bf16[512,1024]{1,0:T(8,128)(2,1)}, bf16[512,1024]{1,0:T(8,128)(2,1)}, bf...) custom-call(s32[1]{0:T(128)} %bitcast.2.order.parity, ...), custom_call_target="tpu_custom_call" | custom-call | flops 512 | bytes 512 | tf_op jit(solution)/shard_map/pallas_call | solution.py:41
  294.8 14.7 %shard_map.298 = bf16[1024,2048]{1,0:T(8,128)(2,1)} custom-call(bf16[512,1024]{1,0:T(8,128)(2,1)} %get-tuple-element.214.refs_0_.refs_4_.refs_5_, bf16[512,1024]{1,0:T(8,128)(2,1)} %get-tuple-element.215.refs_1_.refs_6_.refs_7_, bf16[512,1024]{1,0:T(8,128)(2,1)} %get-tuple-element.216.refs_2_.refs_8_.refs_9_, ...), custom_call_target="tpu_custom_call" | custom-call | flops 1024 | bytes 1024 | tf_op jit(solution)/shard_map/pallas_call | solution.py:41
  309.5 8.1 collective-permute-start.22
  321.9 13.1 %collective-permute-done.19.refs_1_ = bf16[512,2048]{1,0:T(8,128)(2,1)} collective-permute-done((bf16[512,2048]{1,0:T(8,128)(2,1)S(1)}, bf16[512,2048]{1,0:T(8,128)(2,1)}, u32[]{:S(2)}, u32[]{:S(2)}) %collective-permute-start.19) | collective-permute-done | bytes 2097184 | tf_op jit(solution)/shard_map/ppermute | solution.py:536
  335.0 13.5 %shard_map.299 = bf16[2048,1024]{1,0:T(8,128)(2,1)} custom-call(bf16[512,2048]{1,0:T(8,128)(2,1)} %get-tuple-element.199.xa_ref.refs_0_, bf16[512,2048]{1,0:T(8,128)(2,1)} %get-tuple-element.195.xa_ref.refs_1_, bf16[512,2048]{1,0:T(8,128)(2,1)} %copy-done.25, bf16[512,2048]{1,0:T(8,128)(2,1)} %copy-done.24, bf16[512,1024]{1,0:T(8,128)(2,1)} %get-tuple-element.218.refs_4_, ...), custom_call_target="tpu_custom_call" | custom-call | flops 1024 | bytes 1024 | tf_op jit(solution)/shard_map/pallas_call | solution.py:41
  348.5 14.7 %shard_map.300 = bf16[1024,2048]{1,0:T(8,128)(2,1)} custom-call(bf16[512,1024]{1,0:T(8,128)(2,1)} %get-tuple-element.248.refs_0_, bf16[512,1024]{1,0:T(8,128)(2,1)} %get-tuple-element.222.refs_1_, bf16[512,1024]{1,0:T(8,128)(2,1)} %get-tuple-element.223.refs_2_, bf16[512,1024]{1,0:T(8,128)(2,1)} %get-tuple-element.224.refs_3_, bf16[1024,2048]{1,0:T(8,128)(2,1)} %refs_3_.3, ...), custom_call_target="tpu_custom_call" | custom-call | flops 1024 | bytes 1024 | tf_op jit(solution)/shard_map/pallas_call | solution.py:41
  363.2 16.1 %collective-permute-done.21.refs_1_ = bf16[512,2048]{1,0:T(8,128)(2,1)} collective-permute-done((bf16[512,2048]{1,0:T(8,128)(2,1)}, bf16[512,2048]{1,0:T(8,128)(2,1)}, u32[]{:S(2)}, u32[]{:S(2)}) %collective-permute-start.21) | collective-permute-done | bytes 2097184 | tf_op jit(solution)/shard_map/ppermute | solution.py:536
  379.4 13.9 %shard_map.301 = bf16[2048,1024]{1,0:T(8,128)(2,1)} custom-call(bf16[512,2048]{1,0:T(8,128)(2,1)} %get-tuple-element.199.xa_ref.refs_0_, bf16[512,2048]{1,0:T(8,128)(2,1)} %get-tuple-element.195.xa_ref.refs_1_, bf16[512,2048]{1,0:T(8,128)(2,1)} %copy-done.25, bf16[512,2048]{1,0:T(8,128)(2,1)} %copy-done.24, ...), custom_call_target="tpu_custom_call" | custom-call | flops 1024 | bytes 1024 | tf_op jit(solution)/shard_map/pallas_call | solution.py:41
  393.8 12.6 %shard_map.302 = (f32[512,2048]{1,0:T(8,128)}, bf16[512,2048]{1,0:T(8,128)(2,1)}, bf16[512,512]{1,0:T(8,128)(2,1)}, bf16[512,512]{1,0:T(8,128)(2,1)}, f32[8,2048]{1,0:T(8,128)}) custom-call(bf16[512,2048]{1,0:T(8,128)(2,1)} %copy-done.31, bf16[512,2048]{1,0:T(8,128)(2,1)} %collective-permute-done.19.refs_1_, f32[512,2048]{1,0:T(8,128)} %get-tuple-element.233.refs_2_, ...), custom_call_target="tpu_custom_call" | custom-call | flops 2147483648 | bytes 20971520 | tf_op jit(solution)/shard_map/pallas_call | solution.py:41
  406.4 12.8 %shard_map.303 = (f32[512,2048]{1,0:T(8,128)}, bf16[512,2048]{1,0:T(8,128)(2,1)}, bf16[512,512]{1,0:T(8,128)(2,1)}, bf16[512,512]{1,0:T(8,128)(2,1)}, f32[8,2048]{1,0:T(8,128)}) custom-call(bf16[512,2048]{1,0:T(8,128)(2,1)} %add_convert_fusion.5.refs_0_, bf16[512,2048]{1,0:T(8,128)(2,1)} %collective-permute-done.21.refs_1_, ...), custom_call_target="tpu_custom_call" | custom-call | flops 2147483648 | bytes 20971520 | tf_op jit(solution)/shard_map/pallas_call | solution.py:41
  430.9 8.2 collective-permute-start.29
  440.5 4.5 add_convert_fusion.2
  449.4 26.2 %shard_map.304 = (bf16[1024,256]{1,0:T(8,128)(2,1)S(1)}, bf16[1024,256]{1,0:T(8,128)(2,1)}, f32[4096,256]{1,0:T(8,128)}) custom-call(s32[5,8]{1,0:T(8,128)S(1)} %stack.4.info, bf16[1024,512]{1,0:T(8,128)(2,1)S(1)} %get-tuple-element.171.qa_ref, bf16[1024,512]{1,0:T(8,128)(2,1)} %collective-permute-done.qb_ref, ...), custom_call_target="tpu_custom_call" | custom-call | flops 2097152 | bytes 1024 | tf_op jit(solution)/shard_map/pallas_call | solution.py:41
  478.8 23.7 %shard_map.305 = (bf16[1024,2048]{1,0:T(8,128)(2,1)}, bf16[1024,2048]{1,0:T(8,128)(2,1)}) custom-call(s32[1]{0:T(128)} %bitcast.2.order.parity, bf16[512,1024]{1,0:T(8,128)(2,1)} %get-tuple-element.248.refs_0_, bf16[512,1024]{1,0:T(8,128)(2,1)} %get-tuple-element.222.refs_1_, bf16[512,1024]{1,0:T(8,128)(2,1)} %get-tuple-element.223.refs_2_, ...), custom_call_target="tpu_custom_call" | custom-call | flops 1024 | bytes 1024 | tf_op jit(solution)/shard_map/pallas_call | solution.py:41
  504.6 26.1 %shard_map.306 = (bf16[1024,256]{1,0:T(8,128)(2,1)S(1)}, bf16[1024,256]{1,0:T(8,128)(2,1)S(1)}, f32[4096,256]{1,0:T(8,128)}) custom-call(s32[5,8]{1,0:T(8,128)S(1)} %stack.4.info, bf16[1024,512]{1,0:T(8,128)(2,1)S(1)} %get-tuple-element.171.qa_ref, bf16[1024,512]{1,0:T(8,128)(2,1)} %collective-permute-done.qb_ref, ...), custom_call_target="tpu_custom_call" | custom-call | flops 2097152 | bytes 1024 | tf_op jit(solution)/shard_map/pallas_call | solution.py:41
  530.7 4.3 add.563
  536.7 27.9 %collective-permute-start.30 = (bf16[256,2048]{1,0:T(8,128)(2,1)S(1)}, bf16[256,2048]{1,0:T(8,128)(2,1)}, u32[]{:S(2)}, u32[]{:S(2)}) collective-permute-start(bf16[256,2048]{1,0:T(8,128)(2,1)S(1)} %constant_dynamic-slice_fusion.9), channel_id=1, source_target_pairs={{0,2},{1,3},{2,0},{3,1},{4,6},{5,7},{6,4},{7,5},{8,10},{9,11},{10,... | collective-permute-start | bytes 3145736 | tf_op jit(solution)/shard_map/ppermute | solution.py:533
  564.7 6.7 pad_maximum_fusion.refs_11_
  574.6 14.1 %collective-permute-done.30 = bf16[256,2048]{1,0:T(8,128)(2,1)} collective-permute-done((bf16[256,2048]{1,0:T(8,128)(2,1)S(1)}, bf16[256,2048]{1,0:T(8,128)(2,1)}, u32[]{:S(2)}, u32[]{:S(2)}) %collective-permute-start.30) | collective-permute-done | bytes 1048608 | tf_op jit(solution)/shard_map/ppermute | solution.py:533
  593.2 6.1 collective-permute-done.32
  602.1 5.6 add_convert_fusion.1
  617.6 5.9 convolution_convert_fusion
  625.6 28.3 %collective-permute-done.34 = bf16[640,1024]{1,0:T(8,128)(2,1)} collective-permute-done((bf16[640,1024]{1,0:T(8,128)(2,1)}, bf16[640,1024]{1,0:T(8,128)(2,1)}, u32[]{:S(2)}, u32[]{:S(2)}) %collective-permute-start.34) | collective-permute-done | bytes 1310752 | tf_op jit(solution)/shard_map/ppermute | solution.py:594
  657.6 4.5 collective-permute-start.35
  666.8 6.1 add_convert_fusion
  672.9 35.5 %collective-permute-done.35 = bf16[640,1024]{1,0:T(8,128)(2,1)S(1)} collective-permute-done((bf16[640,1024]{1,0:T(8,128)(2,1)S(1)}, bf16[640,1024]{1,0:T(8,128)(2,1)S(1)}, u32[]{:S(2)}, u32[]{:S(2)}) %collective-permute-start.35) | collective-permute-done | bytes 1310752 | tf_op jit(solution)/shard_map/ppermute | solution.py:594
  711.3 5.5 collective-permute-start.38
  722.2 25.2 %shard_map.307 = (bf16[1024,2048]{1,0:T(8,128)(2,1)}, f32[8,2048]{1,0:T(8,128)}) custom-call(bf16[1024,512]{1,0:T(8,128)(2,1)} %pad_maximum_fusion.5.refs_0_, bf16[1024,512]{1,0:T(8,128)(2,1)} %collective-permute-done.39.refs_1_, bf16[1024,512]{1,0:T(8,128)(2,1)} %copy-done.53, bf16[1024,512]{1,0:T(8,128)(2,1)} %collective-permute-done.41.refs_3_, ...), custom_call_target="tpu_custom_call" | custom-call | flops 9663676416 | bytes 41943040 | tf_op jit(solution)/shard_map/pallas_call | solution.py:41
  750.1 15.6 %collective-permute-done.38 = bf16[640,1024]{1,0:T(8,128)(2,1)} collective-permute-done((bf16[640,1024]{1,0:T(8,128)(2,1)}, bf16[640,1024]{1,0:T(8,128)(2,1)}, u32[]{:S(2)}, u32[]{:S(2)}) %collective-permute-start.38) | collective-permute-done | bytes 1310752 | tf_op jit(solution)/shard_map/ppermute | solution.py:594
  767.4 9.3 collective-permute-done.43
  776.7 6.4 broadcast_in_dim.48
  783.1 4.5 constant_dynamic-update-slice_fusion.24
  793.7 4.6 collective-permute-start.49
  799.0 16.2 %collective-permute-done.46 = bf16[640,1024]{1,0:T(8,128)(2,1)S(1)} collective-permute-done((bf16[640,1024]{1,0:T(8,128)(2,1)}, bf16[640,1024]{1,0:T(8,128)(2,1)S(1)}, u32[]{:S(2)}, u32[]{:S(2)}) %collective-permute-start.46) | collective-permute-done | bytes 1310752 | tf_op jit(solution)/shard_map/ppermute | solution.py:594
  822.5 8.6 collective-permute-start.54
  832.1 7.5 maximum_convert_fusion
  839.7 9.0 collective-permute-done.53
  850.8 7.2 fusion.1
  859.8 10.7 %collective-permute-start.56 = (bf16[256,640]{1,0:T(8,128)(2,1)S(1)}, bf16[256,640]{1,0:T(8,128)(2,1)S(1)}, u32[]{:S(2)}, u32[]{:S(2)}) collective-permute-start(bf16[256,640]{1,0:T(8,128)(2,1)S(1)} %get-tuple-element.345), channel_id=1, source_target_pairs={{0,8},{8,16},{16,24},{1,9},{9,17},{17,25},{2,10},{10,18},{18,26},{... | collective-permute-start | bytes 983048 | tf_op jit(solution)/shard_map/ppermute | solution.py:594
  874.7 9.1 collective-permute-done.60
  890.8 6.6 bitcast_convert_fusion
  904.2 4.8 collective-permute-start.63
  909.0 9.7 collective-permute-done.63
  929.8 7.5 collective-permute-done.69
  938.2 16.9 %collective-permute-done.70 = bf16[1024,640]{1,0:T(8,128)(2,1)S(1)} collective-permute-done((bf16[1024,640]{1,0:T(8,128)(2,1)S(1)}, bf16[1024,640]{1,0:T(8,128)(2,1)S(1)}, u32[]{:S(2)}, u32[]{:S(2)}) %collective-permute-start.70) | collective-permute-done | bytes 1310752 | tf_op jit(solution)/shard_map/ppermute | solution.py:533
  958.8 5.4 collective-permute-done.72
  964.1 6.8 fusion.2
  971.0 6.2 shard_map.308
  (374 shorter events, 174.9 us)
Async XLA Ops:
  7.2 586.0 %all-reduce.4.cloned.1.call-start = ((), (), s32[]{:S(2)}) async-start(), calls=%async_computation | async-start | bytes 4194304 | tf_op jit(solution)/shard_map/psum | solution.py:1029
  18.4 18.4 %collective-permute-start.2 = (bf16[1024,256]{0,1:T(8,128)(2,1)S(1)}, bf16[1024,256]{0,1:T(8,128)(2,1)S(1)}, u32[]{:S(2)}, u32[]{:S(2)}) collective-permute-start(bf16[1024,256]{0,1:T(8,128)(2,1)S(1)} %copy.78), channel_id=1, source_target_pairs={{0,2},{1,3},{2,0},{3,1},{4,6},{5,7},{6,4},{7,5},{8,10},{9,11},{10,... | collective-permute-start | bytes 1572872 | tf_op jit(solution)/shard_map/ppermute | solution.py:533
  21.4 18.7 %collective-permute-start.1 = (bf16[1024,256]{0,1:T(8,128)(2,1)S(1)}, bf16[1024,256]{0,1:T(8,128)(2,1)S(1)}, u32[]{:S(2)}, u32[]{:S(2)}) collective-permute-start(bf16[1024,256]{0,1:T(8,128)(2,1)S(1)} %copy.78), channel_id=1, source_target_pairs={{0,1},{1,0},{2,3},{3,2},{4,5},{5,4},{6,7},{7,6},{8,9},{9,8},{10,11... | collective-permute-start | bytes 1572872 | tf_op jit(solution)/shard_map/ppermute | solution.py:530
  29.2 15.7 %collective-permute-start = (bf16[1024,512]{1,0:T(8,128)(2,1)}, bf16[1024,512]{1,0:T(8,128)(2,1)}, u32[]{:S(2)}, u32[]{:S(2)}) collective-permute-start(bf16[1024,512]{1,0:T(8,128)(2,1)} %get-tuple-element.172), channel_id=1, source_target_pairs={{0,1},{1,0},{2,3},{3,2},{4,5},{5,4},{6,7},{7,6},{8,9},{9,8},{10,11... | collective-permute-start | bytes 3145736 | tf_op jit(solution)/shard_map/ppermute | solution.py:530
  29.7 58.6 %collective-permute-start.5 = (bf16[1024,2048]{1,0:T(8,128)(2,1)}, bf16[1024,2048]{1,0:T(8,128)(2,1)}, u32[]{:S(2)}, u32[]{:S(2)}) collective-permute-start(bf16[1024,2048]{1,0:T(8,128)(2,1)} %refs_3_.3), channel_id=1, source_target_pairs={{0,1},{1,0},{2,3},{3,2},{4,5},{5,4},{6,7},{7,6},{8,9},{9,8},{10,11... | collective-permute-start | bytes 12582920 | tf_op jit(solution)/shard_map/ppermute | solution.py:530
  34.6 54.8 %collective-permute-start.6 = (bf16[512,2048]{1,0:T(8,128)(2,1)}, bf16[512,2048]{1,0:T(8,128)(2,1)}, u32[]{:S(2)}, u32[]{:S(2)}) collective-permute-start(bf16[512,2048]{1,0:T(8,128)(2,1)} %get-tuple-element.343.refs_4_.refs_5_), channel_id=1, source_target_pairs={{0,4},{4,0},{1,5},{5,1},{2,6},{6,2},{3,7},{7,3},{8,12},{12,8},{9,1... | collective-permute-start | bytes 6291464 | tf_op jit(solution)/shard_map/ppermute | solution.py:536
  40.1 48.2 %collective-permute-start.7 = (bf16[2048,512]{1,0:T(8,128)(2,1)}, bf16[2048,512]{1,0:T(8,128)(2,1)}, u32[]{:S(2)}, u32[]{:S(2)}) collective-permute-start(bf16[2048,512]{1,0:T(8,128)(2,1)} %constant_dynamic-slice_fusion.13), channel_id=1, source_target_pairs={{0,2},{1,3},{2,0},{3,1},{4,6},{5,7},{6,4},{7,5},{8,10},{9,11},{10,... | collective-permute-start | bytes 6291464 | tf_op jit(solution)/shard_map/ppermute | solution.py:533
  88.2 24.6 %collective-permute-start.8 = (bf16[1024,512]{1,0:T(8,128)(2,1)S(1)}, bf16[1024,512]{1,0:T(8,128)(2,1)S(1)}, u32[]{:S(2)}, u32[]{:S(2)}) collective-permute-start(bf16[1024,512]{1,0:T(8,128)(2,1)S(1)} %pad_maximum_fusion.3.refs_0_), channel_id=1, source_target_pairs={{0,4},{4,0},{1,5},{5,1},{2,6},{6,2},{3,7},{7,3},{8,12},{12,8},{9,1... | collective-permute-start | bytes 3145736 | tf_op jit(solution)/shard_map/ppermute | solution.py:536
  89.0 46.9 %collective-permute-start.11 = (bf16[512,2048]{1,0:T(8,128)(2,1)S(1)}, bf16[512,2048]{1,0:T(8,128)(2,1)}, u32[]{:S(2)}, u32[]{:S(2)}) collective-permute-start(bf16[512,2048]{1,0:T(8,128)(2,1)S(1)} %constant_dynamic-slice_fusion.12), channel_id=1, source_target_pairs={{0,2},{1,3},{2,0},{3,1},{4,6},{5,7},{6,4},{7,5},{8,10},{9,11},{10,... | collective-permute-start | bytes 6291464 | tf_op jit(solution)/shard_map/ppermute | solution.py:533
  89.4 46.9 %collective-permute-start.12 = (bf16[2048,512]{1,0:T(8,128)(2,1)}, bf16[2048,512]{1,0:T(8,128)(2,1)}, u32[]{:S(2)}, u32[]{:S(2)}) collective-permute-start(bf16[2048,512]{1,0:T(8,128)(2,1)} %collective-permute-done.7.rest_0_.rest_2_), channel_id=1, source_target_pairs={{0,8},{8,0},{16,24},{24,16},{1,9},{9,1},{17,25},{25,17},{2,10},{10... | collective-permute-start | bytes 6291464 | tf_op jit(solution)/shard_map/ppermute | solution.py:539
  91.2 48.8 %collective-permute-start.13 = (bf16[512,2048]{1,0:T(8,128)(2,1)}, bf16[512,2048]{1,0:T(8,128)(2,1)}, u32[]{:S(2)}, u32[]{:S(2)}) collective-permute-start(bf16[512,2048]{1,0:T(8,128)(2,1)} %collective-permute-done.6.refs_6_), channel_id=1, source_target_pairs={{0,1},{1,0},{2,3},{3,2},{4,5},{5,4},{6,7},{7,6},{8,9},{9,8},{10,11... | collective-permute-start | bytes 6291464 | tf_op jit(solution)/shard_map/ppermute | solution.py:530
  114.8 25.3 %collective-permute-start.10 = (bf16[1024,512]{1,0:T(8,128)(2,1)S(1)}, bf16[1024,512]{1,0:T(8,128)(2,1)S(1)}, u32[]{:S(2)}, u32[]{:S(2)}) collective-permute-start(bf16[1024,512]{1,0:T(8,128)(2,1)S(1)} %constant_dynamic-update-slice_fusion.refs_2_), channel_id=1, source_target_pairs={{0,4},{4,0},{1,5},{5,1},{2,6},{6,2},{3,7},{7,3},{8,12},{12,8},{9,1... | collective-permute-start | bytes 3145736 | tf_op jit(solution)/shard_map/ppermute | solution.py:536
  153.1 20.2 %collective-permute-start.14 = (bf16[512,2048]{1,0:T(8,128)(2,1)}, bf16[512,2048]{1,0:T(8,128)(2,1)S(1)}, u32[]{:S(2)}, u32[]{:S(2)}) collective-permute-start(bf16[512,2048]{1,0:T(8,128)(2,1)} %get-tuple-element.195.xa_ref.refs_1_), channel_id=1, source_target_pairs={{0,1},{1,0},{2,3},{3,2},{4,5},{5,4},{6,7},{7,6},{8,9},{9,8},{10,11... | collective-permute-start | bytes 6291464 | tf_op jit(solution)/shard_map/ppermute | solution.py:530
  165.3 25.7 %collective-permute-start.16 = (bf16[512,2048]{1,0:T(8,128)(2,1)}, bf16[512,2048]{1,0:T(8,128)(2,1)S(1)}, u32[]{:S(2)}, u32[]{:S(2)}) collective-permute-start(bf16[512,2048]{1,0:T(8,128)(2,1)} %get-tuple-element.199.xa_ref.refs_0_), channel_id=1, source_target_pairs={{0,1},{1,0},{2,3},{3,2},{4,5},{5,4},{6,7},{7,6},{8,9},{9,8},{10,11... | collective-permute-start | bytes 6291464 | tf_op jit(solution)/shard_map/ppermute | solution.py:530
  165.7 47.8 %collective-permute-start.17 = (bf16[512,2048]{1,0:T(8,128)(2,1)}, bf16[512,2048]{1,0:T(8,128)(2,1)S(1)}, u32[]{:S(2)}, u32[]{:S(2)}) collective-permute-start(bf16[512,2048]{1,0:T(8,128)(2,1)} %collective-permute-done.11.rest_4_.refs_13_), channel_id=1, source_target_pairs={{0,8},{8,0},{16,24},{24,16},{1,9},{9,1},{17,25},{25,17},{2,10},{10... | collective-permute-start | bytes 6291464 | tf_op jit(solution)/shard_map/ppermute | solution.py:539
  167.3 23.6 %collective-permute-start.15 = (f32[1024]{0:T(1024)S(1)}, f32[1024]{0:T(1024)S(1)}, u32[]{:S(2)}, u32[]{:S(2)}) collective-permute-start(f32[1024]{0:T(1024)S(1)} %copy-done.58), channel_id=1, source_target_pairs={{0,2},{1,3},{2,0},{3,1},{4,6},{5,7},{6,4},{7,5},{8,10},{9,11},{10,... | collective-permute-start | bytes 12296 | tf_op jit(solution)/shard_map/ppermute | solution.py:533
  286.4 48.6 %collective-permute-start.19 = (bf16[512,2048]{1,0:T(8,128)(2,1)S(1)}, bf16[512,2048]{1,0:T(8,128)(2,1)}, u32[]{:S(2)}, u32[]{:S(2)}) collective-permute-start(bf16[512,2048]{1,0:T(8,128)(2,1)S(1)} %add_convert_fusion.6.refs_0_), channel_id=1, source_target_pairs={{0,4},{4,0},{1,5},{5,1},{2,6},{6,2},{3,7},{7,3},{8,12},{12,8},{9,1... | collective-permute-start | bytes 6291464 | tf_op jit(solution)/shard_map/ppermute | solution.py:536
  294.3 85.0 %collective-permute-start.21 = (bf16[512,2048]{1,0:T(8,128)(2,1)}, bf16[512,2048]{1,0:T(8,128)(2,1)}, u32[]{:S(2)}, u32[]{:S(2)}) collective-permute-start(bf16[512,2048]{1,0:T(8,128)(2,1)} %add_convert_fusion.5.refs_0_), channel_id=1, source_target_pairs={{0,4},{4,0},{1,5},{5,1},{2,6},{6,2},{3,7},{7,3},{8,12},{12,8},{9,1... | collective-permute-start | bytes 6291464 | tf_op jit(solution)/shard_map/ppermute | solution.py:536
  309.5 121.4 %collective-permute-start.22 = (bf16[1024,2048]{1,0:T(8,128)(2,1)}, bf16[1024,2048]{1,0:T(8,128)(2,1)}, u32[]{:S(2)}, u32[]{:S(2)}) collective-permute-start(bf16[1024,2048]{1,0:T(8,128)(2,1)} %shard_map.298), channel_id=1, source_target_pairs={{0,2},{1,3},{2,0},{3,1},{4,6},{5,7},{6,4},{7,5},{8,10},{9,11},{10,... | collective-permute-start | bytes 12582920 | tf_op jit(solution)/shard_map/ppermute | solution.py:533
  393.3 47.3 %collective-permute-start.26 = (bf16[2048,512]{1,0:T(8,128)(2,1)S(1)}, bf16[2048,512]{1,0:T(8,128)(2,1)}, u32[]{:S(2)}, u32[]{:S(2)}) collective-permute-start(bf16[2048,512]{1,0:T(8,128)(2,1)S(1)} %get-tuple-element.250.refs_4_), channel_id=1, source_target_pairs={{0,4},{4,0},{1,5},{5,1},{2,6},{6,2},{3,7},{7,3},{8,12},{12,8},{9,1... | collective-permute-start | bytes 6291464 | tf_op jit(solution)/shard_map/ppermute | solution.py:536
  425.2 22.0 %collective-permute-start.23 = (bf16[512,2048]{1,0:T(8,128)(2,1)}, bf16[512,2048]{1,0:T(8,128)(2,1)S(1)}, u32[]{:S(2)}, u32[]{:S(2)}) collective-permute-start(bf16[512,2048]{1,0:T(8,128)(2,1)} %convolution_convert_fusion.2), channel_id=1, source_target_pairs={{0,1},{1,0},{2,3},{3,2},{4,5},{5,4},{6,7},{7,6},{8,9},{9,8},{10,11... | collective-permute-start | bytes 6291464 | tf_op jit(solution)/shard_map/ppermute | solution.py:530
  427.7 17.3 %collective-permute-start.24 = (bf16[512,512]{1,0:T(8,128)(2,1)}, bf16[512,512]{1,0:T(8,128)(2,1)}, u32[]{:S(2)}, u32[]{:S(2)}) collective-permute-start(bf16[512,512]{1,0:T(8,128)(2,1)} %get-tuple-element.244), channel_id=1, source_target_pairs={{0,1},{1,0},{2,3},{3,2},{4,5},{5,4},{6,7},{7,6},{8,9},{9,8},{10,11... | collective-permute-start | bytes 1572872 | tf_op jit(solution)/shard_map/ppermute | solution.py:530
  428.2 17.9 %collective-permute-start.25 = (bf16[512,512]{1,0:T(8,128)(2,1)}, bf16[512,512]{1,0:T(8,128)(2,1)}, u32[]{:S(2)}, u32[]{:S(2)}) collective-permute-start(bf16[512,512]{1,0:T(8,128)(2,1)} %get-tuple-element.245), channel_id=1, source_target_pairs={{0,1},{1,0},{2,3},{3,2},{4,5},{5,4},{6,7},{7,6},{8,9},{9,8},{10,11... | collective-permute-start | bytes 1572872 | tf_op jit(solution)/shard_map/ppermute | solution.py:530
  430.9 171.2 %collective-permute-start.29 = (bf16[2048,1024]{1,0:T(8,128)(2,1)}, bf16[2048,1024]{1,0:T(8,128)(2,1)}, u32[]{:S(2)}, u32[]{:S(2)}) collective-permute-start(bf16[2048,1024]{1,0:T(8,128)(2,1)} %shard_map.299), channel_id=1, source_target_pairs={{0,2},{1,3},{2,0},{3,1},{4,6},{5,7},{6,4},{7,5},{8,10},{9,11},{10,... | collective-permute-start | bytes 12582920 | tf_op jit(solution)/shard_map/ppermute | solution.py:533
  440.5 64.1 %collective-permute-start.27 = (bf16[2048,512]{1,0:T(8,128)(2,1)}, bf16[2048,512]{1,0:T(8,128)(2,1)}, u32[]{:S(2)}, u32[]{:S(2)}) collective-permute-start(bf16[2048,512]{1,0:T(8,128)(2,1)} %collective-permute-done.26.refs_6_), channel_id=1, source_target_pairs={{0,1},{1,0},{2,3},{3,2},{4,5},{5,4},{6,7},{7,6},{8,9},{9,8},{10,11... | collective-permute-start | bytes 6291464 | tf_op jit(solution)/shard_map/ppermute | solution.py:530
  475.6 26.9 %collective-permute-start.28 = (bf16[1024,256]{1,0:T(8,128)(2,1)}, bf16[1024,256]{1,0:T(8,128)(2,1)}, u32[]{:S(2)}, u32[]{:S(2)}) collective-permute-start(bf16[1024,256]{1,0:T(8,128)(2,1)} %get-tuple-element.253), channel_id=1, source_target_pairs={{0,1},{1,0},{2,3},{3,2},{4,5},{5,4},{6,7},{7,6},{8,9},{9,8},{10,11... | collective-permute-start | bytes 1572872 | tf_op jit(solution)/shard_map/ppermute | solution.py:530
  478.7 320.3 %all-reduce.6.cloned.1.call-start = ((), (), s32[]{:S(2)}) async-start(), calls=%async_computation.1 | async-start | bytes 4194304 | tf_op jit(solution)/shard_map/psum | solution.py:1038
  535.1 36.2 %collective-permute-start.31 = (bf16[2,1024,256]{2,1,0:T(8,128)(2,1)S(1)}, bf16[2,1024,256]{2,1,0:T(8,128)(2,1)}, u32[]{:S(2)}, u32[]{:S(2)}) collective-permute-start(bf16[2,1024,256]{2,1,0:T(8,128)(2,1)S(1)} %fusion.13), channel_id=1, source_target_pairs={{0,1},{1,0},{2,3},{3,2},{4,5},{5,4},{6,7},{7,6},{8,9},{9,8},{10,11... | collective-permute-start | bytes 3145736 | tf_op jit(solution)/shard_map/ppermute | solution.py:530
  536.7 52.0 %collective-permute-start.30 = (bf16[256,2048]{1,0:T(8,128)(2,1)S(1)}, bf16[256,2048]{1,0:T(8,128)(2,1)}, u32[]{:S(2)}, u32[]{:S(2)}) collective-permute-start(bf16[256,2048]{1,0:T(8,128)(2,1)S(1)} %constant_dynamic-slice_fusion.9), channel_id=1, source_target_pairs={{0,2},{1,3},{2,0},{3,1},{4,6},{5,7},{6,4},{7,5},{8,10},{9,11},{10,... | collective-permute-start | bytes 3145736 | tf_op jit(solution)/shard_map/ppermute | solution.py:533
  574.2 25.0 %collective-permute-start.32 = (bf16[1024,256]{1,0:T(8,128)(2,1)S(1)}, bf16[1024,256]{1,0:T(8,128)(2,1)S(1)}, u32[]{:S(2)}, u32[]{:S(2)}) collective-permute-start(bf16[1024,256]{1,0:T(8,128)(2,1)S(1)} %fusion.19), channel_id=1, source_target_pairs={{0,2},{1,3},{2,0},{3,1},{4,6},{5,7},{6,4},{7,5},{8,10},{9,11},{10,... | collective-permute-start | bytes 1572872 | tf_op jit(solution)/shard_map/ppermute | solution.py:533
  574.5 92.2 %collective-permute-start.42 = (bf16[1024,2048]{1,0:T(8,128)(2,1)}, bf16[1024,2048]{1,0:T(8,128)(2,1)}, u32[]{:S(2)}, u32[]{:S(2)}) collective-permute-start(bf16[1024,2048]{1,0:T(8,128)(2,1)} %get-tuple-element.279), channel_id=1, source_target_pairs={{0,1},{1,0},{2,3},{3,2},{4,5},{5,4},{6,7},{7,6},{8,9},{9,8},{10,11... | collective-permute-start | bytes 12582920 | tf_op jit(solution)/shard_map/ppermute | solution.py:530
  600.6 16.8 %collective-permute-start.33 = (bf16[1024,256]{1,0:T(8,128)(2,1)S(1)}, bf16[1024,256]{1,0:T(8,128)(2,1)S(1)}, u32[]{:S(2)}, u32[]{:S(2)}) collective-permute-start(bf16[1024,256]{1,0:T(8,128)(2,1)S(1)} %fusion.18), channel_id=1, source_target_pairs={{0,4},{4,0},{1,5},{5,1},{2,6},{6,2},{3,7},{7,3},{8,12},{12,8},{9,1... | collective-permute-start | bytes 1572872 | tf_op jit(solution)/shard_map/ppermute | solution.py:536
  612.0 41.8 %collective-permute-start.34 = (bf16[640,1024]{1,0:T(8,128)(2,1)}, bf16[640,1024]{1,0:T(8,128)(2,1)}, u32[]{:S(2)}, u32[]{:S(2)}) collective-permute-start(bf16[640,1024]{1,0:T(8,128)(2,1)} %get-tuple-element.337), channel_id=1, source_target_pairs={{0,8},{1,9},{2,10},{3,11},{4,12},{5,13},{6,14},{7,15}} | collective-permute-start | bytes 3932168 | tf_op jit(solution)/shard_map/ppermute | solution.py:594
  615.6 38.2 %collective-permute-start.36 = (bf16[640,1024]{1,0:T(8,128)(2,1)}, bf16[640,1024]{1,0:T(8,128)(2,1)}, u32[]{:S(2)}, u32[]{:S(2)}) collective-permute-start(bf16[640,1024]{1,0:T(8,128)(2,1)} %get-tuple-element.336), channel_id=1, source_target_pairs={{24,16},{25,17},{26,18},{27,19},{28,20},{29,21},{30,22},{31,23}} | collective-permute-start | bytes 3932168 | tf_op jit(solution)/shard_map/ppermute | solution.py:595
  623.5 93.3 %collective-permute-start.44 = (bf16[2048,640]{1,0:T(8,128)(2,1)}, bf16[2048,640]{1,0:T(8,128)(2,1)}, u32[]{:S(2)}, u32[]{:S(2)}) collective-permute-start(bf16[2048,640]{1,0:T(8,128)(2,1)} %convolution_convert_fusion), channel_id=1, source_target_pairs={{0,1},{1,0},{2,3},{3,2},{4,5},{5,4},{6,7},{7,6},{8,9},{9,8},{10,11... | collective-permute-start | bytes 7864328 | tf_op jit(solution)/shard_map/ppermute | solution.py:530
  624.7 97.5 %collective-permute-start.39 = (bf16[1024,512]{1,0:T(8,128)(2,1)}, bf16[1024,512]{1,0:T(8,128)(2,1)}, u32[]{:S(2)}, u32[]{:S(2)}) collective-permute-start(bf16[1024,512]{1,0:T(8,128)(2,1)} %pad_maximum_fusion.5.refs_0_), channel_id=1, source_target_pairs={{0,4},{4,0},{1,5},{5,1},{2,6},{6,2},{3,7},{7,3},{8,12},{12,8},{9,1... | collective-permute-start | bytes 3145736 | tf_op jit(solution)/shard_map/ppermute | solution.py:536
  657.6 50.8 %collective-permute-start.35 = (bf16[640,1024]{1,0:T(8,128)(2,1)S(1)}, bf16[640,1024]{1,0:T(8,128)(2,1)S(1)}, u32[]{:S(2)}, u32[]{:S(2)}) collective-permute-start(bf16[640,1024]{1,0:T(8,128)(2,1)S(1)} %get-tuple-element.335), channel_id=1, source_target_pairs={{0,8},{8,16},{1,9},{9,17},{2,10},{10,18},{3,11},{11,19},{4,12},{12... | collective-permute-start | bytes 3932168 | tf_op jit(solution)/shard_map/ppermute | solution.py:594
  662.1 46.3 %collective-permute-start.37 = (bf16[640,1024]{1,0:T(8,128)(2,1)S(1)}, bf16[640,1024]{1,0:T(8,128)(2,1)S(1)}, u32[]{:S(2)}, u32[]{:S(2)}) collective-permute-start(bf16[640,1024]{1,0:T(8,128)(2,1)S(1)} %get-tuple-element.334), channel_id=1, source_target_pairs={{24,16},{16,8},{25,17},{17,9},{26,18},{18,10},{27,19},{19,11},{28,... | collective-permute-start | bytes 3932168 | tf_op jit(solution)/shard_map/ppermute | solution.py:595
  666.7 55.5 %collective-permute-start.41 = (bf16[1024,512]{1,0:T(8,128)(2,1)S(1)}, bf16[1024,512]{1,0:T(8,128)(2,1)}, u32[]{:S(2)}, u32[]{:S(2)}) collective-permute-start(bf16[1024,512]{1,0:T(8,128)(2,1)S(1)} %constant_dynamic-update-slice_fusion.8.refs_2_), channel_id=1, source_target_pairs={{0,4},{4,0},{1,5},{5,1},{2,6},{6,2},{3,7},{7,3},{8,12},{12,8},{9,1... | collective-permute-start | bytes 3145736 | tf_op jit(solution)/shard_map/ppermute | solution.py:536
  711.3 54.4 %collective-permute-start.38 = (bf16[640,1024]{1,0:T(8,128)(2,1)}, bf16[640,1024]{1,0:T(8,128)(2,1)}, u32[]{:S(2)}, u32[]{:S(2)}) collective-permute-start(bf16[640,1024]{1,0:T(8,128)(2,1)} %get-tuple-element.333), channel_id=1, source_target_pairs={{0,8},{8,16},{16,24},{1,9},{9,17},{17,25},{2,10},{10,18},{18,26},{... | collective-permute-start | bytes 3932168 | tf_op jit(solution)/shard_map/ppermute | solution.py:594
  720.5 45.2 %collective-permute-start.45 = (bf16[1024,640]{1,0:T(8,128)(2,1)}, bf16[1024,640]{1,0:T(8,128)(2,1)}, u32[]{:S(2)}, u32[]{:S(2)}) collective-permute-start(bf16[1024,640]{1,0:T(8,128)(2,1)} %constant_dynamic-slice_fusion.3), channel_id=1, source_target_pairs={{0,2},{1,3},{2,0},{3,1},{4,6},{5,7},{6,4},{7,5},{8,10},{9,11},{10,... | collective-permute-start | bytes 3932168 | tf_op jit(solution)/shard_map/ppermute | solution.py:533
  747.5 29.2 %collective-permute-start.43 = (bf16[640,1024]{1,0:T(8,128)(2,1)}, bf16[640,1024]{1,0:T(8,128)(2,1)}, u32[]{:S(2)}, u32[]{:S(2)}) collective-permute-start(bf16[640,1024]{1,0:T(8,128)(2,1)} %get-tuple-element.332), channel_id=1, source_target_pairs={{24,16},{16,8},{8,0},{25,17},{17,9},{9,1},{26,18},{18,10},{10,2},{... | collective-permute-start | bytes 3932168 | tf_op jit(solution)/shard_map/ppermute | solution.py:595
  748.8 102.0 %collective-permute-start.59 = (bf16[1024,2048]{1,0:T(8,128)(2,1)}, bf16[1024,2048]{1,0:T(8,128)(2,1)}, u32[]{:S(2)}, u32[]{:S(2)}) collective-permute-start(bf16[1024,2048]{1,0:T(8,128)(2,1)} %add_convert_fusion), channel_id=1, source_target_pairs={{0,4},{4,0},{1,5},{5,1},{2,6},{6,2},{3,7},{7,3},{8,12},{12,8},{9,1... | collective-permute-start | bytes 12582920 | tf_op jit(solution)/shard_map/ppermute | solution.py:536
  787.6 27.6 %collective-permute-start.46 = (bf16[640,1024]{1,0:T(8,128)(2,1)}, bf16[640,1024]{1,0:T(8,128)(2,1)S(1)}, u32[]{:S(2)}, u32[]{:S(2)}) collective-permute-start(bf16[640,1024]{1,0:T(8,128)(2,1)} %get-tuple-element.331), channel_id=1, source_target_pairs={{0,8},{8,16},{16,24},{1,9},{9,17},{17,25},{2,10},{10,18},{18,26},{... | collective-permute-start | bytes 3932168 | tf_op jit(solution)/shard_map/ppermute | solution.py:594
  791.4 27.3 %collective-permute-start.48 = (bf16[640,1024]{1,0:T(8,128)(2,1)}, bf16[640,1024]{1,0:T(8,128)(2,1)}, u32[]{:S(2)}, u32[]{:S(2)}) collective-permute-start(bf16[640,1024]{1,0:T(8,128)(2,1)} %get-tuple-element.331), channel_id=1, source_target_pairs={{24,16},{16,8},{8,0},{25,17},{17,9},{9,1},{26,18},{18,10},{10,2},{... | collective-permute-start | bytes 3932168 | tf_op jit(solution)/shard_map/ppermute | solution.py:595
  793.7 25.0 %collective-permute-start.49 = (bf16[256,640]{1,0:T(8,128)(2,1)}, bf16[256,640]{1,0:T(8,128)(2,1)S(1)}, u32[]{:S(2)}, u32[]{:S(2)}) collective-permute-start(bf16[256,640]{1,0:T(8,128)(2,1)} %get-tuple-element.349), channel_id=1, source_target_pairs={{0,8},{1,9},{2,10},{3,11},{4,12},{5,13},{6,14},{7,15}} | collective-permute-start | bytes 983048 | tf_op jit(solution)/shard_map/ppermute | solution.py:594
  798.3 20.5 %collective-permute-start.50 = (bf16[256,640]{1,0:T(8,128)(2,1)}, bf16[256,640]{1,0:T(8,128)(2,1)S(1)}, u32[]{:S(2)}, u32[]{:S(2)}) collective-permute-start(bf16[256,640]{1,0:T(8,128)(2,1)} %get-tuple-element.348), channel_id=1, source_target_pairs={{24,16},{25,17},{26,18},{27,19},{28,20},{29,21},{30,22},{31,23}} | collective-permute-start | bytes 983048 | tf_op jit(solution)/shard_map/ppermute | solution.py:595
  818.7 21.0 %collective-permute-start.51 = (bf16[640,1024]{1,0:T(8,128)(2,1)S(1)}, bf16[640,1024]{1,0:T(8,128)(2,1)}, u32[]{:S(2)}, u32[]{:S(2)}) collective-permute-start(bf16[640,1024]{1,0:T(8,128)(2,1)S(1)} %collective-permute-done.46), channel_id=1, source_target_pairs={{8,16},{16,24},{9,17},{17,25},{10,18},{18,26},{11,19},{19,27},{12,... | collective-permute-start | bytes 3932168 | tf_op jit(solution)/shard_map/ppermute | solution.py:594
  820.4 28.3 %collective-permute-start.53 = (bf16[640,1024]{1,0:T(8,128)(2,1)}, bf16[640,1024]{1,0:T(8,128)(2,1)}, u32[]{:S(2)}, u32[]{:S(2)}) collective-permute-start(bf16[640,1024]{1,0:T(8,128)(2,1)} %collective-permute-done.48), channel_id=1, source_target_pairs={{16,8},{8,0},{17,9},{9,1},{18,10},{10,2},{19,11},{11,3},{20,12},{1... | collective-permute-start | bytes 3932168 | tf_op jit(solution)/shard_map/ppermute | solution.py:595
  821.7 9.4 collective-permute-start.52
  822.5 17.2 %collective-permute-start.54 = (bf16[256,640]{1,0:T(8,128)(2,1)S(1)}, bf16[256,640]{1,0:T(8,128)(2,1)S(1)}, u32[]{:S(2)}, u32[]{:S(2)}) collective-permute-start(bf16[256,640]{1,0:T(8,128)(2,1)S(1)} %get-tuple-element.347), channel_id=1, source_target_pairs={{0,8},{8,16},{1,9},{9,17},{2,10},{10,18},{3,11},{11,19},{4,12},{12... | collective-permute-start | bytes 983048 | tf_op jit(solution)/shard_map/ppermute | solution.py:594
  848.7 35.2 %collective-permute-start.57 = (bf16[640,1024]{1,0:T(8,128)(2,1)}, bf16[640,1024]{1,0:T(8,128)(2,1)S(1)}, u32[]{:S(2)}, u32[]{:S(2)}) collective-permute-start(bf16[640,1024]{1,0:T(8,128)(2,1)} %collective-permute-done.51), channel_id=1, source_target_pairs={{16,24},{17,25},{18,26},{19,27},{20,28},{21,29},{22,30},{23,31}} | collective-permute-start | bytes 3932168 | tf_op jit(solution)/shard_map/ppermute | solution.py:594
  849.4 34.6 %collective-permute-start.58 = (bf16[640,1024]{1,0:T(8,128)(2,1)}, bf16[640,1024]{1,0:T(8,128)(2,1)S(1)}, u32[]{:S(2)}, u32[]{:S(2)}) collective-permute-start(bf16[640,1024]{1,0:T(8,128)(2,1)} %collective-permute-done.53), channel_id=1, source_target_pairs={{8,0},{9,1},{10,2},{11,3},{12,4},{13,5},{14,6},{15,7}} | collective-permute-start | bytes 3932168 | tf_op jit(solution)/shard_map/ppermute | solution.py:595
  859.8 37.7 %collective-permute-start.56 = (bf16[256,640]{1,0:T(8,128)(2,1)S(1)}, bf16[256,640]{1,0:T(8,128)(2,1)S(1)}, u32[]{:S(2)}, u32[]{:S(2)}) collective-permute-start(bf16[256,640]{1,0:T(8,128)(2,1)S(1)} %get-tuple-element.345), channel_id=1, source_target_pairs={{0,8},{8,16},{16,24},{1,9},{9,17},{17,25},{2,10},{10,18},{18,26},{... | collective-permute-start | bytes 983048 | tf_op jit(solution)/shard_map/ppermute | solution.py:594
  870.4 13.4 %collective-permute-start.60 = (f32[17536]{0:T(1024)S(1)}, f32[17536]{0:T(1024)S(1)}, u32[]{:S(2)}, u32[]{:S(2)}) collective-permute-start(f32[17536]{0:T(1024)S(1)} %add.603), channel_id=1, source_target_pairs={{0,8},{8,0},{16,24},{24,16},{1,9},{9,1},{17,25},{25,17},{2,10},{10... | collective-permute-start | bytes 210440 | tf_op jit(solution)/shard_map/ppermute | solution.py:630
  870.5 27.0 %collective-permute-start.61 = (bf16[256,640]{1,0:T(8,128)(2,1)S(1)}, bf16[256,640]{1,0:T(8,128)(2,1)}, u32[]{:S(2)}, u32[]{:S(2)}) collective-permute-start(bf16[256,640]{1,0:T(8,128)(2,1)S(1)} %get-tuple-element.344), channel_id=1, source_target_pairs={{24,16},{16,8},{8,0},{25,17},{17,9},{9,1},{26,18},{18,10},{10,2},{... | collective-permute-start | bytes 983048 | tf_op jit(solution)/shard_map/ppermute | solution.py:595
  889.7 31.8 %collective-permute-start.67 = (bf16[256,2048]{1,0:T(8,128)(2,1)S(1)}, bf16[256,2048]{1,0:T(8,128)(2,1)}, u32[]{:S(2)}, u32[]{:S(2)}) collective-permute-start(bf16[256,2048]{1,0:T(8,128)(2,1)S(1)} %reshape.699), channel_id=1, source_target_pairs={{0,2},{1,3},{2,0},{3,1},{4,6},{5,7},{6,4},{7,5},{8,10},{9,11},{10,... | collective-permute-start | bytes 3145736 | tf_op jit(solution)/shard_map/ppermute | solution.py:533
  901.4 17.3 %collective-permute-start.62 = (bf16[256,640]{1,0:T(8,128)(2,1)S(1)}, bf16[256,640]{1,0:T(8,128)(2,1)S(1)}, u32[]{:S(2)}, u32[]{:S(2)}) collective-permute-start(bf16[256,640]{1,0:T(8,128)(2,1)S(1)} %get-tuple-element.329), channel_id=1, source_target_pairs={{0,8},{8,16},{16,24},{1,9},{9,17},{17,25},{2,10},{10,18},{18,26},{... | collective-permute-start | bytes 983048 | tf_op jit(solution)/shard_map/ppermute | solution.py:594
  902.9 16.5 %collective-permute-start.64 = (bf16[256,640]{1,0:T(8,128)(2,1)S(1)}, bf16[256,640]{1,0:T(8,128)(2,1)S(1)}, u32[]{:S(2)}, u32[]{:S(2)}) collective-permute-start(bf16[256,640]{1,0:T(8,128)(2,1)S(1)} %get-tuple-element.329), channel_id=1, source_target_pairs={{24,16},{16,8},{8,0},{25,17},{17,9},{9,1},{26,18},{18,10},{10,2},{... | collective-permute-start | bytes 983048 | tf_op jit(solution)/shard_map/ppermute | solution.py:595
  904.2 14.5 %collective-permute-start.63 = (f32[17536]{0:T(1024)S(1)}, f32[17536]{0:T(1024)S(1)}, u32[]{:S(2)}, u32[]{:S(2)}) collective-permute-start(f32[17536]{0:T(1024)S(1)} %add.623), channel_id=1, source_target_pairs={{0,16},{8,24},{16,0},{24,8},{1,17},{9,25},{17,1},{25,9},{2,18},{10... | collective-permute-start | bytes 210440 | tf_op jit(solution)/shard_map/ppermute | solution.py:630
  919.4 9.0 collective-permute-start.66
  928.3 9.0 collective-permute-start.69
  937.5 17.7 %collective-permute-start.70 = (bf16[1024,640]{1,0:T(8,128)(2,1)S(1)}, bf16[1024,640]{1,0:T(8,128)(2,1)S(1)}, u32[]{:S(2)}, u32[]{:S(2)}) collective-permute-start(bf16[1024,640]{1,0:T(8,128)(2,1)S(1)} %slice.139), channel_id=1, source_target_pairs={{0,2},{1,3},{2,0},{3,1},{4,6},{5,7},{6,4},{7,5},{8,10},{9,11},{10,... | collective-permute-start | bytes 3932168 | tf_op jit(solution)/shard_map/ppermute | solution.py:533
  955.8 15.2 %collective-permute-start.71 = (bf16[2048,640]{1,0:T(8,128)(2,1)S(1)}, bf16[2048,640]{1,0:T(8,128)(2,1)}, u32[]{:S(2)}, u32[]{:S(2)}) collective-permute-start(bf16[2048,640]{1,0:T(8,128)(2,1)S(1)} %maximum_select_fusion.1.mine_ref), channel_id=1, source_target_pairs={{0,1},{1,0},{2,3},{3,2},{4,5},{5,4},{6,7},{7,6},{8,9},{9,8},{10,11... | collective-permute-start | bytes 7864328 | tf_op jit(solution)/shard_map/ppermute | solution.py:530
  (77 other events, 1047.0 us)
Sparse Core Ops, SparseCore 0:
  478.8 102.7 all-reduce.3
  625.4 137.7 all-reduce.5
